TPU v7x, 32 devices: a whole 2x2x4 slice. The times are simulated.
32 devices in a mesh: blk: 8 (over y, x, core), kv: 4 (over z).
Axes of the slice: x: 2, y: 2, z: 4, core: 2. Of those that a mesh axis runs over, the one named last changes fastest.
Arguments:
- tokens: bfloat16 [4096, 2560], P('blk'), may hold values from -6 to 6
- attn_gain: float32 [2560], replicated, may hold values from 0.1 to 1.9
- mlp_gain: float32 [2560], replicated, may hold values from 0.1 to 1.9
- w_query: float32 [2560, 2560], P(('blk', 'kv')), may hold values from -0.375 to 0.375
- w_key: float32 [2560, 640], P(('blk', 'kv')), may hold values from -0.125 to 0.125
- w_value: float32 [2560, 640], P(('blk', 'kv')), may hold values from -0.125 to 0.125
- w_gate: float32 [2560, 6912], P(('blk', 'kv')), may hold values from -0.125 to 0.125
- w_up: float32 [2560, 6912], P(('blk', 'kv')), may hold values from -0.125 to 0.125
- w_out: bfloat16 [2560, 2560], P('kv'), may hold values from -0.125 to 0.125
- w_down: bfloat16 [6912, 2560], P('kv'), may hold values from -0.078125 to 0.078125
- cache: bfloat16 [2, 64, 8, 80, 128], P(None, 'blk', 'kv'), may hold values from -300 to 300
- slot_prompt: int32 [64], replicated, may hold values from 0 to 7, as said below
- prefix_len: int32 [8], replicated, may hold values from 1 to 2048, as said below
- new_len: int32 [8], replicated, may hold values from 256 to 512, as said below
Outputs:
- mixed: bfloat16 [4096, 2560], P('blk', 'kv')
Inputs may be any that keep to these rules, and one draw needn't show every extreme that they name: `slot_prompt`: the 8 slots of one index of blk hold at most 2 blocks of one prompt. One prompt, drawn afresh, has exactly 2 blocks on every index of blk; the other 6 slots of an index hold blocks of distinct prompts; every prompt has at least one block. `prefix_len`: A prompt with c slots has a prefix longer than (c - 1) * 128 and at most c * 128. Rows i >= new_len[p] of prompt p are padding.
All inputs are finite; a program needn't handle non-finite values.
Results may differ from a plain program's by a relative error of at most 0.019.
The roundings to bfloat16 on the way count: a program that leaves them out, or rounds other values in their place, can miss the bound.
Values may be sent and summed in bfloat16 or wider, within the bound.
No kernel may reach another device: no remote copies, remote signals or barrier semaphores. Data moves between devices by JAX's collectives and lax.ppermute only.
A program may use at most 128 MiB of HBM per device.

v0:
```python
import math

import jax
import jax.numpy as jnp
from jax import lax
from jax.sharding import PartitionSpec as P

HEADS = 32
KV_HEADS = 8
HD = 80
WINDOW = 4096
SINKS = 4
BLOCK = 128
CAP = 2


FLOOR_SCORE = -1e30
EPSILON = 1e-05
ROPE_BASE = 10000.0


def rms_scale(row_data, gain_vec):
    values = row_data.astype(jnp.float32)
    mean_square = jnp.mean(values * values, axis=-1, keepdims=True)
    return (values * lax.rsqrt(mean_square + EPSILON) * gain_vec).astype(jnp.bfloat16)


def rotate(values, positions):
    head_width = values.shape[-1]
    half_width = head_width // 2
    frequency = ROPE_BASE ** (-2.0 * jnp.arange(half_width, dtype=jnp.float32) / head_width)
    angles = positions.astype(jnp.float32)[:, None] * frequency[None, :]
    cosine = jnp.cos(angles)[:, None, :]
    sine_wave = jnp.sin(angles)[:, None, :]
    first_half = values[..., :half_width]
    second_half = values[..., half_width:]
    return jnp.concatenate(
        [
            first_half * cosine - second_half * sine_wave,
            second_half * cosine + first_half * sine_wave,
        ],
        axis=-1,
    )


def slot_ranks(slot_prompt, prompts, slots):
    onehot = (slot_prompt[:, None] == jnp.arange(prompts, dtype=jnp.int32)[None, :]).astype(
        jnp.int32
    )
    running = jnp.cumsum(onehot, axis=0)
    global_rank = jnp.sum(onehot * (running - 1), axis=1)
    local_count = jnp.cumsum(onehot.reshape(-1, slots, prompts), axis=1).reshape(-1, prompts)
    local_rank = jnp.sum(onehot * (local_count - 1), axis=1)
    return (global_rank, local_rank)


def visible(query_pos, key_pos):
    distance = query_pos - key_pos
    return (distance >= 0) & ((distance < WINDOW) | (key_pos < SINKS))


def partial_block(scores, seen_mask):
    masked = jnp.where(seen_mask, scores, FLOOR_SCORE)
    row_max = jnp.max(masked, axis=-1)
    weights = jnp.where(seen_mask, jnp.exp(masked - row_max[..., None]), 0.0)
    return (row_max, jnp.sum(weights, axis=-1), weights.astype(jnp.bfloat16))


def combine(first_part, second_part):
    maxima = jnp.maximum(first_part[0], second_part[0])
    scale_first = jnp.exp(first_part[0] - maxima)
    scale_second = jnp.exp(second_part[0] - maxima)
    totals = first_part[1] * scale_first + second_part[1] * scale_second
    outputs = first_part[2] * scale_first[..., None] + second_part[2] * scale_second[..., None]
    return (maxima, totals, outputs)


def pack_groups(matrices, groups):
    pieces = [
        matrix.reshape(matrix.shape[0], groups, matrix.shape[1] // groups) for matrix in matrices
    ]
    joined = jnp.concatenate(pieces, axis=2)
    return joined.reshape(matrices[0].shape[0], -1).astype(jnp.bfloat16)


def restack(moved_rows, groups, n_blocks):
    columns = moved_rows.shape[1]
    ordered = moved_rows.reshape(groups, n_blocks, -1, columns)
    return jnp.transpose(ordered, (1, 0, 2, 3)).reshape(-1, columns)


def shards(
    tokens,
    attn_gain,
    mlp_gain,
    w_query,
    w_key,
    w_value,
    w_gate,
    w_up,
    w_out,
    w_down,
    cache,
    slot_prompt,
    prefix_len,
    new_len,
):
    groups = lax.axis_size("kv")
    n_blocks = lax.axis_size("blk")
    blk_index = lax.axis_index("blk")
    kv_index = lax.axis_index("kv")
    merged_attn = pack_groups((w_query, w_key, w_value), groups)
    merged_mlp = pack_groups((w_gate, w_up), groups)
    collected = (
        lax.all_gather(merged_attn, "blk", axis=0, tiled=True),
        lax.all_gather(merged_mlp, "blk", axis=0, tiled=True),
    )
    moved_attn, moved_mlp = (
        lax.all_to_all(collected[0], "kv", split_axis=1, concat_axis=0, tiled=True),
        lax.all_to_all(collected[1], "kv", split_axis=1, concat_axis=0, tiled=True),
    )
    w_qkv = restack(moved_attn, groups, n_blocks)
    w_pair = restack(moved_mlp, groups, n_blocks)
    query_width = w_query.shape[1] // groups
    key_width = w_key.shape[1] // groups
    kv_local = key_width // HD
    per_group = HEADS // KV_HEADS
    new_rows = tokens.shape[0]
    prompts = prefix_len.shape[0]
    slots = cache.shape[1]
    score_scale = 1.0 / math.sqrt(HD)
    prefix_here = prefix_len[blk_index]
    live_count = new_len[blk_index]
    row_ids = jnp.arange(new_rows, dtype=jnp.int32)
    positions = prefix_here + row_ids
    offsets = jnp.arange(BLOCK, dtype=jnp.int32)
    normed = rms_scale(tokens, attn_gain)
    projected = jnp.dot(normed, w_qkv, preferred_element_type=jnp.float32)
    queries = rotate(projected[:, :query_width].reshape(new_rows, -1, HD), positions).astype(
        jnp.bfloat16
    )
    key_new = rotate(
        projected[:, query_width : query_width + key_width].reshape(new_rows, kv_local, HD),
        positions,
    ).astype(jnp.bfloat16)
    value_new = (
        projected[:, query_width + key_width :].reshape(new_rows, kv_local, HD).astype(jnp.bfloat16)
    )
    grouped_q = queries.reshape(new_rows, kv_local, per_group, HD)
    own_scores = (
        jnp.einsum("qgnd,kgd->gnqk", grouped_q, key_new, preferred_element_type=jnp.float32)
        * score_scale
    )
    own_mask = (row_ids[None, :] < live_count) & visible(positions[:, None], positions[None, :])
    own_max, own_sum, own_weights = partial_block(own_scores, own_mask)
    own_out = jnp.einsum(
        "gnqk,kgd->gnqd", own_weights, value_new, preferred_element_type=jnp.float32
    )
    running = (own_max, own_sum, own_out)
    global_rank, local_rank = slot_ranks(slot_prompt, prompts, slots)
    own_prompts = lax.dynamic_slice_in_dim(slot_prompt, blk_index * slots, slots)
    own_ranks = lax.dynamic_slice_in_dim(local_rank, blk_index * slots, slots)
    placed = own_prompts * CAP + own_ranks
    buffer_ids = jnp.arange(prompts * CAP, dtype=jnp.int32)
    matches = placed[None, :] == buffer_ids[:, None]
    source_slot = jnp.sum(
        jnp.where(matches, jnp.arange(slots, dtype=jnp.int32)[None, :], 0), axis=1
    )
    filled = jnp.any(matches, axis=1)
    outgoing = jnp.where(
        filled[None, :, None, None, None],
        jnp.take(cache, source_slot, axis=1),
        jnp.zeros((), cache.dtype),
    )
    arrived = lax.all_to_all(outgoing, "blk", split_axis=1, concat_axis=1, tiled=True)
    slot_ids = jnp.arange(prompts * slots, dtype=jnp.int32)
    landing = slot_ids // slots * CAP + local_rank
    for_me = slot_prompt == blk_index
    received = (landing[None, :] == buffer_ids[:, None]) & for_me[None, :]
    block_number = jnp.sum(jnp.where(received, global_rank[None, :], 0), axis=1)
    block_live = jnp.any(received, axis=1)
    total_slots = prompts * CAP
    group_slots = min(total_slots, max(1, 512 // BLOCK))
    step_count = total_slots // group_slots
    key_blocks = arrived[0].reshape(step_count, group_slots, kv_local, HD, BLOCK)
    value_blocks = arrived[1].reshape(step_count, group_slots, kv_local, HD, BLOCK)
    numbers = block_number.reshape(step_count, group_slots)
    live_flags = block_live.reshape(step_count, group_slots)

    def prefix_step(running_state, inputs):
        key_part, value_part, number_part, flag_part = inputs
        scores = (
            jnp.einsum("qgnd,sgdt->gnqst", grouped_q, key_part, preferred_element_type=jnp.float32)
            * score_scale
        )
        scores = scores.reshape(kv_local, per_group, new_rows, group_slots * BLOCK)
        key_pos = number_part[:, None] * BLOCK + offsets[None, :]
        key_live = (flag_part[:, None] & (key_pos < prefix_here)).reshape(-1)
        seen_mask = key_live[None, :] & visible(positions[:, None], key_pos.reshape(-1)[None, :])
        block_max, block_sum, weights = partial_block(scores, seen_mask)
        weights = weights.reshape(kv_local, per_group, new_rows, group_slots, BLOCK)
        block_out = jnp.einsum(
            "gnqst,sgdt->gnqd", weights, value_part, preferred_element_type=jnp.float32
        )
        return (combine(running_state, (block_max, block_sum, block_out)), None)

    running = lax.scan(prefix_step, running, (key_blocks, value_blocks, numbers, live_flags))[0]
    totals = running[1]
    outputs = running[2]
    attended = (
        jnp.transpose(outputs / totals[..., None], (2, 0, 1, 3))
        .reshape(new_rows, -1)
        .astype(jnp.bfloat16)
    )
    projected_out = jnp.dot(attended, w_out, preferred_element_type=jnp.float32)
    summed = lax.psum(projected_out.astype(jnp.bfloat16), "kv").astype(jnp.float32)
    middle = (tokens.astype(jnp.float32) + summed).astype(jnp.bfloat16)
    normed_mid = rms_scale(middle, mlp_gain)
    paired = jnp.dot(normed_mid, w_pair, preferred_element_type=jnp.float32)
    hidden_width = w_pair.shape[1] // 2
    hidden = (jax.nn.silu(paired[:, :hidden_width]) * paired[:, hidden_width:]).astype(jnp.bfloat16)
    down_part = jnp.dot(hidden, w_down, preferred_element_type=jnp.float32)
    reduced = lax.psum_scatter(
        down_part.astype(jnp.bfloat16), "kv", scatter_dimension=1, tiled=True
    ).astype(jnp.float32)
    out_width = reduced.shape[1]
    residual = lax.dynamic_slice_in_dim(middle, kv_index * out_width, out_width, 1).astype(
        jnp.float32
    )
    mixed = jnp.where((row_ids < live_count)[:, None], residual + reduced, 0.0)
    return mixed.astype(jnp.bfloat16)


def solution(mesh):
    return jax.shard_map(
        shards,
        mesh=mesh,
        in_specs=(
            P("blk", None),
            P(),
            P(),
            P(("blk", "kv"), None),
            P(("blk", "kv"), None),
            P(("blk", "kv"), None),
            P(("blk", "kv"), None),
            P(("blk", "kv"), None),
            P("kv", None),
            P("kv", None),
            P(None, "blk", "kv", None, None),
            P(),
            P(),
            P(),
        ),
        out_specs=P("blk", "kv"),
        check_vma=False,
    )
```

profile of v0, /device:TPU:0, one launch (start us, length us, event | category | flops | bytes accessed | tf_op | source)
XLA Modules:
  0.0 794.8 jit_solution(18064742600255205790)
XLA Ops:
  13.3 2.3 pad_maximum_fusion.1
  15.6 2.8 convert_element_type.84
  18.5 2.8 convert.46
  21.3 3.3 reshape.317
  24.5 2.7 convert.45
  27.3 3.3 reshape.316
  30.5 3.1 pad_maximum_fusion
  36.0 2.9 gather_fusion
  39.0 2.6 select_bitcast_fusion
  41.6 5.2 all-to-all-start.1
  46.8 24.8 %all-gather.3.cloned.1.call-done = bf16[640,3840]{1,0:T(8,128)(2,1)} async-done(((bf16[80,3840]{1,0:T(8,128)(2,1)}), bf16[640,3840]{1,0:T(8,128)(2,1)}) %all-gather.3.cloned.1.call-update) | async-done | bytes 4915216 | tf_op jit(solution)/shard_map/all_gather | solution.py:115
  71.6 7.7 copy.59
  79.2 5.0 all-to-all-start
  84.2 86.5 %all-gather.5.cloned.1.call-done = bf16[640,13824]{1,0:T(8,128)(2,1)} async-done(((bf16[80,13824]{1,0:T(8,128)(2,1)}), bf16[640,13824]{1,0:T(8,128)(2,1)}) %all-gather.5.cloned.1.call-update) | async-done | bytes 17694736 | tf_op jit(solution)/shard_map/all_gather | solution.py:116
  170.8 22.9 %copy.65 = bf16[640,13824]{0,1:T(8,128)(2,1)} copy(bf16[640,13824]{1,0:T(8,128)(2,1)} %all-gather.5.cloned.1.call-done) | data formatting | bytes 35389440 | tf_op jit(solution)/shard_map/all_gather | solution.py:116
  193.7 7.3 all-to-all-start.2
  206.5 2.3 fusion.38
  210.3 2.4 fusion.78
  212.7 7.9 copy.60
  220.7 3.4 copy.61
  224.1 2.9 fusion.46
  230.0 3.7 fusion.42
  233.6 2.0 fusion.34
  235.6 51.4 %while.16 = (s32[]{:T(128)}, f32[2,4,512]{2,1,0:T(4,128)}, f32[2,4,512]{2,1,0:T(4,128)S(1)}, f32[2,4,512,80]{2,3,1,0:T(8,128)}, pred[4,4]{1,0:T(4,128)(4,1)}, /*...) while((s32[]{:T(128)}, f32[2,4,512]{2,1,0:T(4,128)}, ...), condition=%wide.region_14.15_spmd.clone.clone, body=%wide.region_11.14_spmd.clone.clone.sunk | while | flops 700926976 | bytes 41331012 | solution.py:207
  240.2 2.7 fusion.96
  242.9 2.0 fusion.97
  245.0 2.6 fusion.98
  253.0 2.7 fusion.96
  255.7 2.0 fusion.97
  257.8 2.6 fusion.98
  265.8 2.7 fusion.96
  268.5 2.0 fusion.97
  270.6 2.6 fusion.98
  278.6 2.7 fusion.96
  281.3 2.0 fusion.97
  283.4 2.6 fusion.98
  288.5 3.8 convolution_convert_fusion.1
  292.4 336.4 %all-reduce.2.cloned.1.call-done = bf16[512,2560]{1,0:T(8,128)(2,1)} async-done(((bf16[512,2560]{1,0:T(8,128)(2,1)}), bf16[512,2560]{1,0:T(8,128)(2,1)}) %all-reduce.2.cloned.1.call-update) | async-done | bytes 2621456 | tf_op jit(solution)/shard_map/psum | solution.py:216
  628.7 5.2 fusion.35
  633.9 35.1 %all-to-all-done.2 = bf16[640,4,3456]{0,2,1:T(8,128)(2,1)} async-done(((bf16[640,4,3456]{0,2,1:T(8,128)(2,1)}), bf16[640,4,3456]{0,2,1:T(8,128)(2,1)}, u32[]{:S(2)}, u32[]{:S(2)}) %all-to-all-start.2) | async-done | bytes 17694752 | tf_op jit(solution)/shard_map/all_to_all | solution.py:120
  669.1 23.4 %copy.66 = bf16[4,640,3456]{2,1,0:T(8,128)(2,1)} copy(bf16[4,640,3456]{1,2,0:T(8,128)(2,1)} %bitcast.25) | data formatting | bytes 35389440 | tf_op jit(solution)/shard_map/all_to_all | solution.py:120
  692.4 8.2 %copy.67 = bf16[8,4,80,3456]{3,2,1,0:T(8,128)(2,1)S(1)} copy(bf16[8,4,80,3456]{3,2,0,1:T(8,128)(2,1)} %bitcast.158) | data formatting | bytes 35389440 | tf_op jit(solution)/shard_map/transpose | solution.py:89
  700.7 13.2 %fusion.48 = f32[512,3456]{1,0:T(8,128)} fusion(bf16[2560,3456]{1,0:T(8,128)(2,1)S(1)} %bitcast.161, bf16[512,2560]{1,0:T(8,128)(2,1)} %get-tuple-element.196, f32[2560]{0:T(1024)S(1)} %copy-done.13, f32[512]{0:T(512)S(1)} %add_rsqrt_fusion), kind=kOutput, calls=%fused_computation.63 | convolution fusion | flops 9064939520 | bytes 27406336 | tf_op jit(solution)/shard_map/dot_general | solution.py:219
  713.9 12.2 %convolution_convert_fusion = bf16[512,2560]{1,0:T(8,128)(2,1)} fusion(bf16[1728,2560]{1,0:T(8,128)(2,1)} %param.25, f32[512,3456]{1,0:T(8,128)} %fusion.48), kind=kOutput, calls=%fused_computation.56 | convolution fusion | flops 4536467456 | bytes 18808832 | tf_op jit(solution)/shard_map/dot_general | solution.py:222
  726.1 4.4 copy.77
  730.6 53.2 %reduce-scatter.4.cloned.1.call-done = bf16[640,512]{1,0:T(8,128)(2,1)} async-done(((bf16[2560,512]{1,0:T(8,128)(2,1)}), bf16[640,512]{1,0:T(8,128)(2,1)}) %reduce-scatter.4.cloned.1.call-update) | async-done | bytes 655376
  783.7 2.2 copy.78
  785.9 2.3 select_convert_fusion
  (142 shorter events, 42.3 us)
Async XLA Ops:
  6.5 282.0 %copy-start = (bf16[640,2560]{1,0:T(8,128)(2,1)S(1)}, bf16[640,2560]{1,0:T(8,128)(2,1)}, u32[]{:S(2)}) copy-start(bf16[640,2560]{1,0:T(8,128)(2,1)} %param.24) | copy-start | bytes 9830404
  6.5 65.1 %all-gather.3.cloned.1.call-start = ((), (), s32[]{:S(2)}) async-start(), calls=%async_computation.4 | async-start | bytes 5529600 | tf_op jit(solution)/shard_map/all_gather | solution.py:115
  18.5 152.3 %all-gather.5.cloned.1.call-start = ((), (), s32[]{:S(2)}) async-start(), calls=%async_computation.6 | async-start | bytes 19906560 | tf_op jit(solution)/shard_map/all_gather | solution.py:116
  33.6 1.7 copy-start.9
  41.6 37.7 %all-to-all-start.1 = ((bf16[2,16,2,80,128]{4,3,2,0,1:T(8,128)(2,1)}), bf16[2,16,2,80,128]{4,3,2,0,1:T(8,128)(2,1)}, u32[]{:S(2)}, u32[]{:S(2)}) async-start(bf16[2,16,2,80,128]{4,3,2,0,1:T(8,128)(2,1)} %select_bitcast_fusion), calls=%async_computation.1 | async-start | bytes 2621440 | tf_op jit(solution)/shard_map/all_to_all | solution.py:175
  79.2 114.4 %all-to-all-start = ((bf16[640,4,960]{0,2,1:T(8,128)(2,1)}), bf16[640,4,960]{0,2,1:T(8,128)(2,1)}, u32[]{:S(2)}, u32[]{:S(2)}) async-start(bf16[640,4,960]{0,2,1:T(8,128)(2,1)} %bitcast.160), calls=%async_computation | async-start | bytes 9830400 | tf_op jit(solution)/shard_map/all_to_all | solution.py:119
  193.6 7.6 copy-start.14
  193.6 8.2 %copy-start.15 = (s32[8]{0:T(128)S(1)}, s32[8]{0:T(128)}, u32[]{:S(2)}) copy-start(s32[8]{0:T(128)} %param.29) | copy-start | bytes 100
  193.7 475.4 %all-to-all-start.2 = ((bf16[640,4,3456]{0,2,1:T(8,128)(2,1)}), bf16[640,4,3456]{0,2,1:T(8,128)(2,1)}, u32[]{:S(2)}, u32[]{:S(2)}) async-start(bf16[640,4,3456]{0,2,1:T(8,128)(2,1)} %bitcast.157), calls=%async_computation.2 | async-start | bytes 35389440 | tf_op jit(solution)/shard_map/all_to_all | solution.py:120
  201.0 427.8 %all-reduce.2.cloned.1.call-start = ((), (), s32[]{:S(2)}) async-start(), calls=%async_computation.5 | async-start | bytes 5242880 | tf_op jit(solution)/shard_map/psum | solution.py:216
  205.8 4.5 copy-start.10
  220.7 3.4 copy-start.1
  220.7 3.4 copy-start.12
  224.1 3.1 copy-start.4
  224.1 3.1 copy-start.5
  229.9 3.7 copy-start.6
  242.9 2.1 copy-start.7
  242.9 2.1 copy-start.2
  245.0 2.6 copy-start.8
  247.6 1.1 copy-start.3
  255.7 2.1 copy-start.7
  255.7 2.1 copy-start.2
  257.8 2.6 copy-start.8
  260.4 1.1 copy-start.3
  268.5 2.1 copy-start.7
  268.5 2.1 copy-start.2
  270.6 2.6 copy-start.8
  273.2 1.1 copy-start.3
  281.3 2.1 copy-start.7
  281.3 2.1 copy-start.2
  283.4 2.6 copy-start.8
  286.0 1.1 copy-start.3
  292.3 491.4 %reduce-scatter.4.cloned.1.call-start = ((), (), s32[]{:S(2)}) async-start(), calls=%async_computation.7 | async-start | bytes 3276800
  692.4 8.2 %copy-start.13 = (f32[2560]{0:T(1024)S(1)}, f32[2560]{0:T(1024)}, u32[]{:S(2)}) copy-start(f32[2560]{0:T(1024)} %param.18) | copy-start | bytes 30724
  726.1 59.7 %copy-start.11 = (pred[512]{0:T(512)(128)(4,1)S(1)}, pred[512]{0:T(512)(128)(4,1)}, u32[]{:S(2)}) copy-start(pred[512]{0:T(512)(128)(4,1)} %copy-done.10) | copy-start | bytes 1540
Sparse Core Ops, SparseCore 0:
  18.6 52.9 all-gather.2
  73.5 97.2 all-gather.4
  292.4 336.2 all-reduce.1
  730.7 52.9 reduce-scatter.3
where the time goes:
time: 798 us; the launch traced here: 795 us
  waiting for transfers between devices  536 us (67%)
  local copies, waits for them, and re-layouts  113 us (14%)
  matrix products  58.3 us (7%)
  other arithmetic  55.5 us (7%)
  starting transfers between devices  17.8 us (2%)
  between operations  13.4 us (2%)
    psum x1, waiting for transfers between devices, shards(): lax.psum(projected_out.astype(jnp.bfloat16), 'kv').astype(jnp.float32)  336 us
    all_gather x1, waiting for transfers between devices, shards(): lax.all_gather(merged_mlp, 'blk', axis=0, tiled=True)  86.5 us
    unnamed x5, waiting for transfers between devices  53.2 us
    all_to_all x1, waiting for transfers between devices, shards(): lax.all_to_all(collected[1], 'kv', split_axis=1, concat_axis=0, tiled=True)  35.1 us
    all_gather x1, waiting for transfers between devices, shards(): lax.all_gather(merged_attn, 'blk', axis=0, tiled=True)  24.8 us
    all_to_all x1, local copies, waits for them, and re-layouts, shards(): lax.all_to_all(collected[1], 'kv', split_axis=1, concat_axis=0, tiled=True)  23.4 us
    all_gather x1, local copies, waits for them, and re-layouts, shards(): lax.all_gather(merged_mlp, 'blk', axis=0, tiled=True)  22.9 us
  transfers between devices with their start and end apart: 7, of which 5 were waited for; matrix products, arithmetic and copies ran while one was open for 18% of the time, Pallas kernels for 0%

commit v1 on v0

--- a/solution.py
+++ b/solution.py
@@ -76,17 +76,20 @@
 
 
 def pack_groups(matrices, groups):
-    pieces = [
-        matrix.reshape(matrix.shape[0], groups, matrix.shape[1] // groups) for matrix in matrices
-    ]
-    joined = jnp.concatenate(pieces, axis=2)
-    return joined.reshape(matrices[0].shape[0], -1).astype(jnp.bfloat16)
-
-
-def restack(moved_rows, groups, n_blocks):
-    columns = moved_rows.shape[1]
-    ordered = moved_rows.reshape(groups, n_blocks, -1, columns)
-    return jnp.transpose(ordered, (1, 0, 2, 3)).reshape(-1, columns)
+    pieces = []
+    for group in range(groups):
+        columns = []
+        for matrix in matrices:
+            width = matrix.shape[1] // groups
+            columns.append(matrix[:, group * width : (group + 1) * width].astype(jnp.bfloat16))
+        pieces.append(jnp.concatenate(columns, axis=1))
+    return jnp.stack(pieces, axis=0)
+
+
+def regroup(packed):
+    moved = lax.all_to_all(packed, "kv", split_axis=0, concat_axis=0, tiled=True)
+    rows = moved.reshape(-1, moved.shape[2])
+    return lax.all_gather(rows, "blk", axis=0, tiled=True)
 
 
 def shards(
@@ -106,21 +109,10 @@
     new_len,
 ):
     groups = lax.axis_size("kv")
-    n_blocks = lax.axis_size("blk")
     blk_index = lax.axis_index("blk")
     kv_index = lax.axis_index("kv")
-    merged_attn = pack_groups((w_query, w_key, w_value), groups)
-    merged_mlp = pack_groups((w_gate, w_up), groups)
-    collected = (
-        lax.all_gather(merged_attn, "blk", axis=0, tiled=True),
-        lax.all_gather(merged_mlp, "blk", axis=0, tiled=True),
-    )
-    moved_attn, moved_mlp = (
-        lax.all_to_all(collected[0], "kv", split_axis=1, concat_axis=0, tiled=True),
-        lax.all_to_all(collected[1], "kv", split_axis=1, concat_axis=0, tiled=True),
-    )
-    w_qkv = restack(moved_attn, groups, n_blocks)
-    w_pair = restack(moved_mlp, groups, n_blocks)
+    w_qkv = regroup(pack_groups((w_query, w_key, w_value), groups))
+    w_pair = regroup(pack_groups((w_gate, w_up), groups))
     query_width = w_query.shape[1] // groups
     key_width = w_key.shape[1] // groups
     kv_local = key_width // HD

time: 798 us -> 449 us (0.56)
  waiting for transfers between devices: 536 us -> 267 us
  local copies, waits for them, and re-layouts: 113 us -> 27 us
  blocking collectives: 0 us -> 23.5 us
  starting transfers between devices: 17.8 us -> 9.12 us
  other arithmetic: 55.5 us -> 47.5 us
    psum x1, waiting for transfers between devices: 336 us -> 103 us  [shards(): lax.psum(projected_out.astype(jnp.bfloat16), 'kv').astype(jnp.float32)]
    all_to_all x2 -> x1, waiting for transfers between devices: 35.1 us -> 0.01 us  [regroup(): lax.all_to_all(packed, 'kv', split_axis=0, concat_axis=0, tiled=True)]
    all_to_all x2 -> x0, local copies, waits for them, and re-layouts: 31.3 us -> none  [the longest x1 23.4 us: shards(): lax.all_to_all(collected[1], 'kv', split_axis=1, concat_axis=0, tiled=True)]
    all_gather x2 -> x0, local copies, waits for them, and re-layouts: 30.5 us -> none  [the longest x1 22.9 us: shards(): lax.all_gather(merged_mlp, 'blk', axis=0, tiled=True)]
    all_to_all x0 -> x1, blocking collectives: none -> 23.5 us  [regroup(): lax.all_to_all(packed, 'kv', split_axis=0, concat_axis=0, tiled=True)]
    transpose x2 -> x0, local copies, waits for them, and re-layouts: 11.6 us -> none  [restack(): return jnp.transpose(ordered, (1, 0, 2, 3)).reshape(-1, columns)]
    reshape x5 -> x0, local copies, waits for them, and re-layouts: 9.33 us -> none  [pack_groups(): matrix.reshape(matrix.shape[0], groups, matrix.shape[1] // groups)]
    all_gather x2, waiting for transfers between devices: 111 us -> 103 us  [regroup(): return lax.all_gather(rows, 'blk', axis=0, tiled=True)]
  transfers between devices with their start and end apart: 7 -> 6, of which waited for: 5 -> 5; matrix products, arithmetic and copies ran while one was open for 18% -> 21% of each run, Pallas kernels for 0% -> 0%
where the time goes in v1:
time: 449 us; the launch traced here: 448 us
  waiting for transfers between devices  267 us (59%)
  matrix products  60.6 us (13%)
  other arithmetic  47.5 us (11%)
  local copies, waits for them, and re-layouts  27 us (6%)
  blocking collectives  23.5 us (5%)
  between operations  13.5 us (3%)
  starting transfers between devices  9.12 us (2%)
    all_gather x2, waiting for transfers between devices, regroup(): return lax.all_gather(rows, 'blk', axis=0, tiled=True)  103 us
    psum x1, waiting for transfers between devices, shards(): lax.psum(projected_out.astype(jnp.bfloat16), 'kv').astype(jnp.float32)  103 us
    unnamed x5, waiting for transfers between devices  53 us
    all_to_all x1, blocking collectives, regroup(): lax.all_to_all(packed, 'kv', split_axis=0, concat_axis=0, tiled=True)  23.5 us
    dot_general x1, matrix products, shards(): paired = jnp.dot(normed_mid, w_pair, preferred_element_type=jnp.float32)  14.6 us
    dot_general x4, matrix products, prefix_step(): jnp.einsum('qgnd,sgdt->gnqst', grouped_q, key_part, preferred_element_typ...  10.7 us
    reduce_sum x5, other arithmetic, partial_block(): return (row_max, jnp.sum(weights, axis=-1), weights.astype(jnp.bfloat16))  10.4 us
    dot_general x4, matrix products, prefix_step(): jnp.einsum('gnqst,sgdt->gnqd', weights, value_part, preferred_element_typ...  10.2 us
  transfers between devices with their start and end apart: 6, of which 5 were waited for; matrix products, arithmetic and copies ran while one was open for 21% of the time, Pallas kernels for 0%

profile of v1, /device:TPU:0, one launch (start us, length us, event | category | flops | bytes accessed | tf_op | source)
XLA Modules:
  0.0 448.3 jit_solution(8336770460502608767)
XLA Ops:
  6.5 1.3 convert.47
  10.4 23.5 %all_to_all.15 = bf16[4,80,960]{2,1,0:T(8,128)(2,1)} all-to-all(bf16[4,80,960]{2,1,0:T(8,128)(2,1)S(1)} %pad_maximum_fusion.1), channel_id=1, replica_groups=mesh['blk'=8,'kv'=4] {'kv'}, dimensions={0} | all-to-all | bytes 1228800 | tf_op jit(solution)/shard_map/all_to_all | solution.py:90
  34.7 2.9 gather_fusion
  37.7 2.7 select_bitcast_fusion
  40.4 4.3 all-to-all-start.1
  47.6 1.9 convert.55
  49.5 1.7 convert.56
  51.3 1.2 iota_compare_fusion.4
  53.6 1.0 multiply_cosine_fusion
  56.8 1.7 pad_maximum_fusion
  58.5 7.0 %all-to-all-done.1 = bf16[2,16,2,80,128]{4,3,2,0,1:T(8,128)(2,1)} async-done(((bf16[2,16,2,80,128]{4,3,2,0,1:T(8,128)(2,1)}), bf16[2,16,2,80,128]{4,3,2,0,1:T(8,128)(2,1)}, u32[]{:S(2)}, u32[]{:S(2)}) %all-to-all-start.1) | async-done | bytes 1310752 | tf_op jit(solution)/shard_map/all_to_all | solution.py:167
  65.5 4.6 %all-to-all-start.2 = ((bf16[4,80,3456]{2,1,0:T(8,128)(2,1)}), bf16[4,80,3456]{2,1,0:T(8,128)(2,1)}, u32[]{:S(2)}, u32[]{:S(2)}) async-start(bf16[4,80,3456]{2,1,0:T(8,128)(2,1)} %pad_maximum_fusion), calls=%async_computation.2 | async-start | bytes 4423680 | tf_op jit(solution)/shard_map/all_to_all | solution.py:90
  70.1 2.5 fusion.78
  72.6 13.8 %all-gather.3.cloned.1.call-done = bf16[2560,960]{1,0:T(8,128)(2,1)} async-done(((bf16[320,960]{1,0:T(8,128)(2,1)}), bf16[2560,960]{1,0:T(8,128)(2,1)}) %all-gather.3.cloned.1.call-update) | async-done | bytes 4915216 | tf_op jit(solution)/shard_map/all_gather | solution.py:92
  86.4 6.2 %fusion.46 = f32[512,960]{0,1:T(8,128)S(1)} fusion(bf16[2560,960]{1,0:T(8,128)(2,1)} %all-gather.3.cloned.1.call-done, bf16[512,2560]{1,0:T(8,128)(2,1)} %param.16, f32[2560]{0:T(1024)S(1)} %copy-done.12, f32[512]{0:T(512)S(1)} %add_rsqrt_fusion.1), kind=kOutput, calls=%fused_computation.62 | convolution fusion | flops 2521825280 | bytes 9515008 | tf_op jit(solution)/shard_map/dot_general | solution.py:130
  94.7 1.6 fusion.32
  96.3 2.2 fusion.34
  98.5 3.7 fusion.42
  102.2 49.6 %while.16 = (s32[]{:T(128)}, f32[2,4,512]{2,1,0:T(4,128)}, f32[2,4,512]{2,1,0:T(4,128)S(1)}, f32[2,4,512,80]{2,3,1,0:T(8,128)}, pred[4,4]{1,0:T(4,128)(4,1)}, /*...) while((s32[]{:T(128)}, f32[2,4,512]{2,1,0:T(4,128)}, ...), condition=%wide.region_14.15_spmd.clone.clone, body=%wide.region_11.14_spmd.clone.clone.sunk | while | flops 700926976 | bytes 41331004 | solution.py:199
  105.1 1.0 constant_dynamic-slice_fusion.4
  106.2 2.7 fusion.101
  108.9 2.0 fusion.102
  111.0 2.6 fusion.103
  113.6 1.1 copy-done.3
  118.5 2.7 fusion.101
  121.3 2.0 fusion.102
  123.4 2.6 fusion.103
  125.9 1.1 copy-done.3
  129.9 1.0 constant_dynamic-slice_fusion.4
  130.9 2.7 fusion.101
  133.7 2.0 fusion.102
  135.8 2.6 fusion.103
  138.3 1.1 copy-done.3
  143.3 2.7 fusion.101
  146.0 2.0 fusion.102
  148.2 2.6 fusion.103
  150.7 1.1 copy-done.3
  151.8 1.5 divide_convert_fusion
  153.3 3.7 convolution_convert_fusion.1
  158.1 103.3 %all-reduce.2.cloned.1.call-done = bf16[512,2560]{1,0:T(8,128)(2,1)} async-done(((bf16[512,2560]{1,0:T(8,128)(2,1)}), bf16[512,2560]{1,0:T(8,128)(2,1)}) %all-reduce.2.cloned.1.call-update) | async-done | bytes 2621456 | tf_op jit(solution)/shard_map/psum | solution.py:208
  261.3 5.1 %fusion.35 = (f32[512]{0:T(512)S(1)}, bf16[512,2560]{1,0:T(8,128)(2,1)}) fusion(bf16[512,2560]{1,0:T(8,128)(2,1)} %all-reduce.2.cloned.1.call-done, bf16[512,2560]{1,0:T(8,128)(2,1)} %param.16), kind=kLoop, calls=%fused_computation.49 | loop fusion | flops 9174528 | bytes 7866368 | tf_op jit(solution)/shard_map/reduce_sum | solution.py:24
  266.5 89.5 %all-gather.5.cloned.1.call-done = bf16[2560,3456]{1,0:T(8,128)(2,1)} async-done(((bf16[320,3456]{1,0:T(8,128)(2,1)}), bf16[2560,3456]{1,0:T(8,128)(2,1)}) %all-gather.5.cloned.1.call-update) | async-done | bytes 17694736 | tf_op jit(solution)/shard_map/all_gather | solution.py:92
  356.0 14.6 %fusion.48 = f32[512,3456]{1,0:T(8,128)S(1)} fusion(bf16[2560,3456]{1,0:T(8,128)(2,1)} %all-gather.5.cloned.1.call-done, bf16[512,2560]{1,0:T(8,128)(2,1)} %get-tuple-element.186, f32[2560]{0:T(1024)S(1)} %copy-done.13, f32[512]{0:T(512)S(1)} %add_rsqrt_fusion), kind=kOutput, calls=%fused_computation.63 | convolution fusion | flops 9064939520 | bytes 27406336 | tf_op jit(solution)/shard_map/dot_general | solution.py:211
  370.6 10.0 %convolution_convert_fusion = bf16[512,2560]{1,0:T(8,128)(2,1)} fusion(bf16[1728,2560]{1,0:T(8,128)(2,1)} %param.25, f32[512,3456]{1,0:T(8,128)S(1)} %fusion.48), kind=kOutput, calls=%fused_computation.56 | convolution fusion | flops 4536467456 | bytes 18808832 | tf_op jit(solution)/shard_map/dot_general | solution.py:214
  380.5 4.4 copy.42
  385.0 52.3 %reduce-scatter.4.cloned.1.call-done = bf16[640,512]{1,0:T(8,128)(2,1)} async-done(((bf16[2560,512]{1,0:T(8,128)(2,1)}), bf16[640,512]{1,0:T(8,128)(2,1)}) %reduce-scatter.4.cloned.1.call-update) | async-done | bytes 655376
  437.2 2.2 copy.43
  439.4 2.3 select_convert_fusion
  (138 shorter events, 26.3 us)
Async XLA Ops:
  6.5 146.8 %copy-start = (bf16[640,2560]{1,0:T(8,128)(2,1)S(1)}, bf16[640,2560]{1,0:T(8,128)(2,1)}, u32[]{:S(2)}) copy-start(bf16[640,2560]{1,0:T(8,128)(2,1)} %param.24) | copy-start | bytes 9830404
  6.5 79.9 %all-gather.3.cloned.1.call-start = ((), (), s32[]{:S(2)}) async-start(), calls=%async_computation.4 | async-start | bytes 5898240 | tf_op jit(solution)/shard_map/all_gather | solution.py:92
  7.9 26.0 %copy-start.9 = (s32[64]{0:T(128)S(1)}, s32[64]{0:T(128)}, u32[]{:S(2)}) copy-start(s32[64]{0:T(128)} %param.27) | copy-start | bytes 772
  37.6 7.1 %copy-start.14 = (s32[8]{0:T(128)S(1)}, s32[8]{0:T(128)}, u32[]{:S(2)}) copy-start(s32[8]{0:T(128)} %param.28) | copy-start | bytes 100
  37.6 7.6 %copy-start.15 = (s32[8]{0:T(128)S(1)}, s32[8]{0:T(128)}, u32[]{:S(2)}) copy-start(s32[8]{0:T(128)} %param.29) | copy-start | bytes 100
  40.4 25.2 %all-to-all-start.1 = ((bf16[2,16,2,80,128]{4,3,2,0,1:T(8,128)(2,1)}), bf16[2,16,2,80,128]{4,3,2,0,1:T(8,128)(2,1)}, u32[]{:S(2)}, u32[]{:S(2)}) async-start(bf16[2,16,2,80,128]{4,3,2,0,1:T(8,128)(2,1)} %select_bitcast_fusion), calls=%async_computation.1 | async-start | bytes 2621440 | tf_op jit(solution)/shard_map/all_to_all | solution.py:167
  47.6 7.4 %copy-start.1 = (bf16[512,2560]{1,0:T(8,128)(2,1)S(1)}, bf16[512,2560]{1,0:T(8,128)(2,1)}, u32[]{:S(2)}) copy-start(bf16[512,2560]{1,0:T(8,128)(2,1)} %param.16) | copy-start | bytes 7864324
  52.5 2.2 copy-start.10
  58.5 27.9 %copy-start.12 = (f32[2560]{0:T(1024)S(1)}, f32[2560]{0:T(1024)}, u32[]{:S(2)}) copy-start(f32[2560]{0:T(1024)} %param.17) | copy-start | bytes 30724
  65.5 91.5 %all-to-all-start.2 = ((bf16[4,80,3456]{2,1,0:T(8,128)(2,1)}), bf16[4,80,3456]{2,1,0:T(8,128)(2,1)}, u32[]{:S(2)}, u32[]{:S(2)}) async-start(bf16[4,80,3456]{2,1,0:T(8,128)(2,1)} %pad_maximum_fusion), calls=%async_computation.2 | async-start | bytes 4423680 | tf_op jit(solution)/shard_map/all_to_all | solution.py:90
  70.1 191.2 %all-reduce.2.cloned.1.call-start = ((), (), s32[]{:S(2)}) async-start(), calls=%async_computation.5 | async-start | bytes 5242880 | tf_op jit(solution)/shard_map/psum | solution.py:208
  92.6 0.9 copy-start.4
  92.6 0.9 copy-start.5
  96.3 2.2 copy-start.6
  108.8 2.1 copy-start.7
  108.9 2.1 copy-start.2
  111.0 2.6 copy-start.8
  113.5 1.1 copy-start.3
  121.2 2.1 copy-start.7
  121.2 2.1 copy-start.2
  123.3 2.6 copy-start.8
  125.9 1.1 copy-start.3
  133.6 2.1 copy-start.7
  133.6 2.1 copy-start.2
  135.7 2.6 copy-start.8
  138.3 1.1 copy-start.3
  146.0 2.1 copy-start.7
  146.0 2.1 copy-start.2
  148.1 2.6 copy-start.8
  150.7 1.1 copy-start.3
  157.0 199.0 %all-gather.5.cloned.1.call-start = ((), (), s32[]{:S(2)}) async-start(), calls=%async_computation.6 | async-start | bytes 19906560 | tf_op jit(solution)/shard_map/all_gather | solution.py:92
  157.8 198.2 %copy-start.13 = (f32[2560]{0:T(1024)S(1)}, f32[2560]{0:T(1024)}, u32[]{:S(2)}) copy-start(f32[2560]{0:T(1024)} %param.18) | copy-start | bytes 30724
  157.8 279.4 %reduce-scatter.4.cloned.1.call-start = ((), (), s32[]{:S(2)}) async-start(), calls=%async_computation.7 | async-start | bytes 3276800
  384.9 54.5 %copy-start.11 = (pred[512]{0:T(512)(128)(4,1)S(1)}, pred[512]{0:T(512)(128)(4,1)}, u32[]{:S(2)}) copy-start(pred[512]{0:T(512)(128)(4,1)} %copy-done.10) | copy-start | bytes 1540
Sparse Core Ops, SparseCore 0:
  34.0 52.3 all-gather.2
  157.2 104.1 all-reduce.1
  263.2 92.7 all-gather.4
  385.1 52.0 reduce-scatter.3

commit v2 on v1

v2 whole, which is shorter than its diff:
```python
import functools
import math

import jax
import jax.numpy as jnp
from jax import lax
from jax.experimental import pallas as pl
from jax.experimental.pallas import tpu as pltpu
from jax.sharding import PartitionSpec as P

HEADS = 32
KV_HEADS = 8
HD = 80
WINDOW = 4096
SINKS = 4
BLOCK = 128
CAP = 2


FLOOR_SCORE = -1e30
EPSILON = 1e-05
ROPE_BASE = 10000.0
FAR = 1 << 30
LANES = 128
TILE = 256
ROW_TILE = 128
VMEM_LIMIT = 56 * 1024 * 1024

ANY = pl.BlockSpec(memory_space=pl.ANY)
VMEM = pl.BlockSpec(memory_space=pltpu.VMEM)
SMEM = pl.BlockSpec(memory_space=pltpu.SMEM)


def rms_scale(row_data, gain_vec):
    values = row_data.astype(jnp.float32)
    mean_square = jnp.mean(values * values, axis=-1, keepdims=True)
    return (values * lax.rsqrt(mean_square + EPSILON) * gain_vec).astype(jnp.bfloat16)


def rope_tables(positions):
    half_width = HD // 2
    frequency = ROPE_BASE ** (-2.0 * jnp.arange(half_width, dtype=jnp.float32) / HD)
    angles = positions.astype(jnp.float32)[:, None] * frequency[None, :]
    cosine = jnp.cos(angles)
    sine = jnp.sin(angles)
    return (
        jnp.concatenate([cosine, cosine], axis=1),
        jnp.concatenate([-sine, sine], axis=1),
    )


def slot_ranks(slot_prompt, prompts, slots):
    onehot = (slot_prompt[:, None] == jnp.arange(prompts, dtype=jnp.int32)[None, :]).astype(
        jnp.int32
    )
    running = jnp.cumsum(onehot, axis=0)
    global_rank = jnp.sum(onehot * (running - 1), axis=1)
    local_count = jnp.cumsum(onehot.reshape(-1, slots, prompts), axis=1).reshape(-1, prompts)
    local_rank = jnp.sum(onehot * (local_count - 1), axis=1)
    return (global_rank, local_rank)


def swap(values, axis, bit):
    pairs = [(index, index ^ bit) for index in range(lax.axis_size(axis))]
    return lax.ppermute(values, axis, pairs)


def half_up(width):
    return (width // 2 + LANES - 1) // LANES * LANES


def group_columns(matrices, groups, spans):
    pieces = []
    for group in range(groups):
        columns = []
        for which, first, last in spans:
            start = group * (matrices[which].shape[1] // groups)
            columns.append(matrices[which][:, start + first : start + last])
        pieces.append(jnp.concatenate(columns, axis=1).astype(jnp.bfloat16))
    return jnp.stack(pieces, axis=0)


def exchange(packed):
    moved = lax.all_to_all(packed, "kv", split_axis=0, concat_axis=0, tiled=True)
    return moved.reshape(-1, moved.shape[2])


def plane_gather(piece, diagonal_bit):
    if lax.axis_size("blk") != 8:
        return None
    by_x = swap(piece, "blk", 2)
    by_y = swap(piece, "blk", 4)
    if diagonal_bit == 2:
        across = swap(by_y, "blk", 2)
    else:
        across = swap(by_x, "blk", 4)
    mine = [(0, piece), (2, by_x), (4, by_y), (6, across)]
    return mine + [(index ^ 1, swap(values, "blk", 1)) for index, values in mine]


def gather_rows(piece, diagonal_bit):
    gathered = plane_gather(piece, diagonal_bit)
    if gathered is None:
        return [(0, lax.all_gather(piece, "blk", axis=0, tiled=True))]
    return gathered


def on_columns(body, index, width, count):
    if width % LANES == 0:
        body(pl.ds(pl.multiple_of(index * width, LANES), width))
        return
    for choice in range(count):
        pl.when(index == choice)(functools.partial(body, pl.ds(choice * width, width)))


def row_copies(sources, refs, buffer, sem, blk_index, column):
    copies = []
    for (index, _), ref in zip(sources, refs):
        rows, width = ref.shape
        first = pl.multiple_of((blk_index ^ index) * rows, 16)
        copies.append(
            pltpu.make_async_copy(
                ref, buffer.at[pl.ds(first, rows), pl.ds(column, width)], sem
            )
        )
    return copies


def attention_kernel(
    left_sources,
    right_sources,
    kv_local,
    per_group,
    place_ref,
    normed_ref,
    cos_ref,
    sin_ref,
    blocks_ref,
    cached_ref,
    own_ref,
    *refs,
):
    count_left, count_right = len(left_sources), len(right_sources)
    left = refs[:count_left]
    right = refs[count_left : count_left + count_right]
    out_ref, weights, projected, queries, keys, values, scores, probs, sem = refs[
        count_left + count_right :
    ]
    blk_index = place_ref[0]
    prefix_here = place_ref[1]
    copies = row_copies(left_sources, left, weights, sem.at[0], blk_index, 0)
    copies += row_copies(
        right_sources, right, weights, sem.at[0], blk_index, left[0].shape[1]
    )
    for copy in copies:
        copy.start()
    new_rows = normed_ref.shape[0]
    cached = blocks_ref.shape[1] * BLOCK
    span = cached + new_rows
    for head in range(kv_local):
        for block in range(blocks_ref.shape[1]):
            place = pl.ds(block * BLOCK, BLOCK)
            keys[head, :, place] = blocks_ref[0, block, head]
            values[head, place, :] = blocks_ref[1, block, head].astype(jnp.float32).T.astype(
                jnp.bfloat16
            )
    for copy in copies:
        copy.wait()

    def project(step, carry):
        rows = pl.ds(pl.multiple_of(step * TILE, TILE), TILE)
        projected[rows, :] = jnp.dot(
            normed_ref[rows, :], weights[...], preferred_element_type=jnp.float32
        )
        return carry

    lax.fori_loop(0, new_rows // TILE, project, 0)

    def rotated(rows, column):
        part = projected[rows, column : column + HD]
        turned = jnp.concatenate([part[:, HD // 2 :], part[:, : HD // 2]], axis=1)
        return part * cos_ref[rows, :] + turned * sin_ref[rows, :]

    query_width = kv_local * per_group * HD
    for chunk in range(new_rows // ROW_TILE):
        rows = pl.ds(chunk * ROW_TILE, ROW_TILE)
        for head in range(kv_local):
            for sub in range(per_group):
                queries[chunk, head, sub * ROW_TILE : (sub + 1) * ROW_TILE, :] = rotated(
                    rows, (head * per_group + sub) * HD
                ).astype(jnp.bfloat16)
            fresh = rotated(rows, query_width + head * HD)
            place = pl.ds(cached + chunk * ROW_TILE, ROW_TILE)
            keys[head, :, place] = fresh.T.astype(jnp.bfloat16)
            column = query_width + (kv_local + head) * HD
            values[head, place, :] = projected[rows, column : column + HD].astype(jnp.bfloat16)

    factor = math.log2(math.e) / math.sqrt(HD)
    group = 16

    def attend(step, carry):
        for head in range(kv_local):
            scores[...] = jnp.dot(
                queries[step, head], keys[head], preferred_element_type=jnp.float32
            )

            def soften(part, inner):
                rows = pl.ds(pl.multiple_of(part * group, group), group)
                row_id = step * ROW_TILE + lax.rem(part * group, ROW_TILE) + (
                    lax.broadcasted_iota(jnp.int32, (group, 1), 0)
                )
                floor_pos = prefix_here + row_id - WINDOW
                seen = cached_ref[...] > floor_pos
                old = jnp.where(seen, scores[rows, :cached], FLOOR_SCORE)
                own_id = lax.broadcasted_iota(jnp.int32, (1, new_rows), 1)
                seen_own = (own_ref[...] > floor_pos) & (own_id <= row_id)
                new = jnp.where(seen_own, scores[rows, cached:], FLOOR_SCORE)
                top = jnp.maximum(
                    jnp.max(old, axis=1, keepdims=True), jnp.max(new, axis=1, keepdims=True)
                )
                shift = top * factor
                old = jnp.exp2(old * factor - shift)
                new = jnp.exp2(new * factor - shift)
                total = jnp.sum(old, axis=1, keepdims=True) + jnp.sum(
                    new, axis=1, keepdims=True
                )
                probs[rows, :cached] = old.astype(jnp.bfloat16)
                probs[rows, cached:] = new.astype(jnp.bfloat16)
                scores[rows, 0:LANES] = jnp.broadcast_to(total, (group, LANES))
                return inner

            lax.fori_loop(0, per_group * ROW_TILE // group, soften, 0, unroll=2)
            summed = jnp.dot(probs[...], values[head], preferred_element_type=jnp.float32)
            summed = (summed / scores[:, 0:HD]).astype(jnp.bfloat16)
            rows = pl.ds(pl.multiple_of(step * ROW_TILE, ROW_TILE), ROW_TILE)
            for sub in range(per_group):
                column = (head * per_group + sub) * HD
                out_ref[rows, column : column + HD] = summed[
                    sub * ROW_TILE : (sub + 1) * ROW_TILE
                ]
        return carry

    lax.fori_loop(0, new_rows // ROW_TILE, attend, 0)


def attend_rows(place, normed, tables, blocks, cached_pos, own_pos, left, right, per_group):
    new_rows = normed.shape[0]
    kv_local = blocks.shape[2]
    width = left[0][1].shape[1] + right[0][1].shape[1]
    cached = blocks.shape[1] * BLOCK
    span = cached + new_rows
    heads = kv_local * per_group
    chunk_rows = per_group * ROW_TILE
    arrays = [values for _, values in left + right]
    return pl.pallas_call(
        functools.partial(attention_kernel, left, right, kv_local, per_group),
        out_shape=jax.ShapeDtypeStruct((new_rows, heads * HD), jnp.bfloat16),
        in_specs=[SMEM] + [VMEM] * 6 + [ANY] * len(arrays),
        out_specs=VMEM,
        scratch_shapes=[
            pltpu.VMEM((normed.shape[1], width), jnp.bfloat16),
            pltpu.VMEM((new_rows, width), jnp.float32),
            pltpu.VMEM((new_rows // ROW_TILE, kv_local, chunk_rows, HD), jnp.bfloat16),
            pltpu.VMEM((kv_local, HD, span), jnp.bfloat16),
            pltpu.VMEM((kv_local, span, HD), jnp.bfloat16),
            pltpu.VMEM((chunk_rows, span), jnp.float32),
            pltpu.VMEM((chunk_rows, span), jnp.bfloat16),
            pltpu.SemaphoreType.DMA((1,)),
        ],
        compiler_params=pltpu.CompilerParams(vmem_limit_bytes=VMEM_LIMIT),
        cost_estimate=pl.CostEstimate(
            flops=2 * new_rows * normed.shape[1] * width + 8 * heads * new_rows * span * LANES,
            bytes_accessed=2 * normed.shape[1] * width,
            transcendentals=heads * new_rows * span,
        ),
        name="attention",
    )(place, normed, *tables, blocks, cached_pos, own_pos, *arrays)


def middle_kernel(
    counts, groups, place_ref, tokens_ref, gain_ref, *refs
):
    att = refs[:groups]
    own_ref = refs[groups]
    left_count, right_count = counts
    rest = refs[groups + 1 :]
    left = rest[:left_count]
    right = rest[left_count : left_count + right_count]
    normed_ref, residual_ref, gathered, weights, middle, sem = rest[left_count + right_count :]
    blk_index = place_ref[0]
    kv_index = place_ref[2]
    group_rows = own_ref.shape[0]
    copies = []
    if right_count:
        copies.append(pltpu.make_async_copy(own_ref, weights.at[pl.ds(0, group_rows)], sem.at[0]))
        column = 0
        for side in (left, right):
            part, width = side[0].shape[1:]
            for index, ref in enumerate(side):
                first = pl.multiple_of((blk_index ^ XOR_ORDER[index]) * part, 16)
                for other in range(1, groups):
                    copies.append(
                        pltpu.make_async_copy(
                            ref.at[other - 1],
                            weights.at[
                                pl.ds(other * group_rows + first, part), pl.ds(column, width)
                            ],
                            sem.at[0],
                        )
                    )
            column += width
    else:
        for other in range(groups):
            first = pl.multiple_of((kv_index ^ other) * group_rows, 16)
            copies.append(
                pltpu.make_async_copy(
                    left[0].at[pl.ds(first, group_rows)],
                    weights.at[pl.ds(other * group_rows, group_rows)],
                    sem.at[0],
                )
            )
    for copy in copies:
        copy.start()
    feature = att[0].shape[1]
    for other in range(groups):
        gathered[:, other * feature : (other + 1) * feature] = att[other][...]
    for copy in copies:
        copy.wait()
    new_rows, model = tokens_ref.shape
    tile = 2 * TILE

    def product(step, carry):
        columns = pl.ds(pl.multiple_of(step * tile, tile), tile)
        summed = jnp.dot(gathered[...], weights[:, columns], preferred_element_type=jnp.float32)
        middle[:, columns] = (tokens_ref[:, columns].astype(jnp.float32) + summed).astype(
            jnp.bfloat16
        )
        return carry

    lax.fori_loop(0, model // tile, product, 0)

    def scale(step, carry):
        rows = pl.ds(pl.multiple_of(step * 16, 16), 16)
        part = middle[rows, :].astype(jnp.float32)
        mean_square = jnp.mean(part * part, axis=1, keepdims=True)
        normed_ref[rows, :] = (part * lax.rsqrt(mean_square + EPSILON) * gain_ref[...]).astype(
            jnp.bfloat16
        )
        return carry

    lax.fori_loop(0, new_rows // 16, scale, 0, unroll=2)
    out_width = model // groups

    def keep(columns):
        residual_ref[...] = middle[:, columns]

    on_columns(keep, kv_index, out_width, groups)


XOR_ORDER = (0, 2, 4, 6, 1, 3, 5, 7)


def middle_rows(place, tokens, gain, attended, own, left, right):
    new_rows, model = tokens.shape
    groups = len(attended)
    arrays = left + right
    return pl.pallas_call(
        functools.partial(middle_kernel, (len(left), len(right)), groups),
        out_shape=(
            jax.ShapeDtypeStruct((new_rows, model), jnp.bfloat16),
            jax.ShapeDtypeStruct((new_rows, model // groups), jnp.bfloat16),
        ),
        in_specs=[SMEM, VMEM, VMEM] + [VMEM] * groups + [ANY] * (1 + len(arrays)),
        out_specs=(VMEM, VMEM),
        scratch_shapes=[
            pltpu.VMEM((new_rows, model), jnp.bfloat16),
            pltpu.VMEM((model, model), jnp.bfloat16),
            pltpu.VMEM((new_rows, model), jnp.bfloat16),
            pltpu.SemaphoreType.DMA((1,)),
        ],
        compiler_params=pltpu.CompilerParams(vmem_limit_bytes=VMEM_LIMIT),
        cost_estimate=pl.CostEstimate(
            flops=2 * new_rows * model * model,
            bytes_accessed=2 * model * model,
            transcendentals=0,
        ),
        name="middle",
    )(place, tokens, gain, *attended, own, *arrays)


def hidden_chunks(width):
    whole = width // LANES * LANES
    chunks = []
    first = 0
    while first < whole:
        units = min(TILE, whole - first)
        chunks.append((first, first, whole + first, units))
        first += units
    if width > whole:
        chunks.append((whole, 2 * whole, 2 * whole + width - whole, width - whole))
    return chunks


def mlp_kernel(left_sources, right_sources, groups, widths, place_ref, normed_ref, down_ref, *refs):
    count_left, count_right = len(left_sources), len(right_sources)
    left = refs[:count_left]
    right = refs[count_left : count_left + count_right]
    outs = refs[count_left + count_right : count_left + count_right + groups]
    first_half, second_half, down, hidden, sems = refs[count_left + count_right + groups :]
    blk_index = place_ref[0]
    kv_index = place_ref[2]
    loads = (
        row_copies(left_sources, left, first_half, sems.at[0], blk_index, 0),
        row_copies(right_sources, right, second_half, sems.at[1], blk_index, 0),
        [pltpu.make_async_copy(down_ref, down, sems.at[2])],
    )
    for copies in loads:
        for copy in copies:
            copy.start()
    base = 0
    for half, (width, buffer) in enumerate(zip(widths, (first_half, second_half))):
        for copy in loads[half]:
            copy.wait()
        for first, gate, up, units in hidden_chunks(width):
            if units < LANES:
                both = jnp.dot(
                    normed_ref[...],
                    buffer[:, gate : gate + 2 * units],
                    preferred_element_type=jnp.float32,
                )
                gated, raised = both[:, :units], both[:, units:]
            else:
                gated = jnp.dot(
                    normed_ref[...],
                    buffer[:, gate : gate + units],
                    preferred_element_type=jnp.float32,
                )
                raised = jnp.dot(
                    normed_ref[...], buffer[:, up : up + units], preferred_element_type=jnp.float32
                )
            hidden[:, base + first : base + first + units] = (
                gated / (1.0 + jnp.exp(-gated)) * raised
            ).astype(jnp.bfloat16)
        base += width
    for copy in loads[2]:
        copy.wait()
    out_width = outs[0].shape[1]
    for other in range(groups):

        def product(columns, out=outs[other]):
            out[...] = jnp.dot(
                hidden[...], down[:, columns], preferred_element_type=jnp.float32
            ).astype(out.dtype)

        on_columns(product, kv_index ^ other, out_width, groups)


def mlp_parts(place, normed, w_down, left, right, groups, widths):
    new_rows, model = normed.shape
    out_width = model // groups
    arrays = [values for _, values in left + right]
    return pl.pallas_call(
        functools.partial(mlp_kernel, left, right, groups, widths),
        out_shape=tuple(
            jax.ShapeDtypeStruct((new_rows, out_width), jnp.bfloat16 if other else jnp.float32)
            for other in range(groups)
        ),
        in_specs=[SMEM, VMEM, ANY] + [ANY] * len(arrays),
        out_specs=(VMEM,) * groups,
        scratch_shapes=[
            pltpu.VMEM((model, left[0][1].shape[1]), jnp.bfloat16),
            pltpu.VMEM((model, right[0][1].shape[1]), jnp.bfloat16),
            pltpu.VMEM(w_down.shape, jnp.bfloat16),
            pltpu.VMEM((new_rows, w_down.shape[0]), jnp.bfloat16),
            pltpu.SemaphoreType.DMA((3,)),
        ],
        compiler_params=pltpu.CompilerParams(vmem_limit_bytes=VMEM_LIMIT),
        cost_estimate=pl.CostEstimate(
            flops=6 * new_rows * model * w_down.shape[0],
            bytes_accessed=6 * model * w_down.shape[0],
            transcendentals=new_rows * w_down.shape[0],
        ),
        name="mlp",
    )(place, normed, w_down, *arrays)


def shards(
    tokens,
    attn_gain,
    mlp_gain,
    w_query,
    w_key,
    w_value,
    w_gate,
    w_up,
    w_out,
    w_down,
    cache,
    slot_prompt,
    prefix_len,
    new_len,
):
    groups = lax.axis_size("kv")
    blk_index = lax.axis_index("blk")
    kv_index = lax.axis_index("kv")
    query_width = w_query.shape[1] // groups
    key_width = w_key.shape[1] // groups
    per_group = HEADS // KV_HEADS
    new_rows = tokens.shape[0]
    prompts = prefix_len.shape[0]
    slots = cache.shape[1]
    prefix_here = prefix_len[blk_index]
    live_count = new_len[blk_index]
    place = jnp.stack([blk_index, prefix_here, kv_index]).astype(jnp.int32)

    cut = half_up(query_width + 2 * key_width)
    if cut <= query_width:
        spans = (
            [(0, 0, cut)],
            [(0, cut, query_width), (1, 0, key_width), (2, 0, key_width)],
        )
    else:
        spans = (
            [(0, 0, query_width), (1, 0, cut - query_width)],
            [(1, cut - query_width, key_width), (2, 0, key_width)],
        )
    qkv = [
        gather_rows(exchange(group_columns((w_query, w_key, w_value), groups, span)), bit)
        for span, bit in zip(spans, (2, 4))
    ]

    global_rank, local_rank = slot_ranks(slot_prompt, prompts, slots)
    own_prompts = lax.dynamic_slice_in_dim(slot_prompt, blk_index * slots, slots)
    own_ranks = lax.dynamic_slice_in_dim(local_rank, blk_index * slots, slots)
    placed = own_prompts * CAP + own_ranks
    buffer_ids = jnp.arange(prompts * CAP, dtype=jnp.int32)
    matches = placed[None, :] == buffer_ids[:, None]
    source_slot = jnp.sum(
        jnp.where(matches, jnp.arange(slots, dtype=jnp.int32)[None, :], 0), axis=1
    )
    outgoing = jnp.take(cache, source_slot, axis=1)
    arrived = lax.all_to_all(outgoing, "blk", split_axis=1, concat_axis=1, tiled=True)
    slot_ids = jnp.arange(prompts * slots, dtype=jnp.int32)
    landing = slot_ids // slots * CAP + local_rank
    for_me = slot_prompt == blk_index
    received = (landing[None, :] == buffer_ids[:, None]) & for_me[None, :]
    block_number = jnp.sum(jnp.where(received, global_rank[None, :], 0), axis=1)
    block_live = jnp.any(received, axis=1)
    key_pos = block_number[:, None] * BLOCK + jnp.arange(BLOCK, dtype=jnp.int32)[None, :]
    key_live = block_live[:, None] & (key_pos < prefix_here)
    cached_pos = jnp.where(key_live, jnp.where(key_pos < SINKS, FAR, key_pos), -FAR)
    cached_pos = cached_pos.reshape(1, -1)
    row_ids = jnp.arange(new_rows, dtype=jnp.int32)
    positions = prefix_here + row_ids
    own_pos = jnp.where(
        row_ids < live_count, jnp.where(positions < SINKS, FAR, positions), -FAR
    ).reshape(1, -1)

    normed = rms_scale(tokens, attn_gain)
    tables = rope_tables(positions)

    eighth = w_out.shape[0] // lax.axis_size("blk")
    if lax.axis_size("blk") == 8 and eighth % 16 == 0:
        share = lax.dynamic_slice_in_dim(w_out, blk_index * eighth, eighth, 0)
        shares = jnp.stack([swap(share, "kv", other) for other in range(1, groups)], axis=0)
        side = half_up(w_out.shape[1])
        out_sides = [
            [values for _, values in gather_rows(shares[:, :, :side], 2)],
            [values for _, values in gather_rows(shares[:, :, side:], 4)],
        ]
    else:
        out_sides = [[lax.all_gather(w_out, "kv", axis=0, tiled=True)], []]

    hidden_width = w_gate.shape[1] // groups
    cut = half_up(hidden_width)
    widths = (cut, hidden_width - cut)
    pair = []
    for first, last, bit in ((0, cut, 2), (cut, hidden_width, 4)):
        whole = first + (last - first) // LANES * LANES
        span = [(0, first, whole), (1, first, whole)]
        if whole < last:
            span += [(0, whole, last), (1, whole, last)]
        pair.append(gather_rows(exchange(group_columns((w_gate, w_up), groups, span)), bit))

    attended = attend_rows(
        place, normed, tables, arrived, cached_pos, own_pos, qkv[0], qkv[1], per_group
    )
    everyone = [attended] + [swap(attended, "kv", other) for other in range(1, groups)]
    normed_mid, residual = middle_rows(
        place, tokens, mlp_gain.reshape(1, -1), everyone, w_out, out_sides[0], out_sides[1]
    )
    parts = mlp_parts(place, normed_mid, w_down, pair[0], pair[1], groups, widths)
    reduced = parts[0]
    for other in range(1, groups):
        reduced = reduced + swap(parts[other], "kv", other).astype(jnp.float32)
    mixed = jnp.where(
        (row_ids < live_count)[:, None], residual.astype(jnp.float32) + reduced, 0.0
    )
    return mixed.astype(jnp.bfloat16)


def solution(mesh):
    return jax.shard_map(
        shards,
        mesh=mesh,
        in_specs=(
            P("blk", None),
            P(),
            P(),
            P(("blk", "kv"), None),
            P(("blk", "kv"), None),
            P(("blk", "kv"), None),
            P(("blk", "kv"), None),
            P(("blk", "kv"), None),
            P("kv", None),
            P("kv", None),
            P(None, "blk", "kv", None, None),
            P(),
            P(),
            P(),
        ),
        out_specs=P("blk", "kv"),
        check_vma=False,
    )
```

time: 449 us -> 474 us (1.056)
  the two profiles are of different devices: /device:TPU:0 before, /device:TPU:12 now
where the time goes in v2:
time: 474 us; the launch traced here: 473 us
  waiting for transfers between devices  230 us (49%)
  Pallas kernels  130 us (27%)
  starting transfers between devices  62 us (13%)
  other arithmetic  30.8 us (6%)
  local copies, waits for them, and re-layouts  20.8 us (4%)
    ppermute x51, waiting for transfers between devices, swap(): return lax.ppermute(values, axis, pairs)  201 us
    pallas_call x1, Pallas kernels, attend_rows(): pl.pallas_call(functools.partial(attention_kernel, left, right, kv_local,...  86 us
    ppermute x51, starting transfers between devices, swap(): return lax.ppermute(values, axis, pairs)  33.1 us
    all_to_all x4, starting transfers between devices, exchange(): lax.all_to_all(packed, 'kv', split_axis=0, concat_axis=0, tiled=True)  24.7 us
    pallas_call x1, Pallas kernels, mlp_parts(): pl.pallas_call(functools.partial(mlp_kernel, left, right, groups, widths)...  24.6 us
    all_to_all x4, waiting for transfers between devices, exchange(): lax.all_to_all(packed, 'kv', split_axis=0, concat_axis=0, tiled=True)  20.1 us
    pallas_call x1, Pallas kernels, middle_rows(): pl.pallas_call(functools.partial(middle_kernel, (len(left), len(right)),...  19 us
  transfers between devices with their start and end apart: 56, of which 18 were waited for; matrix products, arithmetic and copies ran while one was open for 9% of the time, Pallas kernels for 22%

profile of v2, /device:TPU:12, one launch (start us, length us, event | category | flops | bytes accessed | tf_op | source)
XLA Modules:
  0.0 473.5 jit_solution(14182883657906862224)
XLA Ops:
  0.0 1.9 constant_dynamic-slice_fusion
  2.4 2.6 collective-permute-start.18
  9.9 6.2 %all-to-all-start.2 = ((bf16[4,80,448]{2,1,0:T(8,128)(2,1)}), bf16[4,80,448]{2,1,0:T(8,128)(2,1)}, u32[]{:S(2)}, u32[]{:S(2)}) async-start(bf16[4,80,448]{2,1,0:T(8,128)(2,1)} %maximum_maximum_fusion.1), calls=%async_computation.2 | async-start | bytes 655360 | tf_op jit(solution)/shard_map/all_to_all | solution.py:84
  19.2 1.7 slice_bitcast_fusion.19
  24.1 2.1 fusion.2.normed_ref
  27.9 1.2 select_bitcast_fusion
  29.1 18.0 %all-to-all-done.2 = bf16[4,80,448]{2,1,0:T(8,128)(2,1)} async-done(((bf16[4,80,448]{2,1,0:T(8,128)(2,1)}), bf16[4,80,448]{2,1,0:T(8,128)(2,1)}, u32[]{:S(2)}, u32[]{:S(2)}) %all-to-all-start.2) | async-done | bytes 286752 | tf_op jit(solution)/shard_map/all_to_all | solution.py:84
  47.2 6.4 %all-to-all-start.1 = ((bf16[4,80,512]{2,1,0:T(8,128)(2,1)}), bf16[4,80,512]{2,1,0:T(8,128)(2,1)}, u32[]{:S(2)}, u32[]{:S(2)}) async-start(bf16[4,80,512]{2,1,0:T(8,128)(2,1)} %pad_maximum_fusion.2), calls=%async_computation.1 | async-start | bytes 655360 | tf_op jit(solution)/shard_map/all_to_all | solution.py:84
  53.7 1.9 convert.125
  57.3 1.2 slice_bitcast_fusion.6
  58.6 2.1 all-to-all-done.1
  60.6 4.2 all-to-all-start
  64.9 2.4 maximum_maximum_fusion
  67.3 1.4 pad_maximum_fusion
  68.7 1.5 collective-permute-start.7
  71.9 1.5 collective-permute-start.21
  73.9 8.2 %all-to-all-done = bf16[2,16,2,80,128]{4,3,2,0,1:T(8,128)(2,1)S(1)} async-done(((bf16[2,16,2,80,128]{4,3,2,0,1:T(8,128)(2,1)}), bf16[2,16,2,80,128]{4,3,2,0,1:T(8,128)(2,1)S(1)}, u32[]{:S(2)}, u32[]{:S(2)}) %all-to-all-start) | async-done | bytes 1310752 | tf_op jit(solution)/shard_map/all_to_all | solution.py:542
  82.1 6.4 %all-to-all-start.3 = ((bf16[4,80,1792]{2,1,0:T(8,128)(2,1)}), bf16[4,80,1792]{2,1,0:T(8,128)(2,1)}, u32[]{:S(2)}, u32[]{:S(2)}) async-start(bf16[4,80,1792]{2,1,0:T(8,128)(2,1)} %maximum_maximum_fusion), calls=%async_computation.3 | async-start | bytes 2293760 | tf_op jit(solution)/shard_map/all_to_all | solution.py:84
  90.2 1.2 fusion.6.cached_ref
  92.1 15.9 %collective-permute-done.1.refs_2_ = bf16[320,512]{1,0:T(8,128)(2,1)} collective-permute-done((bf16[320,512]{1,0:T(8,128)(2,1)}, bf16[320,512]{1,0:T(8,128)(2,1)}, u32[]{:S(2)}, u32[]{:S(2)}) %collective-permute-start.1) | collective-permute-done | bytes 327712 | tf_op jit(solution)/shard_map/ppermute | solution.py:65
  108.0 1.3 collective-permute-start.27
  110.5 4.3 collective-permute-done.9.refs_11_
  114.8 1.5 collective-permute-start.20
  117.3 1.7 collective-permute-start.28
  121.8 3.2 collective-permute-done.27.refs_14_
  125.0 1.3 collective-permute-start.2
  126.3 1.8 compare_select_fusion.2.own_ref
  128.1 10.1 %collective-permute-done.20.refs_6_ = bf16[3,80,1280]{2,1,0:T(8,128)(2,1)} collective-permute-done((bf16[3,80,1280]{2,1,0:T(8,128)(2,1)}, bf16[3,80,1280]{2,1,0:T(8,128)(2,1)}, u32[]{:S(2)}, u32[]{:S(2)}) %collective-permute-start.20) | collective-permute-done | bytes 614432 | tf_op jit(solution)/shard_map/ppermute | solution.py:65
  138.2 1.3 collective-permute-start.22
  141.3 4.0 collective-permute-done.2.refs_3_
  145.2 1.2 pad_add_fusion.place_ref
  152.1 5.7 %all-to-all-start.4 = ((bf16[4,80,1664]{2,1,0:T(8,128)(2,1)}), bf16[4,80,1664]{2,1,0:T(8,128)(2,1)S(1)}, u32[]{:S(2)}, u32[]{:S(2)}) async-start(bf16[4,80,1664]{2,1,0:T(8,128)(2,1)} %pad_maximum_fusion.1), calls=%async_computation.4 | async-start | bytes 2129920 | tf_op jit(solution)/shard_map/all_to_all | solution.py:84
  158.0 2.0 collective-permute-start.29
  160.6 86.0 %attention.1.refs_0_ = bf16[512,640]{1,0:T(8,128)(2,1)} custom-call(s32[3]{0:T(128)} %pad_add_fusion.place_ref, bf16[512,2560]{1,0:T(8,128)(2,1)} %fusion.2.normed_ref, f32[512,80]{1,0:T(8,128)} %get-tuple-element.62.cos_ref, f32[512,80]{1,0:T(8,128)} %get-tuple-element.63.sin_ref, bf16[2,16,2,80,128]{4,3,2,1,0:T(8,128)(2,1)} %copy.19.blocks_ref, ...), custom_call_target="tpu_custom_call" | custom-call | flops 13254000640 | bytes 4915200 | tf_op jit(solution)/shard_map/attention/pallas_call | solution.py:255
  247.3 2.3 collective-permute-start.15
  251.5 24.2 %collective-permute-done.14.refs_1_ = bf16[512,640]{1,0:T(8,128)(2,1)S(1)} collective-permute-done((bf16[512,640]{1,0:T(8,128)(2,1)}, bf16[512,640]{1,0:T(8,128)(2,1)S(1)}, u32[]{:S(2)}, u32[]{:S(2)}) %collective-permute-start.14) | collective-permute-done | bytes 655392 | tf_op jit(solution)/shard_map/ppermute | solution.py:65
  276.7 16.5 %collective-permute-done.15.refs_2_ = bf16[512,640]{1,0:T(8,128)(2,1)S(1)} collective-permute-done((bf16[512,640]{1,0:T(8,128)(2,1)}, bf16[512,640]{1,0:T(8,128)(2,1)S(1)}, u32[]{:S(2)}, u32[]{:S(2)}) %collective-permute-start.15) | collective-permute-done | bytes 655392 | tf_op jit(solution)/shard_map/ppermute | solution.py:65
  293.4 14.0 %collective-permute-done.16.refs_3_ = bf16[512,640]{1,0:T(8,128)(2,1)} collective-permute-done((bf16[512,640]{1,0:T(8,128)(2,1)}, bf16[512,640]{1,0:T(8,128)(2,1)}, u32[]{:S(2)}, u32[]{:S(2)}) %collective-permute-start.16) | collective-permute-done | bytes 655392 | tf_op jit(solution)/shard_map/ppermute | solution.py:65
  307.9 2.9 collective-permute-done.33.refs_20_
  313.2 25.9 %collective-permute-done.34.refs_1_ = bf16[320,1792]{1,0:T(8,128)(2,1)S(1)} collective-permute-done((bf16[320,1792]{1,0:T(8,128)(2,1)}, bf16[320,1792]{1,0:T(8,128)(2,1)S(1)}, u32[]{:S(2)}, u32[]{:S(2)}) %collective-permute-start.34) | collective-permute-done | bytes 1146912 | tf_op jit(solution)/shard_map/ppermute | solution.py:65
  339.7 23.5 %collective-permute-done.36.refs_3_ = bf16[320,1792]{1,0:T(8,128)(2,1)S(1)} collective-permute-done((bf16[320,1792]{1,0:T(8,128)(2,1)S(1)}, bf16[320,1792]{1,0:T(8,128)(2,1)S(1)}, u32[]{:S(2)}, u32[]{:S(2)}) %collective-permute-start.36) | collective-permute-done | bytes 1146912 | tf_op jit(solution)/shard_map/ppermute | solution.py:65
  365.4 19.0 %middle.1 = (bf16[512,2560]{1,0:T(8,128)(2,1)}, bf16[512,640]{1,0:T(8,128)(2,1)}) custom-call(s32[3]{0:T(128)} %pad_add_fusion.place_ref, bf16[512,2560]{1,0:T(8,128)(2,1)} %tokens_ref.1, f32[1,2560]{1,0:T(1,128)} %reshape.713.gain_ref, bf16[512,640]{1,0:T(8,128)(2,1)} %attention.1.refs_0_, bf16[512,640]{1,0:T(8,128)(2,1)} %copy-done.26, ...), custom_call_target="tpu_custom_call" | custom-call | flops 6710886400 | bytes 13107200 | tf_op jit(solution)/shard_map/middle/pallas_call | solution.py:367
  385.5 24.6 %mlp.1 = (f32[512,640]{1,0:T(8,128)}, bf16[512,640]{1,0:T(8,128)(2,1)}, bf16[512,640]{1,0:T(8,128)(2,1)}, bf16[512,640]{1,0:T(8,128)(2,1)}) custom-call(s32[3]{0:T(128)} %pad_add_fusion.place_ref, bf16[512,2560]{1,0:T(8,128)(2,1)} %get-tuple-element.12.normed_ref, bf16[1728,2560]{1,0:T(8,128)(2,1)} %down_ref.1, bf16[320,1792]{1,0:T(8,128)(2,1)} %bitcast.37.refs_0_, ...), custom_call_target="tpu_custom_call" | custom-call | flops 13589544960 | bytes 26542080 | tf_op jit(solution)/shard_map/mlp/pallas_call | solution.py:462
  410.2 2.9 collective-permute-start.49
  414.2 24.7 %collective-permute-done.48 = bf16[512,640]{1,0:T(8,128)(2,1)S(1)} collective-permute-done((bf16[512,640]{1,0:T(8,128)(2,1)}, bf16[512,640]{1,0:T(8,128)(2,1)S(1)}, u32[]{:S(2)}, u32[]{:S(2)}) %collective-permute-start.48) | collective-permute-done | bytes 655392 | tf_op jit(solution)/shard_map/ppermute | solution.py:65
  438.9 17.7 %collective-permute-done.49 = bf16[512,640]{1,0:T(8,128)(2,1)S(1)} collective-permute-done((bf16[512,640]{1,0:T(8,128)(2,1)}, bf16[512,640]{1,0:T(8,128)(2,1)S(1)}, u32[]{:S(2)}, u32[]{:S(2)}) %collective-permute-start.49) | collective-permute-done | bytes 655392 | tf_op jit(solution)/shard_map/ppermute | solution.py:65
  456.6 14.2 %collective-permute-done.50 = bf16[512,640]{1,0:T(8,128)(2,1)S(1)} collective-permute-done((bf16[512,640]{1,0:T(8,128)(2,1)}, bf16[512,640]{1,0:T(8,128)(2,1)S(1)}, u32[]{:S(2)}, u32[]{:S(2)}) %collective-permute-start.50) | collective-permute-done | bytes 655392 | tf_op jit(solution)/shard_map/ppermute | solution.py:65
  470.8 2.6 select_convert_fusion
  (205 shorter events, 44.5 us)
Async XLA Ops:
  1.9 65.4 %collective-permute-start.17 = (bf16[80,2560]{1,0:T(8,128)(2,1)}, bf16[80,2560]{1,0:T(8,128)(2,1)}, u32[]{:S(2)}, u32[]{:S(2)}) collective-permute-start(bf16[80,2560]{1,0:T(8,128)(2,1)} %constant_dynamic-slice_fusion), channel_id=1, source_target_pairs={{0,1},{1,0},{2,3},{3,2},{4,5},{5,4},{6,7},{7,6},{8,9},{9,8},{10,11... | collective-permute-start | bytes 1228808 | tf_op jit(solution)/shard_map/ppermute | solution.py:65
  2.4 64.9 %collective-permute-start.18 = (bf16[80,2560]{1,0:T(8,128)(2,1)}, bf16[80,2560]{1,0:T(8,128)(2,1)}, u32[]{:S(2)}, u32[]{:S(2)}) collective-permute-start(bf16[80,2560]{1,0:T(8,128)(2,1)} %constant_dynamic-slice_fusion), channel_id=1, source_target_pairs={{0,2},{1,3},{2,0},{3,1},{4,6},{5,7},{6,4},{7,5},{8,10},{9,11},{10,... | collective-permute-start | bytes 1228808 | tf_op jit(solution)/shard_map/ppermute | solution.py:65
  4.9 62.3 %collective-permute-start.19 = (bf16[80,2560]{1,0:T(8,128)(2,1)}, bf16[80,2560]{1,0:T(8,128)(2,1)}, u32[]{:S(2)}, u32[]{:S(2)}) collective-permute-start(bf16[80,2560]{1,0:T(8,128)(2,1)} %constant_dynamic-slice_fusion), channel_id=1, source_target_pairs={{0,3},{1,2},{2,1},{3,0},{4,7},{5,6},{6,5},{7,4},{8,11},{9,10},{10,... | collective-permute-start | bytes 1228808 | tf_op jit(solution)/shard_map/ppermute | solution.py:65
  9.9 37.3 %all-to-all-start.2 = ((bf16[4,80,448]{2,1,0:T(8,128)(2,1)}), bf16[4,80,448]{2,1,0:T(8,128)(2,1)}, u32[]{:S(2)}, u32[]{:S(2)}) async-start(bf16[4,80,448]{2,1,0:T(8,128)(2,1)} %maximum_maximum_fusion.1), calls=%async_computation.2 | async-start | bytes 655360 | tf_op jit(solution)/shard_map/all_to_all | solution.py:84
  60.6 21.5 %all-to-all-start = ((bf16[2,16,2,80,128]{4,3,2,0,1:T(8,128)(2,1)}), bf16[2,16,2,80,128]{4,3,2,0,1:T(8,128)(2,1)S(1)}, u32[]{:S(2)}, u32[]{:S(2)}) async-start(bf16[2,16,2,80,128]{4,3,2,0,1:T(8,128)(2,1)} %select_bitcast_fusion), calls=%async_computation | async-start | bytes 2621440 | tf_op jit(solution)/shard_map/all_to_all | solution.py:542
  68.7 20.1 %collective-permute-start.7 = (bf16[320,448]{1,0:T(8,128)(2,1)}, bf16[320,448]{1,0:T(8,128)(2,1)}, u32[]{:S(2)}, u32[]{:S(2)}) collective-permute-start(bf16[320,448]{1,0:T(8,128)(2,1)} %bitcast.25.refs_8_), channel_id=1, source_target_pairs={{0,8},{4,12},{8,0},{12,4},{16,24},{20,28},{24,16},{28,20},{1,9},{5... | collective-permute-start | bytes 860168 | tf_op jit(solution)/shard_map/ppermute | solution.py:65
  70.2 19.1 %collective-permute-start.8 = (bf16[320,448]{1,0:T(8,128)(2,1)}, bf16[320,448]{1,0:T(8,128)(2,1)}, u32[]{:S(2)}, u32[]{:S(2)}) collective-permute-start(bf16[320,448]{1,0:T(8,128)(2,1)} %bitcast.25.refs_8_), channel_id=1, source_target_pairs={{0,16},{4,20},{8,24},{12,28},{16,0},{20,4},{24,8},{28,12},{1,17},{... | collective-permute-start | bytes 860168 | tf_op jit(solution)/shard_map/ppermute | solution.py:65
  70.8 18.6 %collective-permute-start.10 = (bf16[320,448]{1,0:T(8,128)(2,1)}, bf16[320,448]{1,0:T(8,128)(2,1)}, u32[]{:S(2)}, u32[]{:S(2)}) collective-permute-start(bf16[320,448]{1,0:T(8,128)(2,1)} %bitcast.25.refs_8_), channel_id=1, source_target_pairs={{0,4},{4,0},{8,12},{12,8},{16,20},{20,16},{24,28},{28,24},{1,5},{5... | collective-permute-start | bytes 860168 | tf_op jit(solution)/shard_map/ppermute | solution.py:65
  71.9 47.1 %collective-permute-start.21 = (bf16[3,80,1280]{2,1,0:T(8,128)(2,1)}, bf16[3,80,1280]{2,1,0:T(8,128)(2,1)}, u32[]{:S(2)}, u32[]{:S(2)}) collective-permute-start(bf16[3,80,1280]{2,1,0:T(8,128)(2,1)} %get-tuple-element.18.refs_5_), channel_id=1, source_target_pairs={{0,16},{4,20},{8,24},{12,28},{16,0},{20,4},{24,8},{28,12},{1,17},{... | collective-permute-start | bytes 1843208 | tf_op jit(solution)/shard_map/ppermute | solution.py:65
  73.4 34.6 %collective-permute-start.1 = (bf16[320,512]{1,0:T(8,128)(2,1)}, bf16[320,512]{1,0:T(8,128)(2,1)}, u32[]{:S(2)}, u32[]{:S(2)}) collective-permute-start(bf16[320,512]{1,0:T(8,128)(2,1)} %bitcast.12.refs_0_), channel_id=1, source_target_pairs={{0,16},{4,20},{8,24},{12,28},{16,0},{20,4},{24,8},{28,12},{1,17},{... | collective-permute-start | bytes 983048 | tf_op jit(solution)/shard_map/ppermute | solution.py:65
  82.1 70.0 %all-to-all-start.3 = ((bf16[4,80,1792]{2,1,0:T(8,128)(2,1)}), bf16[4,80,1792]{2,1,0:T(8,128)(2,1)}, u32[]{:S(2)}, u32[]{:S(2)}) async-start(bf16[4,80,1792]{2,1,0:T(8,128)(2,1)} %maximum_maximum_fusion), calls=%async_computation.3 | async-start | bytes 2293760 | tf_op jit(solution)/shard_map/all_to_all | solution.py:84
  88.8 20.5 %collective-permute-start = (bf16[320,512]{1,0:T(8,128)(2,1)}, bf16[320,512]{1,0:T(8,128)(2,1)}, u32[]{:S(2)}, u32[]{:S(2)}) collective-permute-start(bf16[320,512]{1,0:T(8,128)(2,1)} %bitcast.12.refs_0_), channel_id=1, source_target_pairs={{0,8},{4,12},{8,0},{12,4},{16,24},{20,28},{24,16},{28,20},{1,9},{5... | collective-permute-start | bytes 983048 | tf_op jit(solution)/shard_map/ppermute | solution.py:65
  89.3 19.9 %collective-permute-start.3 = (bf16[320,512]{1,0:T(8,128)(2,1)}, bf16[320,512]{1,0:T(8,128)(2,1)S(1)}, u32[]{:S(2)}, u32[]{:S(2)}) collective-permute-start(bf16[320,512]{1,0:T(8,128)(2,1)} %bitcast.12.refs_0_), channel_id=1, source_target_pairs={{0,4},{4,0},{8,12},{12,8},{16,20},{20,16},{24,28},{28,24},{1,5},{5... | collective-permute-start | bytes 983048 | tf_op jit(solution)/shard_map/ppermute | solution.py:65
  89.4 25.4 %collective-permute-start.9 = (bf16[320,448]{1,0:T(8,128)(2,1)}, bf16[320,448]{1,0:T(8,128)(2,1)}, u32[]{:S(2)}, u32[]{:S(2)}) collective-permute-start(bf16[320,448]{1,0:T(8,128)(2,1)} %collective-permute-done.7.refs_9_), channel_id=1, source_target_pairs={{0,16},{4,20},{8,24},{12,28},{16,0},{20,4},{24,8},{28,12},{1,17},{... | collective-permute-start | bytes 860168 | tf_op jit(solution)/shard_map/ppermute | solution.py:65
  114.8 23.4 %collective-permute-start.20 = (bf16[3,80,1280]{2,1,0:T(8,128)(2,1)}, bf16[3,80,1280]{2,1,0:T(8,128)(2,1)}, u32[]{:S(2)}, u32[]{:S(2)}) collective-permute-start(bf16[3,80,1280]{2,1,0:T(8,128)(2,1)} %get-tuple-element.18.refs_5_), channel_id=1, source_target_pairs={{0,8},{4,12},{8,0},{12,4},{16,24},{20,28},{24,16},{28,20},{1,9},{5... | collective-permute-start | bytes 1843208 | tf_op jit(solution)/shard_map/ppermute | solution.py:65
  117.3 23.3 %collective-permute-start.28 = (bf16[3,80,1280]{2,1,0:T(8,128)(2,1)}, bf16[3,80,1280]{2,1,0:T(8,128)(2,1)}, u32[]{:S(2)}, u32[]{:S(2)}) collective-permute-start(bf16[3,80,1280]{2,1,0:T(8,128)(2,1)} %get-tuple-element.17.refs_13_), channel_id=1, source_target_pairs={{0,16},{4,20},{8,24},{12,28},{16,0},{20,4},{24,8},{28,12},{1,17},{... | collective-permute-start | bytes 1843208 | tf_op jit(solution)/shard_map/ppermute | solution.py:65
  119.0 21.7 %collective-permute-start.23 = (bf16[3,80,1280]{2,1,0:T(8,128)(2,1)}, bf16[3,80,1280]{2,1,0:T(8,128)(2,1)}, u32[]{:S(2)}, u32[]{:S(2)}) collective-permute-start(bf16[3,80,1280]{2,1,0:T(8,128)(2,1)} %get-tuple-element.18.refs_5_), channel_id=1, source_target_pairs={{0,4},{4,0},{8,12},{12,8},{16,20},{20,16},{24,28},{28,24},{1,5},{5... | collective-permute-start | bytes 1843208 | tf_op jit(solution)/shard_map/ppermute | solution.py:65
  119.0 22.2 %collective-permute-start.30 = (bf16[3,80,1280]{2,1,0:T(8,128)(2,1)}, bf16[3,80,1280]{2,1,0:T(8,128)(2,1)}, u32[]{:S(2)}, u32[]{:S(2)}) collective-permute-start(bf16[3,80,1280]{2,1,0:T(8,128)(2,1)} %get-tuple-element.17.refs_13_), channel_id=1, source_target_pairs={{0,4},{4,0},{8,12},{12,8},{16,20},{20,16},{24,28},{28,24},{1,5},{5... | collective-permute-start | bytes 1843208 | tf_op jit(solution)/shard_map/ppermute | solution.py:65
  125.0 20.2 %collective-permute-start.2 = (bf16[320,512]{1,0:T(8,128)(2,1)}, bf16[320,512]{1,0:T(8,128)(2,1)}, u32[]{:S(2)}, u32[]{:S(2)}) collective-permute-start(bf16[320,512]{1,0:T(8,128)(2,1)} %collective-permute-done.1.refs_2_), channel_id=1, source_target_pairs={{0,8},{4,12},{8,0},{12,4},{16,24},{20,28},{24,16},{28,20},{1,9},{5... | collective-permute-start | bytes 983048 | tf_op jit(solution)/shard_map/ppermute | solution.py:65
  138.2 22.3 %collective-permute-start.22 = (bf16[3,80,1280]{2,1,0:T(8,128)(2,1)}, bf16[3,80,1280]{2,1,0:T(8,128)(2,1)}, u32[]{:S(2)}, u32[]{:S(2)}) collective-permute-start(bf16[3,80,1280]{2,1,0:T(8,128)(2,1)} %collective-permute-done.21.refs_7_), channel_id=1, source_target_pairs={{0,8},{4,12},{8,0},{12,4},{16,24},{20,28},{24,16},{28,20},{1,9},{5... | collective-permute-start | bytes 1843208 | tf_op jit(solution)/shard_map/ppermute | solution.py:65
  140.7 17.3 %collective-permute-start.4 = (bf16[320,512]{1,0:T(8,128)(2,1)}, bf16[320,512]{1,0:T(8,128)(2,1)S(1)}, u32[]{:S(2)}, u32[]{:S(2)}) collective-permute-start(bf16[320,512]{1,0:T(8,128)(2,1)} %collective-permute-done.refs_1_), channel_id=1, source_target_pairs={{0,4},{4,0},{8,12},{12,8},{16,20},{20,16},{24,28},{28,24},{1,5},{5... | collective-permute-start | bytes 983048 | tf_op jit(solution)/shard_map/ppermute | solution.py:65
  141.2 18.8 %collective-permute-start.13 = (bf16[320,448]{1,0:T(8,128)(2,1)}, bf16[320,448]{1,0:T(8,128)(2,1)}, u32[]{:S(2)}, u32[]{:S(2)}) collective-permute-start(bf16[320,448]{1,0:T(8,128)(2,1)} %collective-permute-done.9.refs_11_), channel_id=1, source_target_pairs={{0,4},{4,0},{8,12},{12,8},{16,20},{20,16},{24,28},{28,24},{1,5},{5... | collective-permute-start | bytes 860168 | tf_op jit(solution)/shard_map/ppermute | solution.py:65
  152.1 99.4 %all-to-all-start.4 = ((bf16[4,80,1664]{2,1,0:T(8,128)(2,1)}), bf16[4,80,1664]{2,1,0:T(8,128)(2,1)S(1)}, u32[]{:S(2)}, u32[]{:S(2)}) async-start(bf16[4,80,1664]{2,1,0:T(8,128)(2,1)} %pad_maximum_fusion.1), calls=%async_computation.4 | async-start | bytes 2129920 | tf_op jit(solution)/shard_map/all_to_all | solution.py:84
  157.8 89.5 %collective-permute-start.25 = (bf16[3,80,1280]{2,1,0:T(8,128)(2,1)}, bf16[3,80,1280]{2,1,0:T(8,128)(2,1)S(1)}, u32[]{:S(2)}, u32[]{:S(2)}) collective-permute-start(bf16[3,80,1280]{2,1,0:T(8,128)(2,1)} %collective-permute-done.21.refs_7_), channel_id=1, source_target_pairs={{0,4},{4,0},{8,12},{12,8},{16,20},{20,16},{24,28},{28,24},{1,5},{5... | collective-permute-start | bytes 1843208 | tf_op jit(solution)/shard_map/ppermute | solution.py:65
  158.0 88.6 %collective-permute-start.29 = (bf16[3,80,1280]{2,1,0:T(8,128)(2,1)}, bf16[3,80,1280]{2,1,0:T(8,128)(2,1)S(1)}, u32[]{:S(2)}, u32[]{:S(2)}) collective-permute-start(bf16[3,80,1280]{2,1,0:T(8,128)(2,1)} %collective-permute-done.27.refs_14_), channel_id=1, source_target_pairs={{0,16},{4,20},{8,24},{12,28},{16,0},{20,4},{24,8},{28,12},{1,17},{... | collective-permute-start | bytes 1843208 | tf_op jit(solution)/shard_map/ppermute | solution.py:65
  160.0 89.6 %collective-permute-start.31 = (bf16[3,80,1280]{2,1,0:T(8,128)(2,1)}, bf16[3,80,1280]{2,1,0:T(8,128)(2,1)S(1)}, u32[]{:S(2)}, u32[]{:S(2)}) collective-permute-start(bf16[3,80,1280]{2,1,0:T(8,128)(2,1)} %collective-permute-done.27.refs_14_), channel_id=1, source_target_pairs={{0,4},{4,0},{8,12},{12,8},{16,20},{20,16},{24,28},{28,24},{1,5},{5... | collective-permute-start | bytes 1843208 | tf_op jit(solution)/shard_map/ppermute | solution.py:65
  160.0 90.2 %collective-permute-start.24 = (bf16[3,80,1280]{2,1,0:T(8,128)(2,1)}, bf16[3,80,1280]{2,1,0:T(8,128)(2,1)S(1)}, u32[]{:S(2)}, u32[]{:S(2)}) collective-permute-start(bf16[3,80,1280]{2,1,0:T(8,128)(2,1)} %collective-permute-done.20.refs_6_), channel_id=1, source_target_pairs={{0,4},{4,0},{8,12},{12,8},{16,20},{20,16},{24,28},{28,24},{1,5},{5... | collective-permute-start | bytes 1843208 | tf_op jit(solution)/shard_map/ppermute | solution.py:65
  160.5 89.7 %collective-permute-start.32 = (bf16[3,80,1280]{2,1,0:T(8,128)(2,1)}, bf16[3,80,1280]{2,1,0:T(8,128)(2,1)S(1)}, u32[]{:S(2)}, u32[]{:S(2)}) collective-permute-start(bf16[3,80,1280]{2,1,0:T(8,128)(2,1)} %collective-permute-done.28.refs_15_), channel_id=1, source_target_pairs={{0,4},{4,0},{8,12},{12,8},{16,20},{20,16},{24,28},{28,24},{1,5},{5... | collective-permute-start | bytes 1843208 | tf_op jit(solution)/shard_map/ppermute | solution.py:65
  246.6 29.1 %collective-permute-start.14 = (bf16[512,640]{1,0:T(8,128)(2,1)}, bf16[512,640]{1,0:T(8,128)(2,1)S(1)}, u32[]{:S(2)}, u32[]{:S(2)}) collective-permute-start(bf16[512,640]{1,0:T(8,128)(2,1)} %attention.1.refs_0_), channel_id=1, source_target_pairs={{0,1},{1,0},{2,3},{3,2},{4,5},{5,4},{6,7},{7,6},{8,9},{9,8},{10,11... | collective-permute-start | bytes 1966088 | tf_op jit(solution)/shard_map/ppermute | solution.py:65
  247.3 45.9 %collective-permute-start.15 = (bf16[512,640]{1,0:T(8,128)(2,1)}, bf16[512,640]{1,0:T(8,128)(2,1)S(1)}, u32[]{:S(2)}, u32[]{:S(2)}) collective-permute-start(bf16[512,640]{1,0:T(8,128)(2,1)} %attention.1.refs_0_), channel_id=1, source_target_pairs={{0,2},{1,3},{2,0},{3,1},{4,6},{5,7},{6,4},{7,5},{8,10},{9,11},{10,... | collective-permute-start | bytes 1966088 | tf_op jit(solution)/shard_map/ppermute | solution.py:65
  249.6 57.8 %collective-permute-start.16 = (bf16[512,640]{1,0:T(8,128)(2,1)}, bf16[512,640]{1,0:T(8,128)(2,1)}, u32[]{:S(2)}, u32[]{:S(2)}) collective-permute-start(bf16[512,640]{1,0:T(8,128)(2,1)} %attention.1.refs_0_), channel_id=1, source_target_pairs={{0,3},{1,2},{2,1},{3,0},{4,7},{5,6},{6,5},{7,4},{8,11},{9,10},{10,... | collective-permute-start | bytes 1966088 | tf_op jit(solution)/shard_map/ppermute | solution.py:65
  250.2 57.3 %collective-permute-start.26 = (bf16[3,80,1280]{2,1,0:T(8,128)(2,1)}, bf16[3,80,1280]{2,1,0:T(8,128)(2,1)}, u32[]{:S(2)}, u32[]{:S(2)}) collective-permute-start(bf16[3,80,1280]{2,1,0:T(8,128)(2,1)} %collective-permute-done.22.refs_8_), channel_id=1, source_target_pairs={{0,4},{4,0},{8,12},{12,8},{16,20},{20,16},{24,28},{28,24},{1,5},{5... | collective-permute-start | bytes 1843208 | tf_op jit(solution)/shard_map/ppermute | solution.py:65
  251.2 60.7 %collective-permute-start.35 = (bf16[320,1792]{1,0:T(8,128)(2,1)}, bf16[320,1792]{1,0:T(8,128)(2,1)S(1)}, u32[]{:S(2)}, u32[]{:S(2)}) collective-permute-start(bf16[320,1792]{1,0:T(8,128)(2,1)} %bitcast.37.refs_0_), channel_id=1, source_target_pairs={{0,16},{4,20},{8,24},{12,28},{16,0},{20,4},{24,8},{28,12},{1,17},{... | collective-permute-start | bytes 3440648 | tf_op jit(solution)/shard_map/ppermute | solution.py:65
  275.7 36.1 %collective-permute-start.41 = (bf16[320,1664]{1,0:T(8,128)(2,1)S(1)}, bf16[320,1664]{1,0:T(8,128)(2,1)S(1)}, u32[]{:S(2)}, u32[]{:S(2)}) collective-permute-start(bf16[320,1664]{1,0:T(8,128)(2,1)S(1)} %bitcast.105), channel_id=1, source_target_pairs={{0,8},{4,12},{8,0},{12,4},{16,24},{20,28},{24,16},{28,20},{1,9},{5... | collective-permute-start | bytes 3194888 | tf_op jit(solution)/shard_map/ppermute | solution.py:65
  293.2 19.8 %collective-permute-start.42 = (bf16[320,1664]{1,0:T(8,128)(2,1)S(1)}, bf16[320,1664]{1,0:T(8,128)(2,1)}, u32[]{:S(2)}, u32[]{:S(2)}) collective-permute-start(bf16[320,1664]{1,0:T(8,128)(2,1)S(1)} %bitcast.106), channel_id=1, source_target_pairs={{0,16},{4,20},{8,24},{12,28},{16,0},{20,4},{24,8},{28,12},{1,17},{... | collective-permute-start | bytes 3194888 | tf_op jit(solution)/shard_map/ppermute | solution.py:65
  310.8 28.3 %collective-permute-start.34 = (bf16[320,1792]{1,0:T(8,128)(2,1)}, bf16[320,1792]{1,0:T(8,128)(2,1)S(1)}, u32[]{:S(2)}, u32[]{:S(2)}) collective-permute-start(bf16[320,1792]{1,0:T(8,128)(2,1)} %bitcast.37.refs_0_), channel_id=1, source_target_pairs={{0,8},{4,12},{8,0},{12,4},{16,24},{20,28},{24,16},{28,20},{1,9},{5... | collective-permute-start | bytes 3440648 | tf_op jit(solution)/shard_map/ppermute | solution.py:65
  311.8 27.3 %collective-permute-start.37 = (bf16[320,1792]{1,0:T(8,128)(2,1)}, bf16[320,1792]{1,0:T(8,128)(2,1)S(1)}, u32[]{:S(2)}, u32[]{:S(2)}) collective-permute-start(bf16[320,1792]{1,0:T(8,128)(2,1)} %bitcast.37.refs_0_), channel_id=1, source_target_pairs={{0,4},{4,0},{8,12},{12,8},{16,20},{20,16},{24,28},{28,24},{1,5},{5... | collective-permute-start | bytes 3440648 | tf_op jit(solution)/shard_map/ppermute | solution.py:65
  311.9 51.3 %collective-permute-start.36 = (bf16[320,1792]{1,0:T(8,128)(2,1)S(1)}, bf16[320,1792]{1,0:T(8,128)(2,1)S(1)}, u32[]{:S(2)}, u32[]{:S(2)}) collective-permute-start(bf16[320,1792]{1,0:T(8,128)(2,1)S(1)} %collective-permute-done.35.refs_2_), channel_id=1, source_target_pairs={{0,8},{4,12},{8,0},{12,4},{16,24},{20,28},{24,16},{28,20},{1,9},{5... | collective-permute-start | bytes 3440648 | tf_op jit(solution)/shard_map/ppermute | solution.py:65
  313.0 50.2 %collective-permute-start.43 = (bf16[320,1664]{1,0:T(8,128)(2,1)S(1)}, bf16[320,1664]{1,0:T(8,128)(2,1)}, u32[]{:S(2)}, u32[]{:S(2)}) collective-permute-start(bf16[320,1664]{1,0:T(8,128)(2,1)S(1)} %collective-permute-done.41.refs_9_), channel_id=1, source_target_pairs={{0,16},{4,20},{8,24},{12,28},{16,0},{20,4},{24,8},{28,12},{1,17},{... | collective-permute-start | bytes 3194888 | tf_op jit(solution)/shard_map/ppermute | solution.py:65
  313.1 50.6 %collective-permute-start.45 = (bf16[320,1664]{1,0:T(8,128)(2,1)S(1)}, bf16[320,1664]{1,0:T(8,128)(2,1)S(1)}, u32[]{:S(2)}, u32[]{:S(2)}) collective-permute-start(bf16[320,1664]{1,0:T(8,128)(2,1)S(1)} %collective-permute-done.41.refs_9_), channel_id=1, source_target_pairs={{0,4},{4,0},{8,12},{12,8},{16,20},{20,16},{24,28},{28,24},{1,5},{5... | collective-permute-start | bytes 3194888 | tf_op jit(solution)/shard_map/ppermute | solution.py:65
  339.1 45.3 %collective-permute-start.39 = (bf16[320,1792]{1,0:T(8,128)(2,1)S(1)}, bf16[320,1792]{1,0:T(8,128)(2,1)S(1)}, u32[]{:S(2)}, u32[]{:S(2)}) collective-permute-start(bf16[320,1792]{1,0:T(8,128)(2,1)S(1)} %collective-permute-done.35.refs_2_), channel_id=1, source_target_pairs={{0,4},{4,0},{8,12},{12,8},{16,20},{20,16},{24,28},{28,24},{1,5},{5... | collective-permute-start | bytes 3440648 | tf_op jit(solution)/shard_map/ppermute | solution.py:65
  339.2 45.3 %collective-permute-start.38 = (bf16[320,1792]{1,0:T(8,128)(2,1)S(1)}, bf16[320,1792]{1,0:T(8,128)(2,1)}, u32[]{:S(2)}, u32[]{:S(2)}) collective-permute-start(bf16[320,1792]{1,0:T(8,128)(2,1)S(1)} %collective-permute-done.34.refs_1_), channel_id=1, source_target_pairs={{0,4},{4,0},{8,12},{12,8},{16,20},{20,16},{24,28},{28,24},{1,5},{5... | collective-permute-start | bytes 3440648 | tf_op jit(solution)/shard_map/ppermute | solution.py:65
  363.2 21.3 %collective-permute-start.40 = (bf16[320,1792]{1,0:T(8,128)(2,1)S(1)}, bf16[320,1792]{1,0:T(8,128)(2,1)}, u32[]{:S(2)}, u32[]{:S(2)}) collective-permute-start(bf16[320,1792]{1,0:T(8,128)(2,1)S(1)} %collective-permute-done.36.refs_3_), channel_id=1, source_target_pairs={{0,4},{4,0},{8,12},{12,8},{16,20},{20,16},{24,28},{28,24},{1,5},{5... | collective-permute-start | bytes 3440648 | tf_op jit(solution)/shard_map/ppermute | solution.py:65
  363.2 21.2 %collective-permute-start.46 = (bf16[320,1664]{1,0:T(8,128)(2,1)}, bf16[320,1664]{1,0:T(8,128)(2,1)}, u32[]{:S(2)}, u32[]{:S(2)}) collective-permute-start(bf16[320,1664]{1,0:T(8,128)(2,1)} %collective-permute-done.42.refs_10_), channel_id=1, source_target_pairs={{0,4},{4,0},{8,12},{12,8},{16,20},{20,16},{24,28},{28,24},{1,5},{5... | collective-permute-start | bytes 3194888 | tf_op jit(solution)/shard_map/ppermute | solution.py:65
  364.7 19.8 %collective-permute-start.47 = (bf16[320,1664]{1,0:T(8,128)(2,1)}, bf16[320,1664]{1,0:T(8,128)(2,1)}, u32[]{:S(2)}, u32[]{:S(2)}) collective-permute-start(bf16[320,1664]{1,0:T(8,128)(2,1)} %collective-permute-done.43.refs_11_), channel_id=1, source_target_pairs={{0,4},{4,0},{8,12},{12,8},{16,20},{20,16},{24,28},{28,24},{1,5},{5... | collective-permute-start | bytes 3194888 | tf_op jit(solution)/shard_map/ppermute | solution.py:65
  410.1 28.8 %collective-permute-start.48 = (bf16[512,640]{1,0:T(8,128)(2,1)}, bf16[512,640]{1,0:T(8,128)(2,1)S(1)}, u32[]{:S(2)}, u32[]{:S(2)}) collective-permute-start(bf16[512,640]{1,0:T(8,128)(2,1)} %get-tuple-element.14), channel_id=1, source_target_pairs={{0,1},{1,0},{2,3},{3,2},{4,5},{5,4},{6,7},{7,6},{8,9},{9,8},{10,11... | collective-permute-start | bytes 1966088 | tf_op jit(solution)/shard_map/ppermute | solution.py:65
  410.2 46.5 %collective-permute-start.49 = (bf16[512,640]{1,0:T(8,128)(2,1)}, bf16[512,640]{1,0:T(8,128)(2,1)S(1)}, u32[]{:S(2)}, u32[]{:S(2)}) collective-permute-start(bf16[512,640]{1,0:T(8,128)(2,1)} %get-tuple-element.15), channel_id=1, source_target_pairs={{0,2},{1,3},{2,0},{3,1},{4,6},{5,7},{6,4},{7,5},{8,10},{9,11},{10,... | collective-permute-start | bytes 1966088 | tf_op jit(solution)/shard_map/ppermute | solution.py:65
  413.1 57.7 %collective-permute-start.50 = (bf16[512,640]{1,0:T(8,128)(2,1)}, bf16[512,640]{1,0:T(8,128)(2,1)S(1)}, u32[]{:S(2)}, u32[]{:S(2)}) collective-permute-start(bf16[512,640]{1,0:T(8,128)(2,1)} %get-tuple-element.16), channel_id=1, source_target_pairs={{0,3},{1,2},{2,1},{3,0},{4,7},{5,6},{6,5},{7,4},{8,11},{9,10},{10,... | collective-permute-start | bytes 1966088 | tf_op jit(solution)/shard_map/ppermute | solution.py:65
  (47 other events, 1104.1 us)

commit v3 on v2

v3 whole, which is shorter than its diff:
```python
import functools
import math

import jax
import jax.numpy as jnp
from jax import lax
from jax.experimental import pallas as pl
from jax.experimental.pallas import tpu as pltpu
from jax.sharding import PartitionSpec as P

HEADS = 32
KV_HEADS = 8
HD = 80
WINDOW = 4096
SINKS = 4
BLOCK = 128
CAP = 2


FLOOR_SCORE = -1e30
EPSILON = 1e-05
ROPE_BASE = 10000.0
FAR = 1 << 30
LANES = 128
TILE = 256
ROW_TILE = 128
VMEM_LIMIT = 56 * 1024 * 1024

ANY = pl.BlockSpec(memory_space=pl.ANY)
VMEM = pl.BlockSpec(memory_space=pltpu.VMEM)
SMEM = pl.BlockSpec(memory_space=pltpu.SMEM)


def rms_scale(row_data, gain_vec):
    values = row_data.astype(jnp.float32)
    mean_square = jnp.mean(values * values, axis=-1, keepdims=True)
    return (values * lax.rsqrt(mean_square + EPSILON) * gain_vec).astype(jnp.bfloat16)


def rope_tables(positions):
    half_width = HD // 2
    frequency = ROPE_BASE ** (-2.0 * jnp.arange(half_width, dtype=jnp.float32) / HD)
    angles = positions.astype(jnp.float32)[:, None] * frequency[None, :]
    cosine = jnp.cos(angles)
    sine = jnp.sin(angles)
    return (
        jnp.concatenate([cosine, cosine], axis=1),
        jnp.concatenate([-sine, sine], axis=1),
    )


def slot_ranks(slot_prompt, prompts, slots):
    onehot = (slot_prompt[:, None] == jnp.arange(prompts, dtype=jnp.int32)[None, :]).astype(
        jnp.int32
    )
    running = jnp.cumsum(onehot, axis=0)
    global_rank = jnp.sum(onehot * (running - 1), axis=1)
    local_count = jnp.cumsum(onehot.reshape(-1, slots, prompts), axis=1).reshape(-1, prompts)
    local_rank = jnp.sum(onehot * (local_count - 1), axis=1)
    return (global_rank, local_rank)


def swap(values, axis, bit):
    pairs = [(index, index ^ bit) for index in range(lax.axis_size(axis))]
    return lax.ppermute(values, axis, pairs)


def half_up(width):
    return (width // 2 + LANES - 1) // LANES * LANES


def pack_kernel(layouts, groups, place_ref, *refs):
    kv_index = place_ref[2]
    outs = refs[len(refs) - groups * len(layouts) :]
    for choice in range(groups):

        @pl.when(kv_index == choice)
        def _():
            for which, spans in enumerate(layouts):
                for other in range(groups):
                    out = outs[which * groups + other]
                    column = 0
                    for matrix, first, last in spans:
                        start = (choice ^ other) * (refs[matrix].shape[1] // groups)
                        width = last - first
                        out[:, column : column + width] = refs[matrix][
                            :, start + first : start + last
                        ].astype(jnp.bfloat16)
                        column += width


def pack(place, matrices, groups, layouts, name):
    rows = matrices[0].shape[0]
    shapes = []
    for spans in layouts:
        width = sum(last - first for _, first, last in spans)
        shapes += [jax.ShapeDtypeStruct((rows, width), jnp.bfloat16)] * groups
    flat = pl.pallas_call(
        functools.partial(pack_kernel, layouts, groups),
        out_shape=tuple(shapes),
        in_specs=[SMEM] + [VMEM] * len(matrices),
        out_specs=(VMEM,) * len(shapes),
        compiler_params=pltpu.CompilerParams(vmem_limit_bytes=VMEM_LIMIT),
        cost_estimate=pl.CostEstimate(
            flops=0,
            bytes_accessed=6 * rows * sum(matrix.shape[1] for matrix in matrices),
            transcendentals=0,
        ),
        name=name,
    )(place, *matrices)
    return [flat[first : first + groups] for first in range(0, len(flat), groups)]


def exchange(parts):
    moved = [parts[0]] + [swap(part, "kv", other) for other, part in enumerate(parts) if other]
    return jnp.concatenate(moved, axis=0)


def exchange_in_order(parts, kv_index):
    moved = jnp.stack(
        [parts[0]] + [swap(part, "kv", other) for other, part in enumerate(parts) if other], axis=0
    )
    order = jnp.arange(len(parts), dtype=jnp.int32) ^ kv_index
    return jnp.take(moved, order, axis=0).reshape(-1, moved.shape[2])


def after(values, *earlier):
    return lax.optimization_barrier((values, *earlier))[0]


def plane_gather(piece):
    rows = piece.shape[0]
    by_x = swap(piece, "blk", 2)
    by_y = swap(piece, "blk", 4)
    upper = swap(by_y[: rows // 2], "blk", 2)
    lower = swap(by_x[rows // 2 :], "blk", 4)
    mine = [(0, 0, piece), (2, 0, by_x), (4, 0, by_y), (6, 0, upper), (6, rows // 2, lower)]
    return mine + [(index ^ 1, first, swap(part, "blk", 1)) for index, first, part in mine]


def on_columns(body, index, width, count):
    if width % LANES == 0:
        body(pl.ds(pl.multiple_of(index * width, LANES), width))
        return
    for choice in range(count):
        pl.when(index == choice)(functools.partial(body, pl.ds(choice * width, width)))


def row_copies(sources, refs, buffer, sem, blk_index, kv_index, groups):
    copies = []
    total = buffer.shape[0]
    for (index, begin, _), ref in zip(sources, refs):
        rows = ref.shape[0]
        piece = total // 8
        block = piece // groups
        if rows == total and index is None:
            copies.append(pltpu.make_async_copy(ref, buffer, sem))
            continue
        for first in range(0, rows, block):
            if rows == total:
                base = first // piece * piece
            else:
                base = (blk_index ^ index) * piece
            other = (begin + first) % piece // block
            target = pl.multiple_of(base + (kv_index ^ other) * block, 16)
            copies.append(
                pltpu.make_async_copy(
                    ref.at[pl.ds(first, block)], buffer.at[pl.ds(target, block)], sem
                )
            )
    return copies


def attention_kernel(
    sources,
    groups,
    kv_local,
    per_group,
    place_ref,
    normed_ref,
    cos_ref,
    sin_ref,
    blocks_ref,
    cached_ref,
    own_ref,
    *refs,
):
    count = len(sources)
    pieces = refs[:count]
    (
        out_ref,
        weights,
        projected,
        queries,
        keys,
        values,
        scores,
        probs,
        folded,
        shifts,
        summed,
        sem,
    ) = refs[count:]
    blk_index = place_ref[0]
    prefix_here = place_ref[1]
    copies = row_copies(sources, pieces, weights, sem.at[0], blk_index, place_ref[2], groups)
    for copy in copies:
        copy.start()
    new_rows = normed_ref.shape[0]
    cached = blocks_ref.shape[1] * BLOCK
    span = cached + new_rows
    chunk_rows = per_group * ROW_TILE
    extra = keys.shape[1] - HD
    first_row = lax.broadcasted_iota(jnp.int32, (extra, 1), 0) == 0
    for head in range(kv_local):
        for block in range(blocks_ref.shape[1]):
            place = pl.ds(block * BLOCK, BLOCK)
            keys[head, :HD, place] = blocks_ref[0, block, head]
            values[head, place, :] = blocks_ref[1, block, head].astype(jnp.float32).T.astype(
                jnp.bfloat16
            )
        for first, flags in ((0, cached_ref), (cached, own_ref)):
            bias = jnp.where((flags[...] > -FAR) | jnp.logical_not(first_row), 0.0, FLOOR_SCORE)
            keys[head, HD:, pl.ds(first, flags.shape[1])] = bias.astype(jnp.bfloat16)
    marker = jnp.where(
        lax.broadcasted_iota(jnp.int32, (chunk_rows, extra), 1) == 0, 1.0, 0.0
    ).astype(jnp.bfloat16)
    for chunk in range(new_rows // ROW_TILE):
        for head in range(kv_local):
            queries[chunk, head, :, HD:] = marker
    for copy in copies:
        copy.wait()

    def project(step, carry):
        rows = pl.ds(pl.multiple_of(step * TILE, TILE), TILE)
        projected[rows, :] = jnp.dot(
            normed_ref[rows, :], weights[...], preferred_element_type=jnp.float32
        )
        return carry

    lax.fori_loop(0, new_rows // TILE, project, 0)

    def rotated(rows, column):
        part = projected[rows, column : column + HD]
        turned = jnp.concatenate([part[:, HD // 2 :], part[:, : HD // 2]], axis=1)
        return part * cos_ref[rows, :] + turned * sin_ref[rows, :]

    query_width = kv_local * per_group * HD
    for chunk in range(new_rows // ROW_TILE):
        rows = pl.ds(chunk * ROW_TILE, ROW_TILE)
        for head in range(kv_local):
            for sub in range(per_group):
                queries[chunk, head, sub * ROW_TILE : (sub + 1) * ROW_TILE, :HD] = rotated(
                    rows, (head * per_group + sub) * HD
                ).astype(jnp.bfloat16)
            fresh = rotated(rows, query_width + head * HD)
            place = pl.ds(cached + chunk * ROW_TILE, ROW_TILE)
            keys[head, :HD, place] = fresh.T.astype(jnp.bfloat16)
            column = query_width + (kv_local + head) * HD
            values[head, place, :] = projected[rows, column : column + HD].astype(jnp.bfloat16)

    factor = 1.0 / math.sqrt(HD)
    group = 64

    def tiles_of(step, head, first, width, own):
        scores[:, pl.ds(first, width)] = jnp.dot(
            queries[step, head], keys[head, :, pl.ds(first, width)],
            preferred_element_type=jnp.float32,
        )
        for part in range(chunk_rows // group):
            rows = pl.ds(part * group, group)
            if own:
                row_id = step * ROW_TILE + (part * group) % ROW_TILE + (
                    lax.broadcasted_iota(jnp.int32, (group, LANES), 0)
                )
            top = folded[rows, :]
            for lane in range(0, width, LANES):
                place = pl.ds(first + lane, LANES)
                piece = scores[rows, place]
                if own:
                    own_id = lane + lax.broadcasted_iota(jnp.int32, (group, LANES), 1)
                    piece = jnp.where(own_id <= row_id, piece, FLOOR_SCORE)
                    scores[rows, place] = piece
                top = jnp.maximum(top, piece)
            folded[rows, :] = top

    def weigh(head, first, width):
        for part in range(chunk_rows // group):
            rows = pl.ds(part * group, group)
            shift = shifts[rows, :]
            total = folded[rows, :]
            for lane in range(0, width, LANES):
                piece = jnp.exp(scores[rows, pl.ds(first + lane, LANES)] * factor - shift)
                total = total + piece
                probs[rows, lane : lane + LANES] = piece.astype(jnp.bfloat16)
            folded[rows, :] = total
        summed[...] += jnp.dot(
            probs[:, :width], values[head, pl.ds(first, width), :],
            preferred_element_type=jnp.float32,
        )

    step_keys = min(4 * LANES, cached)

    def attend(step, carry):
        for head in range(kv_local):
            folded[...] = jnp.full_like(folded, FLOOR_SCORE)

            def score_cached(part, inner):
                first = pl.multiple_of(part * step_keys, step_keys)
                tiles_of(step, head, first, step_keys, False)
                return inner

            lax.fori_loop(0, cached // step_keys, score_cached, 0)
            tiles_of(step, head, cached, new_rows, True)

            @pl.when(prefix_here + new_rows > WINDOW)
            def _():
                folded[...] = jnp.full_like(folded, FLOOR_SCORE)

                def narrow(part, inner):
                    rows = pl.ds(pl.multiple_of(part * 16, 16), 16)
                    row_id = step * ROW_TILE + lax.rem(part * 16, ROW_TILE) + (
                        lax.broadcasted_iota(jnp.int32, (16, 1), 0)
                    )
                    oldest = prefix_here + row_id - WINDOW
                    old = jnp.where(cached_ref[...] > oldest, scores[rows, :cached], FLOOR_SCORE)
                    new = jnp.where(own_ref[...] > oldest, scores[rows, cached:], FLOOR_SCORE)
                    scores[rows, :cached] = old
                    scores[rows, cached:] = new
                    top = jnp.maximum(
                        jnp.max(old, axis=1, keepdims=True), jnp.max(new, axis=1, keepdims=True)
                    )
                    folded[rows, :] = jnp.broadcast_to(top, (16, LANES))
                    return inner

                lax.fori_loop(0, chunk_rows // 16, narrow, 0)

            for part in range(chunk_rows // group):
                rows = pl.ds(part * group, group)
                top = jnp.max(folded[rows, :], axis=1, keepdims=True) * factor
                shifts[rows, :] = jnp.broadcast_to(top, (group, LANES))
            folded[...] = jnp.zeros_like(folded)
            summed[...] = jnp.zeros_like(summed)

            def weigh_cached(part, inner):
                first = pl.multiple_of(part * step_keys, step_keys)
                weigh(head, first, step_keys)
                return inner

            lax.fori_loop(0, cached // step_keys, weigh_cached, 0)
            weigh(head, cached, new_rows)
            rows = pl.ds(pl.multiple_of(step * ROW_TILE, ROW_TILE), ROW_TILE)
            for sub in range(per_group):
                part = pl.ds(sub * ROW_TILE, ROW_TILE)
                total = jnp.sum(folded[part, :], axis=1, keepdims=True)
                column = (head * per_group + sub) * HD
                out_ref[rows, column : column + HD] = (summed[part, :] / total).astype(
                    jnp.bfloat16
                )
        return carry

    lax.fori_loop(0, new_rows // ROW_TILE, attend, 0)


def attend_rows(place, normed, tables, blocks, cached_pos, own_pos, sources, groups, per_group):
    new_rows = normed.shape[0]
    kv_local = blocks.shape[2]
    arrays = [values for _, _, values in sources]
    width = arrays[0].shape[1]
    cached = blocks.shape[1] * BLOCK
    span = cached + new_rows
    heads = kv_local * per_group
    chunk_rows = per_group * ROW_TILE
    widest = max(new_rows, min(4 * LANES, cached))
    return pl.pallas_call(
        functools.partial(attention_kernel, sources, groups, kv_local, per_group),
        out_shape=jax.ShapeDtypeStruct((new_rows, heads * HD), jnp.bfloat16),
        in_specs=[SMEM] + [VMEM] * 6 + [ANY] * len(arrays),
        out_specs=VMEM,
        scratch_shapes=[
            pltpu.VMEM((normed.shape[1], width), jnp.bfloat16),
            pltpu.VMEM((new_rows, width), jnp.float32),
            pltpu.VMEM((new_rows // ROW_TILE, kv_local, chunk_rows, HD + 16), jnp.bfloat16),
            pltpu.VMEM((kv_local, HD + 16, span), jnp.bfloat16),
            pltpu.VMEM((kv_local, span, HD), jnp.bfloat16),
            pltpu.VMEM((chunk_rows, span), jnp.float32),
            pltpu.VMEM((chunk_rows, widest), jnp.bfloat16),
            pltpu.VMEM((chunk_rows, LANES), jnp.float32),
            pltpu.VMEM((chunk_rows, LANES), jnp.float32),
            pltpu.VMEM((chunk_rows, HD), jnp.float32),
            pltpu.SemaphoreType.DMA((1,)),
        ],
        compiler_params=pltpu.CompilerParams(vmem_limit_bytes=VMEM_LIMIT),
        cost_estimate=pl.CostEstimate(
            flops=2 * new_rows * normed.shape[1] * width + 8 * heads * new_rows * span * LANES,
            bytes_accessed=2 * normed.shape[1] * width,
            transcendentals=heads * new_rows * span,
        ),
        name="attention",
    )(place, normed, *tables, blocks, cached_pos, own_pos, *arrays)


def middle_kernel(sources, groups, place_ref, tokens_ref, gain_ref, *refs):
    att = refs[:groups]
    own_ref = refs[groups]
    rest = refs[groups + 1 :]
    shares = rest[: len(sources)]
    normed_ref, residual_ref, gathered, weights, middle, sem = rest[len(sources) :]
    blk_index = place_ref[0]
    kv_index = place_ref[2]
    group_rows = own_ref.shape[0]
    copies = []
    if shares[0].ndim == 3:
        copies.append(pltpu.make_async_copy(own_ref, weights.at[pl.ds(0, group_rows)], sem.at[0]))
        for (index, _, _), ref in zip(sources, shares):
            part = ref.shape[1]
            first = pl.multiple_of((blk_index ^ index) * part, 16)
            for other in range(1, groups):
                copies.append(
                    pltpu.make_async_copy(
                        ref.at[other - 1],
                        weights.at[pl.ds(other * group_rows + first, part)],
                        sem.at[0],
                    )
                )
    else:
        for other in range(groups):
            first = pl.multiple_of((kv_index ^ other) * group_rows, 16)
            copies.append(
                pltpu.make_async_copy(
                    shares[0].at[pl.ds(first, group_rows)],
                    weights.at[pl.ds(other * group_rows, group_rows)],
                    sem.at[0],
                )
            )
    for copy in copies:
        copy.start()
    feature = att[0].shape[1]
    for other in range(groups):
        gathered[:, other * feature : (other + 1) * feature] = att[other][...]
    for copy in copies:
        copy.wait()
    new_rows, model = tokens_ref.shape
    tile = 2 * TILE

    def product(step, carry):
        columns = pl.ds(pl.multiple_of(step * tile, tile), tile)
        summed = jnp.dot(gathered[...], weights[:, columns], preferred_element_type=jnp.float32)
        middle[:, columns] = (tokens_ref[:, columns].astype(jnp.float32) + summed).astype(
            jnp.bfloat16
        )
        return carry

    lax.fori_loop(0, model // tile, product, 0)

    def scale(step, carry):
        rows = pl.ds(pl.multiple_of(step * 16, 16), 16)
        part = middle[rows, :].astype(jnp.float32)
        mean_square = jnp.mean(part * part, axis=1, keepdims=True)
        normed_ref[rows, :] = (part * lax.rsqrt(mean_square + EPSILON) * gain_ref[...]).astype(
            jnp.bfloat16
        )
        return carry

    lax.fori_loop(0, new_rows // 16, scale, 0, unroll=2)
    out_width = model // groups

    def keep(columns):
        residual_ref[...] = middle[:, columns]

    on_columns(keep, kv_index, out_width, groups)


def middle_rows(place, tokens, gain, attended, own, sources):
    new_rows, model = tokens.shape
    groups = len(attended)
    arrays = [values for _, _, values in sources]
    return pl.pallas_call(
        functools.partial(middle_kernel, sources, groups),
        out_shape=(
            jax.ShapeDtypeStruct((new_rows, model), jnp.bfloat16),
            jax.ShapeDtypeStruct((new_rows, model // groups), jnp.bfloat16),
        ),
        in_specs=[SMEM, VMEM, VMEM] + [VMEM] * groups + [ANY] * (1 + len(arrays)),
        out_specs=(VMEM, VMEM),
        scratch_shapes=[
            pltpu.VMEM((new_rows, model), jnp.bfloat16),
            pltpu.VMEM((model, model), jnp.bfloat16),
            pltpu.VMEM((new_rows, model), jnp.bfloat16),
            pltpu.SemaphoreType.DMA((1,)),
        ],
        compiler_params=pltpu.CompilerParams(vmem_limit_bytes=VMEM_LIMIT),
        cost_estimate=pl.CostEstimate(
            flops=2 * new_rows * model * model,
            bytes_accessed=2 * model * model,
            transcendentals=0,
        ),
        name="middle",
    )(place, tokens, gain, *attended, own, *arrays)


def hidden_chunks(width):
    whole = width // LANES * LANES
    chunks = []
    first = 0
    while first < whole:
        units = min(TILE, whole - first)
        chunks.append((first, first, whole + first, units))
        first += units
    if width > whole:
        chunks.append((whole, 2 * whole, 2 * whole + width - whole, width - whole))
    return chunks


def mlp_kernel(sources, groups, widths, place_ref, normed_ref, down_ref, left, right, *refs):
    outs = refs[:groups]
    first_half, second_half, down, hidden, sems = refs[groups:]
    kv_index = place_ref[2]
    blk_index = place_ref[0]
    loads = (
        row_copies(sources[:1], [left], first_half, sems.at[0], blk_index, kv_index, groups),
        row_copies(sources[1:], [right], second_half, sems.at[1], blk_index, kv_index, groups),
        [pltpu.make_async_copy(down_ref, down, sems.at[2])],
    )
    for copies in loads:
        for copy in copies:
            copy.start()
    base = 0
    for half, (width, buffer) in enumerate(zip(widths, (first_half, second_half))):
        for copy in loads[half]:
            copy.wait()
        for first, gate, up, units in hidden_chunks(width):
            if units < LANES:
                both = jnp.dot(
                    normed_ref[...],
                    buffer[:, gate : gate + 2 * units],
                    preferred_element_type=jnp.float32,
                )
                gated, raised = both[:, :units], both[:, units:]
            else:
                gated = jnp.dot(
                    normed_ref[...],
                    buffer[:, gate : gate + units],
                    preferred_element_type=jnp.float32,
                )
                raised = jnp.dot(
                    normed_ref[...], buffer[:, up : up + units], preferred_element_type=jnp.float32
                )
            hidden[:, base + first : base + first + units] = (
                gated / (1.0 + jnp.exp(-gated)) * raised
            ).astype(jnp.bfloat16)
        base += width
    for copy in loads[2]:
        copy.wait()
    out_width = outs[0].shape[1]
    for other in range(groups):

        def product(columns, out=outs[other]):
            out[...] = jnp.dot(
                hidden[...], down[:, columns], preferred_element_type=jnp.float32
            ).astype(out.dtype)

        on_columns(product, kv_index ^ other, out_width, groups)


def mlp_parts(place, normed, w_down, sources, groups, widths):
    (_, _, left), (_, _, right) = sources
    new_rows, model = normed.shape
    out_width = model // groups
    return pl.pallas_call(
        functools.partial(mlp_kernel, sources, groups, widths),
        out_shape=tuple(
            jax.ShapeDtypeStruct((new_rows, out_width), jnp.bfloat16 if other else jnp.float32)
            for other in range(groups)
        ),
        in_specs=[SMEM, VMEM, ANY, ANY, ANY],
        out_specs=(VMEM,) * groups,
        scratch_shapes=[
            pltpu.VMEM(left.shape, jnp.bfloat16),
            pltpu.VMEM(right.shape, jnp.bfloat16),
            pltpu.VMEM(w_down.shape, jnp.bfloat16),
            pltpu.VMEM((new_rows, w_down.shape[0]), jnp.bfloat16),
            pltpu.SemaphoreType.DMA((3,)),
        ],
        compiler_params=pltpu.CompilerParams(vmem_limit_bytes=VMEM_LIMIT),
        cost_estimate=pl.CostEstimate(
            flops=6 * new_rows * model * w_down.shape[0],
            bytes_accessed=6 * model * w_down.shape[0],
            transcendentals=new_rows * w_down.shape[0],
        ),
        name="mlp",
    )(place, normed, w_down, left, right)


def shards(
    tokens,
    attn_gain,
    mlp_gain,
    w_query,
    w_key,
    w_value,
    w_gate,
    w_up,
    w_out,
    w_down,
    cache,
    slot_prompt,
    prefix_len,
    new_len,
):
    groups = lax.axis_size("kv")
    blk_index = lax.axis_index("blk")
    kv_index = lax.axis_index("kv")
    query_width = w_query.shape[1] // groups
    key_width = w_key.shape[1] // groups
    per_group = HEADS // KV_HEADS
    new_rows = tokens.shape[0]
    prompts = prefix_len.shape[0]
    slots = cache.shape[1]
    prefix_here = prefix_len[blk_index]
    live_count = new_len[blk_index]
    place = jnp.stack([blk_index, prefix_here, kv_index]).astype(jnp.int32)

    global_rank, local_rank = slot_ranks(slot_prompt, prompts, slots)
    own_prompts = lax.dynamic_slice_in_dim(slot_prompt, blk_index * slots, slots)
    own_ranks = lax.dynamic_slice_in_dim(local_rank, blk_index * slots, slots)
    placed = own_prompts * CAP + own_ranks
    buffer_ids = jnp.arange(prompts * CAP, dtype=jnp.int32)
    matches = placed[None, :] == buffer_ids[:, None]
    source_slot = jnp.sum(
        jnp.where(matches, jnp.arange(slots, dtype=jnp.int32)[None, :], 0), axis=1
    )
    outgoing = jnp.take(cache, source_slot, axis=1)
    arrived = lax.all_to_all(outgoing, "blk", split_axis=1, concat_axis=1, tiled=True)
    slot_ids = jnp.arange(prompts * slots, dtype=jnp.int32)
    landing = slot_ids // slots * CAP + local_rank
    for_me = slot_prompt == blk_index
    received = (landing[None, :] == buffer_ids[:, None]) & for_me[None, :]
    block_number = jnp.sum(jnp.where(received, global_rank[None, :], 0), axis=1)
    block_live = jnp.any(received, axis=1)
    key_pos = block_number[:, None] * BLOCK + jnp.arange(BLOCK, dtype=jnp.int32)[None, :]
    key_live = block_live[:, None] & (key_pos < prefix_here)
    cached_pos = jnp.where(key_live, jnp.where(key_pos < SINKS, FAR, key_pos), -FAR)
    cached_pos = cached_pos.reshape(1, -1)
    row_ids = jnp.arange(new_rows, dtype=jnp.int32)
    positions = prefix_here + row_ids
    own_pos = jnp.where(
        row_ids < live_count, jnp.where(positions < SINKS, FAR, positions), -FAR
    ).reshape(1, -1)

    in_place = lax.axis_size("blk") == 8 and w_query.shape[0] % 16 == 0
    spans = [(0, 0, query_width), (1, 0, key_width), (2, 0, key_width)]
    (qkv_parts,) = pack(place, (w_query, w_key, w_value), groups, [spans], "pack_qkv")
    if in_place:
        moved_qkv = exchange(qkv_parts)
        qkv = plane_gather(after(moved_qkv, arrived))
        near, across = [qkv[at][2] for at in (1, 2)], [qkv[at][2] for at in (3, 4)]
    else:
        moved_qkv = exchange_in_order(qkv_parts, kv_index)
        qkv = [(None, 0, lax.all_gather(moved_qkv, "blk", axis=0, tiled=True))]
        near, across = [moved_qkv], [moved_qkv]

    normed = rms_scale(tokens, attn_gain)
    tables = rope_tables(positions)

    hidden_width = w_gate.shape[1] // groups
    cut = half_up(hidden_width)
    widths = (cut, hidden_width - cut)
    layouts = []
    for first, last in ((0, cut), (cut, hidden_width)):
        whole = first + (last - first) // LANES * LANES
        layouts.append([(0, first, whole), (1, first, whole)])
        if whole < last:
            layouts[-1] += [(0, whole, last), (1, whole, last)]
    pair = []
    moved = moved_qkv
    packed = pack(place, (w_gate, w_up), groups, layouts, "pack_pair")
    for parts, earlier in zip(packed, (near, across)):
        parts = after(parts, moved)
        if in_place:
            moved = exchange(parts)
            index = 0
        else:
            moved = exchange_in_order(parts, kv_index)
            index = None
        ready = after(moved, *earlier)
        pair.append((index, 0, lax.all_gather(ready, "blk", axis=0, tiled=True)))

    eighth = w_out.shape[0] // lax.axis_size("blk")
    spread = in_place and eighth % 16 == 0
    if spread:
        share = lax.dynamic_slice_in_dim(w_out, blk_index * eighth, eighth, 0)
        share = after(share, moved, *[values for _, _, values in qkv])
        shares = jnp.stack([swap(share, "kv", other) for other in range(1, groups)], axis=0)

    attended = attend_rows(
        place, normed, tables, arrived, cached_pos, own_pos, qkv, groups, per_group
    )
    if spread:
        shares = after(shares, attended)
        by_x = swap(shares, "blk", 2)
        by_y = swap(shares, "blk", 4)
        mine = [(0, 0, shares), (2, 0, by_x), (4, 0, by_y), (6, 0, swap(by_y, "blk", 2))]
        w_out_sources = mine + [
            (index ^ 1, first, swap(part, "blk", 1)) for index, first, part in mine
        ]
    else:
        w_out_sources = [(0, 0, lax.all_gather(w_out, "kv", axis=0, tiled=True))]

    everyone = [attended] + [swap(attended, "kv", other) for other in range(1, groups)]
    normed_mid, residual = middle_rows(
        place, tokens, mlp_gain.reshape(1, -1), everyone, w_out, w_out_sources
    )
    parts = mlp_parts(place, normed_mid, w_down, pair, groups, widths)
    reduced = parts[0]
    for other in range(1, groups):
        reduced = reduced + swap(parts[other], "kv", other).astype(jnp.float32)
    mixed = jnp.where(
        (row_ids < live_count)[:, None], residual.astype(jnp.float32) + reduced, 0.0
    )
    return mixed.astype(jnp.bfloat16)


def solution(mesh):
    return jax.shard_map(
        shards,
        mesh=mesh,
        in_specs=(
            P("blk", None),
            P(),
            P(),
            P(("blk", "kv"), None),
            P(("blk", "kv"), None),
            P(("blk", "kv"), None),
            P(("blk", "kv"), None),
            P(("blk", "kv"), None),
            P("kv", None),
            P("kv", None),
            P(None, "blk", "kv", None, None),
            P(),
            P(),
            P(),
        ),
        out_specs=P("blk", "kv"),
        check_vma=False,
    )
```

time: 474 us -> 386 us (0.81)
  the two profiles are of different devices: /device:TPU:12 before, /device:TPU:0 now
where the time goes in v3:
time: 386 us
  waiting for transfers between devices  180 us (47%)
  Pallas kernels  100 us (26%)
  starting transfers between devices  61.3 us (16%)
  other arithmetic  15.5 us (4%)
  local copies, waits for them, and re-layouts  14.8 us (4%)
  between operations  13.9 us (4%)
    ppermute x34, waiting for transfers between devices, swap(): return lax.ppermute(values, axis, pairs)  179 us
    ppermute x34, starting transfers between devices, swap(): return lax.ppermute(values, axis, pairs)  57.4 us
    pallas_call x1, Pallas kernels, attend_rows(): pl.pallas_call(functools.partial(attention_kernel, sources, groups, kv_lo...  50.3 us
    pallas_call x1, Pallas kernels, mlp_parts(): pl.pallas_call(functools.partial(mlp_kernel, sources, groups, widths), ou...  24.6 us
    pallas_call x1, Pallas kernels, middle_rows(): pl.pallas_call(functools.partial(middle_kernel, sources, groups), out_sha...  19 us
  transfers between devices with their start and end apart: 37, of which 11 were waited for; matrix products, arithmetic and copies ran while one was open for 6% of the time, Pallas kernels for 19%

profile of v3, /device:TPU:0, one launch (start us, length us, event | category | flops | bytes accessed | tf_op | source)
XLA Modules:
  0.0 385.9 jit_solution(2391931443883428385)
XLA Ops:
  6.5 1.4 dynamic_slice.16
  7.9 1.2 pad_add_fusion.place_ref
  9.1 2.3 pack_qkv.1
  11.4 3.0 collective-permute-start
  16.7 1.3 select_bitcast_fusion
  18.0 3.9 all-to-all-start
  21.9 2.7 collective-permute-start.1
  24.8 4.2 %pack_pair.1 = (bf16[80,1792]{1,0:T(8,128)(2,1)}, bf16[80,1792]{1,0:T(8,128)(2,1)}, bf16[80,1792]{1,0:T(8,128)(2,1)}, bf16[80,1792]{1,0:T(8,128)(2,1)}, bf16[80,...) custom-call(s32[3]{0:T(128)} %pad_add_fusion.place_ref, ...), custom_call_target="tpu_custom_call" | custom-call | bytes 6635520 | tf_op jit(solution)/shard_map/pack_pair/pallas_call | solution.py:98
  29.0 7.4 %collective-permute-done.1 = bf16[80,960]{1,0:T(8,128)(2,1)S(1)} collective-permute-done((bf16[80,960]{1,0:T(8,128)(2,1)S(1)}, bf16[80,960]{1,0:T(8,128)(2,1)S(1)}, u32[]{:S(2)}, u32[]{:S(2)}) %collective-permute-start.1) | collective-permute-done | bytes 153632 | tf_op jit(solution)/shard_map/ppermute | solution.py:65
  36.5 4.0 %collective-permute-start.15 = (bf16[80,1792]{1,0:T(8,128)(2,1)}, bf16[80,1792]{1,0:T(8,128)(2,1)S(1)}, u32[]{:S(2)}, u32[]{:S(2)}) collective-permute-start(bf16[80,1792]{1,0:T(8,128)(2,1)} %get-tuple-element.50), channel_id=1, source_target_pairs={{0,1},{1,0},{2,3},{3,2},{4,5},{5,4},{6,7},{7,6},{8,9},{9,8},{10,11... | collective-permute-start | bytes 860168 | tf_op jit(solution)/shard_map/ppermute | solution.py:65
  40.5 1.2 collective-permute-start.16
  42.7 1.5 collective-permute-start.17
  44.1 9.0 %collective-permute-done.15 = bf16[80,1792]{1,0:T(8,128)(2,1)S(1)} collective-permute-done((bf16[80,1792]{1,0:T(8,128)(2,1)}, bf16[80,1792]{1,0:T(8,128)(2,1)S(1)}, u32[]{:S(2)}, u32[]{:S(2)}) %collective-permute-start.15) | collective-permute-done | bytes 286752 | tf_op jit(solution)/shard_map/ppermute | solution.py:65
  53.2 10.5 %collective-permute-done.16 = bf16[80,1792]{1,0:T(8,128)(2,1)S(1)} collective-permute-done((bf16[80,1792]{1,0:T(8,128)(2,1)}, bf16[80,1792]{1,0:T(8,128)(2,1)S(1)}, u32[]{:S(2)}, u32[]{:S(2)}) %collective-permute-start.16) | collective-permute-done | bytes 286752 | tf_op jit(solution)/shard_map/ppermute | solution.py:65
  63.7 1.7 collective-permute-start.3
  65.4 1.5 collective-permute-start.4
  66.9 2.4 collective-permute-start.18
  70.9 1.5 collective-permute-start.20
  72.5 6.5 %collective-permute-done.18 = bf16[80,1664]{1,0:T(8,128)(2,1)S(1)} collective-permute-done((bf16[80,1664]{1,0:T(8,128)(2,1)S(1)}, bf16[80,1664]{1,0:T(8,128)(2,1)S(1)}, u32[]{:S(2)}, u32[]{:S(2)}) %collective-permute-start.18) | collective-permute-done | bytes 266272 | tf_op jit(solution)/shard_map/ppermute | solution.py:65
  80.7 1.7 collective-permute-start.5
  83.4 1.5 collective-permute-start.6
  85.0 6.2 %collective-permute-done.19 = bf16[80,1664]{1,0:T(8,128)(2,1)S(1)} collective-permute-done((bf16[80,1664]{1,0:T(8,128)(2,1)}, bf16[80,1664]{1,0:T(8,128)(2,1)S(1)}, u32[]{:S(2)}, u32[]{:S(2)}) %collective-permute-start.19) | collective-permute-done | bytes 266272 | tf_op jit(solution)/shard_map/ppermute | solution.py:65
  95.4 1.2 fusion.6.cached_ref
  96.7 2.1 fusion.2.normed_ref
  101.0 1.7 compare_select_fusion.2.own_ref
  102.7 1.0 pad_maximum_fusion.1
  104.2 1.0 constant_dynamic-slice_fusion
  105.3 1.2 copy.19.blocks_ref
  106.5 2.3 collective-permute-start.23
  108.9 2.5 collective-permute-start.22
  111.4 50.3 %attention.1.refs_0_ = bf16[512,640]{1,0:T(8,128)(2,1)} custom-call(s32[3]{0:T(128)} %pad_add_fusion.place_ref, bf16[512,2560]{1,0:T(8,128)(2,1)} %fusion.2.normed_ref, f32[512,80]{1,0:T(8,128)} %get-tuple-element.70.cos_ref, f32[512,80]{1,0:T(8,128)} %get-tuple-element.71.sin_ref, bf16[2,16,2,80,128]{4,3,2,1,0:T(8,128)(2,1)} %copy.19.blocks_ref, ...), custom_call_target="tpu_custom_call" | custom-call | flops 13254000640 | bytes 4915200 | tf_op jit(solution)/shard_map/attention/pallas_call | solution.py:375
  161.9 1.7 collective-permute-start.25
  163.6 1.5 collective-permute-start.24
  165.1 42.9 %collective-permute-done.25.refs_7_ = bf16[3,80,2560]{2,1,0:T(8,128)(2,1)S(1)} collective-permute-done((bf16[3,80,2560]{2,1,0:T(8,128)(2,1)S(1)}, bf16[3,80,2560]{2,1,0:T(8,128)(2,1)S(1)}, u32[]{:S(2)}, u32[]{:S(2)}) %collective-permute-start.25) | collective-permute-done | bytes 1228832 | tf_op jit(solution)/shard_map/ppermute | solution.py:65
  207.9 1.5 collective-permute-start.26
  209.4 1.5 collective-permute-start.12
  210.9 2.4 collective-permute-start.13
  213.3 25.6 %collective-permute-done.12.refs_1_ = bf16[512,640]{1,0:T(8,128)(2,1)} collective-permute-done((bf16[512,640]{1,0:T(8,128)(2,1)S(1)}, bf16[512,640]{1,0:T(8,128)(2,1)}, u32[]{:S(2)}, u32[]{:S(2)}) %collective-permute-start.12) | collective-permute-done | bytes 655392 | tf_op jit(solution)/shard_map/ppermute | solution.py:65
  239.4 11.4 %collective-permute-done.26.refs_8_ = bf16[3,80,2560]{2,1,0:T(8,128)(2,1)S(1)} collective-permute-done((bf16[3,80,2560]{2,1,0:T(8,128)(2,1)S(1)}, bf16[3,80,2560]{2,1,0:T(8,128)(2,1)S(1)}, u32[]{:S(2)}, u32[]{:S(2)}) %collective-permute-start.26) | collective-permute-done | bytes 1228832 | tf_op jit(solution)/shard_map/ppermute | solution.py:65
  250.9 3.4 collective-permute-start.14
  254.8 15.1 %collective-permute-done.14.refs_3_ = bf16[512,640]{1,0:T(8,128)(2,1)S(1)} collective-permute-done((bf16[512,640]{1,0:T(8,128)(2,1)S(1)}, bf16[512,640]{1,0:T(8,128)(2,1)S(1)}, u32[]{:S(2)}, u32[]{:S(2)}) %collective-permute-start.14) | collective-permute-done | bytes 655392 | tf_op jit(solution)/shard_map/ppermute | solution.py:65
  272.3 19.0 %middle.1 = (bf16[512,2560]{1,0:T(8,128)(2,1)}, bf16[512,640]{1,0:T(8,128)(2,1)}) custom-call(s32[3]{0:T(128)} %pad_add_fusion.place_ref, bf16[512,2560]{1,0:T(8,128)(2,1)} %tokens_ref.1, f32[1,2560]{1,0:T(1,128)} %reshape.161.gain_ref, bf16[512,640]{1,0:T(8,128)(2,1)} %attention.1.refs_0_, bf16[512,640]{1,0:T(8,128)(2,1)} %collective-permute-done.12.refs_1_, ...), custom_call_target="tpu_custom_call" | custom-call | flops 6710886400 | bytes 13107200 | tf_op jit(solution)/shard_map/middle/pallas_call | solution.py:478
  291.3 24.6 %mlp.1 = (f32[512,640]{1,0:T(8,128)}, bf16[512,640]{1,0:T(8,128)(2,1)}, bf16[512,640]{1,0:T(8,128)(2,1)}, bf16[512,640]{1,0:T(8,128)(2,1)}) custom-call(s32[3]{0:T(128)} %pad_add_fusion.place_ref, bf16[512,2560]{1,0:T(8,128)(2,1)} %get-tuple-element.60.normed_ref, bf16[1728,2560]{1,0:T(8,128)(2,1)} %down_ref.1, ...), custom_call_target="tpu_custom_call" | custom-call | flops 13589544960 | bytes 26542080 | tf_op jit(solution)/shard_map/mlp/pallas_call | solution.py:570
  315.9 3.4 collective-permute-start.33
  319.3 11.8 %collective-permute-start.32 = (bf16[512,640]{1,0:T(8,128)(2,1)}, bf16[512,640]{1,0:T(8,128)(2,1)S(1)}, u32[]{:S(2)}, u32[]{:S(2)}) collective-permute-start(bf16[512,640]{1,0:T(8,128)(2,1)} %get-tuple-element.65), channel_id=1, source_target_pairs={{0,2},{1,3},{2,0},{3,1},{4,6},{5,7},{6,4},{7,5},{8,10},{9,11},{10,... | collective-permute-start | bytes 1966088 | tf_op jit(solution)/shard_map/ppermute | solution.py:65
  331.7 3.3 collective-permute-done.33
  335.0 41.4 %collective-permute-done.32 = bf16[512,640]{1,0:T(8,128)(2,1)S(1)} collective-permute-done((bf16[512,640]{1,0:T(8,128)(2,1)}, bf16[512,640]{1,0:T(8,128)(2,1)S(1)}, u32[]{:S(2)}, u32[]{:S(2)}) %collective-permute-start.32) | collective-permute-done | bytes 655392 | tf_op jit(solution)/shard_map/ppermute | solution.py:65
  376.4 2.6 select_convert_fusion
  (149 shorter events, 19.0 us)
Async XLA Ops:
  11.4 17.5 %collective-permute-start = (bf16[80,960]{1,0:T(8,128)(2,1)}, bf16[80,960]{1,0:T(8,128)(2,1)S(1)}, u32[]{:S(2)}, u32[]{:S(2)}) collective-permute-start(bf16[80,960]{1,0:T(8,128)(2,1)} %get-tuple-element.37), channel_id=1, source_target_pairs={{0,1},{1,0},{2,3},{3,2},{4,5},{5,4},{6,7},{7,6},{8,9},{9,8},{10,11... | collective-permute-start | bytes 460808 | tf_op jit(solution)/shard_map/ppermute | solution.py:65
  18.0 45.7 %all-to-all-start = ((bf16[2,16,2,80,128]{4,3,2,0,1:T(8,128)(2,1)}), bf16[2,16,2,80,128]{4,3,2,0,1:T(8,128)(2,1)S(1)}, u32[]{:S(2)}, u32[]{:S(2)}) async-start(bf16[2,16,2,80,128]{4,3,2,0,1:T(8,128)(2,1)} %select_bitcast_fusion), calls=%async_computation | async-start | bytes 2621440 | tf_op jit(solution)/shard_map/all_to_all | solution.py:634
  21.8 269.5 %all-gather.5.cloned.1.call-start = ((), (), s32[]{:S(2)}) async-start(), calls=%async_computation.2 | async-start | bytes 9584640 | tf_op jit(solution)/shard_map/all_gather | solution.py:687
  21.9 14.5 %collective-permute-start.1 = (bf16[80,960]{1,0:T(8,128)(2,1)S(1)}, bf16[80,960]{1,0:T(8,128)(2,1)S(1)}, u32[]{:S(2)}, u32[]{:S(2)}) collective-permute-start(bf16[80,960]{1,0:T(8,128)(2,1)S(1)} %copy-done.29), channel_id=1, source_target_pairs={{0,2},{1,3},{2,0},{3,1},{4,6},{5,7},{6,4},{7,5},{8,10},{9,11},{10,... | collective-permute-start | bytes 460808 | tf_op jit(solution)/shard_map/ppermute | solution.py:65
  24.5 11.9 %collective-permute-start.2 = (bf16[80,960]{1,0:T(8,128)(2,1)S(1)}, bf16[80,960]{1,0:T(8,128)(2,1)S(1)}, u32[]{:S(2)}, u32[]{:S(2)}) collective-permute-start(bf16[80,960]{1,0:T(8,128)(2,1)S(1)} %copy-done.28), channel_id=1, source_target_pairs={{0,3},{1,2},{2,1},{3,0},{4,7},{5,6},{6,5},{7,4},{8,11},{9,10},{10,... | collective-permute-start | bytes 460808 | tf_op jit(solution)/shard_map/ppermute | solution.py:65
  36.4 30.5 %copy-start.27 = (bf16[80,1664]{1,0:T(8,128)(2,1)S(1)}, bf16[80,1664]{1,0:T(8,128)(2,1)}, u32[]{:S(2)}) copy-start(bf16[80,1664]{1,0:T(8,128)(2,1)} %get-tuple-element.54) | copy-start | bytes 798724
  36.4 33.8 %copy-start.8 = (bf16[80,1664]{1,0:T(8,128)(2,1)S(1)}, bf16[80,1664]{1,0:T(8,128)(2,1)}, u32[]{:S(2)}) copy-start(bf16[80,1664]{1,0:T(8,128)(2,1)} %get-tuple-element.53) | copy-start | bytes 798724
  36.4 27.2 %copy-start.10 = (bf16[320,960]{1,0:T(8,128)(2,1)}, bf16[320,960]{1,0:T(8,128)(2,1)S(1)}, u32[]{:S(2)}) copy-start(bf16[320,960]{1,0:T(8,128)(2,1)S(1)} %constant_dynamic-update-slice_fusion.refs_0_) | copy-start | bytes 1843204
  36.4 34.5 %copy-start.26 = (bf16[80,1664]{1,0:T(8,128)(2,1)S(1)}, bf16[80,1664]{1,0:T(8,128)(2,1)}, u32[]{:S(2)}) copy-start(bf16[80,1664]{1,0:T(8,128)(2,1)} %get-tuple-element.56) | copy-start | bytes 798724
  36.5 16.7 %collective-permute-start.15 = (bf16[80,1792]{1,0:T(8,128)(2,1)}, bf16[80,1792]{1,0:T(8,128)(2,1)S(1)}, u32[]{:S(2)}, u32[]{:S(2)}) collective-permute-start(bf16[80,1792]{1,0:T(8,128)(2,1)} %get-tuple-element.50), channel_id=1, source_target_pairs={{0,1},{1,0},{2,3},{3,2},{4,5},{5,4},{6,7},{7,6},{8,9},{9,8},{10,11... | collective-permute-start | bytes 860168 | tf_op jit(solution)/shard_map/ppermute | solution.py:65
  40.5 23.1 %collective-permute-start.16 = (bf16[80,1792]{1,0:T(8,128)(2,1)}, bf16[80,1792]{1,0:T(8,128)(2,1)S(1)}, u32[]{:S(2)}, u32[]{:S(2)}) collective-permute-start(bf16[80,1792]{1,0:T(8,128)(2,1)} %get-tuple-element.51), channel_id=1, source_target_pairs={{0,2},{1,3},{2,0},{3,1},{4,6},{5,7},{6,4},{7,5},{8,10},{9,11},{10,... | collective-permute-start | bytes 860168 | tf_op jit(solution)/shard_map/ppermute | solution.py:65
  42.7 24.2 %collective-permute-start.17 = (bf16[80,1792]{1,0:T(8,128)(2,1)}, bf16[80,1792]{1,0:T(8,128)(2,1)S(1)}, u32[]{:S(2)}, u32[]{:S(2)}) collective-permute-start(bf16[80,1792]{1,0:T(8,128)(2,1)} %get-tuple-element.52), channel_id=1, source_target_pairs={{0,3},{1,2},{2,1},{3,0},{4,7},{5,6},{6,5},{7,4},{8,11},{9,10},{10,... | collective-permute-start | bytes 860168 | tf_op jit(solution)/shard_map/ppermute | solution.py:65
  63.7 18.7 %collective-permute-start.3 = (bf16[320,960]{1,0:T(8,128)(2,1)}, bf16[320,960]{1,0:T(8,128)(2,1)}, u32[]{:S(2)}, u32[]{:S(2)}) collective-permute-start(bf16[320,960]{1,0:T(8,128)(2,1)} %copy-done.10), channel_id=1, source_target_pairs={{0,8},{4,12},{8,0},{12,4},{16,24},{20,28},{24,16},{28,20},{1,9},{5... | collective-permute-start | bytes 1843208 | tf_op jit(solution)/shard_map/ppermute | solution.py:65
  65.4 14.3 %collective-permute-start.4 = (bf16[320,960]{1,0:T(8,128)(2,1)}, bf16[320,960]{1,0:T(8,128)(2,1)}, u32[]{:S(2)}, u32[]{:S(2)}) collective-permute-start(bf16[320,960]{1,0:T(8,128)(2,1)} %copy-done.10), channel_id=1, source_target_pairs={{0,16},{4,20},{8,24},{12,28},{16,0},{20,4},{24,8},{28,12},{1,17},{... | collective-permute-start | bytes 1843208 | tf_op jit(solution)/shard_map/ppermute | solution.py:65
  66.9 25.0 %copy-start.5 = (bf16[320,1792]{1,0:T(8,128)(2,1)}, bf16[320,1792]{1,0:T(8,128)(2,1)S(1)}, u32[]{:S(2)}) copy-start(bf16[320,1792]{1,0:T(8,128)(2,1)S(1)} %constant_dynamic-update-slice_fusion.4) | copy-start | bytes 3440644
  66.9 12.1 %collective-permute-start.18 = (bf16[80,1664]{1,0:T(8,128)(2,1)S(1)}, bf16[80,1664]{1,0:T(8,128)(2,1)S(1)}, u32[]{:S(2)}, u32[]{:S(2)}) collective-permute-start(bf16[80,1664]{1,0:T(8,128)(2,1)S(1)} %copy-done.27), channel_id=1, source_target_pairs={{0,1},{1,0},{2,3},{3,2},{4,5},{5,4},{6,7},{7,6},{8,9},{9,8},{10,11... | collective-permute-start | bytes 798728 | tf_op jit(solution)/shard_map/ppermute | solution.py:65
  69.3 21.8 %collective-permute-start.19 = (bf16[80,1664]{1,0:T(8,128)(2,1)}, bf16[80,1664]{1,0:T(8,128)(2,1)S(1)}, u32[]{:S(2)}, u32[]{:S(2)}) collective-permute-start(bf16[80,1664]{1,0:T(8,128)(2,1)} %get-tuple-element.55), channel_id=1, source_target_pairs={{0,2},{1,3},{2,0},{3,1},{4,6},{5,7},{6,4},{7,5},{8,10},{9,11},{10,... | collective-permute-start | bytes 798728 | tf_op jit(solution)/shard_map/ppermute | solution.py:65
  70.9 21.0 %collective-permute-start.20 = (bf16[80,1664]{1,0:T(8,128)(2,1)S(1)}, bf16[80,1664]{1,0:T(8,128)(2,1)S(1)}, u32[]{:S(2)}, u32[]{:S(2)}) collective-permute-start(bf16[80,1664]{1,0:T(8,128)(2,1)S(1)} %copy-done.26), channel_id=1, source_target_pairs={{0,3},{1,2},{2,1},{3,0},{4,7},{5,6},{6,5},{7,4},{8,11},{9,10},{10,... | collective-permute-start | bytes 798728 | tf_op jit(solution)/shard_map/ppermute | solution.py:65
  80.7 11.9 %collective-permute-start.5 = (bf16[160,960]{1,0:T(8,128)(2,1)S(1)}, bf16[160,960]{1,0:T(8,128)(2,1)}, u32[]{:S(2)}, u32[]{:S(2)}) collective-permute-start(bf16[160,960]{1,0:T(8,128)(2,1)S(1)} %slice.10), channel_id=1, source_target_pairs={{0,8},{4,12},{8,0},{12,4},{16,24},{20,28},{24,16},{28,20},{1,9},{5... | collective-permute-start | bytes 921608 | tf_op jit(solution)/shard_map/ppermute | solution.py:65
  83.4 9.2 %collective-permute-start.6 = (bf16[160,960]{1,0:T(8,128)(2,1)S(1)}, bf16[160,960]{1,0:T(8,128)(2,1)}, u32[]{:S(2)}, u32[]{:S(2)}) collective-permute-start(bf16[160,960]{1,0:T(8,128)(2,1)S(1)} %slice.11), channel_id=1, source_target_pairs={{0,16},{4,20},{8,24},{12,28},{16,0},{20,4},{24,8},{28,12},{1,17},{... | collective-permute-start | bytes 921608 | tf_op jit(solution)/shard_map/ppermute | solution.py:65
  92.6 198.7 %all-gather.3.cloned.1.call-start = ((), (), s32[]{:S(2)}) async-start(), calls=%async_computation.1 | async-start | bytes 10321920 | tf_op jit(solution)/shard_map/all_gather | solution.py:687
  98.8 7.7 %collective-permute-start.7 = (bf16[320,960]{1,0:T(8,128)(2,1)S(1)}, bf16[320,960]{1,0:T(8,128)(2,1)}, u32[]{:S(2)}, u32[]{:S(2)}) collective-permute-start(bf16[320,960]{1,0:T(8,128)(2,1)S(1)} %copy-done.11), channel_id=1, source_target_pairs={{0,4},{4,0},{8,12},{12,8},{16,20},{20,16},{24,28},{28,24},{1,5},{5... | collective-permute-start | bytes 1843208 | tf_op jit(solution)/shard_map/ppermute | solution.py:65
  98.8 7.7 %collective-permute-start.8 = (bf16[320,960]{1,0:T(8,128)(2,1)}, bf16[320,960]{1,0:T(8,128)(2,1)}, u32[]{:S(2)}, u32[]{:S(2)}) collective-permute-start(bf16[320,960]{1,0:T(8,128)(2,1)} %collective-permute-done.3.refs_1_), channel_id=1, source_target_pairs={{0,4},{4,0},{8,12},{12,8},{16,20},{20,16},{24,28},{28,24},{1,5},{5... | collective-permute-start | bytes 1843208 | tf_op jit(solution)/shard_map/ppermute | solution.py:65
  99.3 7.2 %collective-permute-start.9 = (bf16[320,960]{1,0:T(8,128)(2,1)}, bf16[320,960]{1,0:T(8,128)(2,1)}, u32[]{:S(2)}, u32[]{:S(2)}) collective-permute-start(bf16[320,960]{1,0:T(8,128)(2,1)} %collective-permute-done.4.refs_2_), channel_id=1, source_target_pairs={{0,4},{4,0},{8,12},{12,8},{16,20},{20,16},{24,28},{28,24},{1,5},{5... | collective-permute-start | bytes 1843208 | tf_op jit(solution)/shard_map/ppermute | solution.py:65
  103.7 2.8 collective-permute-start.10
  104.2 2.3 collective-permute-start.11
  106.5 55.2 %collective-permute-start.23 = (bf16[80,2560]{1,0:T(8,128)(2,1)S(1)}, bf16[80,2560]{1,0:T(8,128)(2,1)S(1)}, u32[]{:S(2)}, u32[]{:S(2)}) collective-permute-start(bf16[80,2560]{1,0:T(8,128)(2,1)S(1)} %constant_dynamic-slice_fusion), channel_id=1, source_target_pairs={{0,3},{1,2},{2,1},{3,0},{4,7},{5,6},{6,5},{7,4},{8,11},{9,10},{10,... | collective-permute-start | bytes 1228808 | tf_op jit(solution)/shard_map/ppermute | solution.py:65
  108.9 52.9 %collective-permute-start.22 = (bf16[80,2560]{1,0:T(8,128)(2,1)S(1)}, bf16[80,2560]{1,0:T(8,128)(2,1)S(1)}, u32[]{:S(2)}, u32[]{:S(2)}) collective-permute-start(bf16[80,2560]{1,0:T(8,128)(2,1)S(1)} %constant_dynamic-slice_fusion), channel_id=1, source_target_pairs={{0,2},{1,3},{2,0},{3,1},{4,6},{5,7},{6,4},{7,5},{8,10},{9,11},{10,... | collective-permute-start | bytes 1228808 | tf_op jit(solution)/shard_map/ppermute | solution.py:65
  111.4 50.3 %collective-permute-start.21 = (bf16[80,2560]{1,0:T(8,128)(2,1)S(1)}, bf16[80,2560]{1,0:T(8,128)(2,1)S(1)}, u32[]{:S(2)}, u32[]{:S(2)}) collective-permute-start(bf16[80,2560]{1,0:T(8,128)(2,1)S(1)} %constant_dynamic-slice_fusion), channel_id=1, source_target_pairs={{0,1},{1,0},{2,3},{3,2},{4,5},{5,4},{6,7},{7,6},{8,9},{9,8},{10,11... | collective-permute-start | bytes 1228808 | tf_op jit(solution)/shard_map/ppermute | solution.py:65
  161.7 47.7 %copy-start.21 = (bf16[512,640]{1,0:T(8,128)(2,1)S(1)}, bf16[512,640]{1,0:T(8,128)(2,1)}, u32[]{:S(2)}) copy-start(bf16[512,640]{1,0:T(8,128)(2,1)} %attention.1.refs_0_) | copy-start | bytes 1966084
  161.7 92.5 %copy-start.12 = (f32[2560]{0:T(1024)S(1)}, f32[2560]{0:T(1024)}, u32[]{:S(2)}) copy-start(f32[2560]{0:T(1024)} %param.16) | copy-start | bytes 30724
  161.9 109.3 %copy-start.6 = (bf16[3,80,2560]{2,1,0:T(8,128)(2,1)}, bf16[3,80,2560]{2,1,0:T(8,128)(2,1)S(1)}, u32[]{:S(2)}) copy-start(bf16[3,80,2560]{2,1,0:T(8,128)(2,1)S(1)} %pad_maximum_fusion.refs_5_) | copy-start | bytes 3686404
  161.9 46.0 %collective-permute-start.25 = (bf16[3,80,2560]{2,1,0:T(8,128)(2,1)S(1)}, bf16[3,80,2560]{2,1,0:T(8,128)(2,1)S(1)}, u32[]{:S(2)}, u32[]{:S(2)}) collective-permute-start(bf16[3,80,2560]{2,1,0:T(8,128)(2,1)S(1)} %pad_maximum_fusion.refs_5_), channel_id=1, source_target_pairs={{0,16},{4,20},{8,24},{12,28},{16,0},{20,4},{24,8},{28,12},{1,17},{... | collective-permute-start | bytes 3686408 | tf_op jit(solution)/shard_map/ppermute | solution.py:65
  163.6 75.3 %collective-permute-start.24 = (bf16[3,80,2560]{2,1,0:T(8,128)(2,1)S(1)}, bf16[3,80,2560]{2,1,0:T(8,128)(2,1)S(1)}, u32[]{:S(2)}, u32[]{:S(2)}) collective-permute-start(bf16[3,80,2560]{2,1,0:T(8,128)(2,1)S(1)} %pad_maximum_fusion.refs_5_), channel_id=1, source_target_pairs={{0,8},{4,12},{8,0},{12,4},{16,24},{20,28},{24,16},{28,20},{1,9},{5... | collective-permute-start | bytes 3686408 | tf_op jit(solution)/shard_map/ppermute | solution.py:65
  207.9 63.3 %copy-start.15 = (bf16[3,80,2560]{2,1,0:T(8,128)(2,1)}, bf16[3,80,2560]{2,1,0:T(8,128)(2,1)S(1)}, u32[]{:S(2)}) copy-start(bf16[3,80,2560]{2,1,0:T(8,128)(2,1)S(1)} %collective-permute-done.25.refs_7_) | copy-start | bytes 3686404
  207.9 42.9 %collective-permute-start.26 = (bf16[3,80,2560]{2,1,0:T(8,128)(2,1)S(1)}, bf16[3,80,2560]{2,1,0:T(8,128)(2,1)S(1)}, u32[]{:S(2)}, u32[]{:S(2)}) collective-permute-start(bf16[3,80,2560]{2,1,0:T(8,128)(2,1)S(1)} %collective-permute-done.25.refs_7_), channel_id=1, source_target_pairs={{0,8},{4,12},{8,0},{12,4},{16,24},{20,28},{24,16},{28,20},{1,9},{5... | collective-permute-start | bytes 3686408 | tf_op jit(solution)/shard_map/ppermute | solution.py:65
  209.4 29.5 %collective-permute-start.12 = (bf16[512,640]{1,0:T(8,128)(2,1)S(1)}, bf16[512,640]{1,0:T(8,128)(2,1)}, u32[]{:S(2)}, u32[]{:S(2)}) collective-permute-start(bf16[512,640]{1,0:T(8,128)(2,1)S(1)} %copy-done.21), channel_id=1, source_target_pairs={{0,1},{1,0},{2,3},{3,2},{4,5},{5,4},{6,7},{7,6},{8,9},{9,8},{10,11... | collective-permute-start | bytes 1966088 | tf_op jit(solution)/shard_map/ppermute | solution.py:65
  210.9 39.9 %collective-permute-start.13 = (bf16[512,640]{1,0:T(8,128)(2,1)S(1)}, bf16[512,640]{1,0:T(8,128)(2,1)S(1)}, u32[]{:S(2)}, u32[]{:S(2)}) collective-permute-start(bf16[512,640]{1,0:T(8,128)(2,1)S(1)} %copy-done.21), channel_id=1, source_target_pairs={{0,2},{1,3},{2,0},{3,1},{4,6},{5,7},{6,4},{7,5},{8,10},{9,11},{10,... | collective-permute-start | bytes 1966088 | tf_op jit(solution)/shard_map/ppermute | solution.py:65
  213.3 56.6 %collective-permute-start.27 = (bf16[3,80,2560]{2,1,0:T(8,128)(2,1)S(1)}, bf16[3,80,2560]{2,1,0:T(8,128)(2,1)S(1)}, u32[]{:S(2)}, u32[]{:S(2)}) collective-permute-start(bf16[3,80,2560]{2,1,0:T(8,128)(2,1)S(1)} %pad_maximum_fusion.refs_5_), channel_id=1, source_target_pairs={{0,4},{4,0},{8,12},{12,8},{16,20},{20,16},{24,28},{28,24},{1,5},{5... | collective-permute-start | bytes 3686408 | tf_op jit(solution)/shard_map/ppermute | solution.py:65
  238.9 31.1 %collective-permute-start.29 = (bf16[3,80,2560]{2,1,0:T(8,128)(2,1)S(1)}, bf16[3,80,2560]{2,1,0:T(8,128)(2,1)S(1)}, u32[]{:S(2)}, u32[]{:S(2)}) collective-permute-start(bf16[3,80,2560]{2,1,0:T(8,128)(2,1)S(1)} %collective-permute-done.25.refs_7_), channel_id=1, source_target_pairs={{0,4},{4,0},{8,12},{12,8},{16,20},{20,16},{24,28},{28,24},{1,5},{5... | collective-permute-start | bytes 3686408 | tf_op jit(solution)/shard_map/ppermute | solution.py:65
  238.9 32.3 %copy-start.16 = (bf16[3,80,2560]{2,1,0:T(8,128)(2,1)}, bf16[3,80,2560]{2,1,0:T(8,128)(2,1)S(1)}, u32[]{:S(2)}) copy-start(bf16[3,80,2560]{2,1,0:T(8,128)(2,1)S(1)} %collective-permute-done.24.refs_6_) | copy-start | bytes 3686404
  238.9 31.0 %collective-permute-start.28 = (bf16[3,80,2560]{2,1,0:T(8,128)(2,1)S(1)}, bf16[3,80,2560]{2,1,0:T(8,128)(2,1)S(1)}, u32[]{:S(2)}, u32[]{:S(2)}) collective-permute-start(bf16[3,80,2560]{2,1,0:T(8,128)(2,1)S(1)} %collective-permute-done.24.refs_6_), channel_id=1, source_target_pairs={{0,4},{4,0},{8,12},{12,8},{16,20},{20,16},{24,28},{28,24},{1,5},{5... | collective-permute-start | bytes 3686408 | tf_op jit(solution)/shard_map/ppermute | solution.py:65
  250.9 20.3 %collective-permute-start.30 = (bf16[3,80,2560]{2,1,0:T(8,128)(2,1)S(1)}, bf16[3,80,2560]{2,1,0:T(8,128)(2,1)}, u32[]{:S(2)}, u32[]{:S(2)}) collective-permute-start(bf16[3,80,2560]{2,1,0:T(8,128)(2,1)S(1)} %collective-permute-done.26.refs_8_), channel_id=1, source_target_pairs={{0,4},{4,0},{8,12},{12,8},{16,20},{20,16},{24,28},{28,24},{1,5},{5... | collective-permute-start | bytes 3686408 | tf_op jit(solution)/shard_map/ppermute | solution.py:65
  250.9 19.1 %collective-permute-start.14 = (bf16[512,640]{1,0:T(8,128)(2,1)S(1)}, bf16[512,640]{1,0:T(8,128)(2,1)S(1)}, u32[]{:S(2)}, u32[]{:S(2)}) collective-permute-start(bf16[512,640]{1,0:T(8,128)(2,1)S(1)} %copy-done.21), channel_id=1, source_target_pairs={{0,3},{1,2},{2,1},{3,0},{4,7},{5,6},{6,5},{7,4},{8,11},{9,10},{10,... | collective-permute-start | bytes 1966088 | tf_op jit(solution)/shard_map/ppermute | solution.py:65
  291.3 85.1 %copy-start.7 = (bf16[512,640]{1,0:T(8,128)(2,1)S(1)}, bf16[512,640]{1,0:T(8,128)(2,1)}, u32[]{:S(2)}) copy-start(bf16[512,640]{1,0:T(8,128)(2,1)} %get-tuple-element.59) | copy-start | bytes 1966084
  315.9 19.0 %collective-permute-start.33 = (bf16[512,640]{1,0:T(8,128)(2,1)}, bf16[512,640]{1,0:T(8,128)(2,1)S(1)}, u32[]{:S(2)}, u32[]{:S(2)}) collective-permute-start(bf16[512,640]{1,0:T(8,128)(2,1)} %get-tuple-element.66), channel_id=1, source_target_pairs={{0,3},{1,2},{2,1},{3,0},{4,7},{5,6},{6,5},{7,4},{8,11},{9,10},{10,... | collective-permute-start | bytes 1966088 | tf_op jit(solution)/shard_map/ppermute | solution.py:65
  319.3 57.1 %collective-permute-start.32 = (bf16[512,640]{1,0:T(8,128)(2,1)}, bf16[512,640]{1,0:T(8,128)(2,1)S(1)}, u32[]{:S(2)}, u32[]{:S(2)}) collective-permute-start(bf16[512,640]{1,0:T(8,128)(2,1)} %get-tuple-element.65), channel_id=1, source_target_pairs={{0,2},{1,3},{2,0},{3,1},{4,6},{5,7},{6,4},{7,5},{8,10},{9,11},{10,... | collective-permute-start | bytes 1966088 | tf_op jit(solution)/shard_map/ppermute | solution.py:65
  331.1 45.3 %collective-permute-start.31 = (bf16[512,640]{1,0:T(8,128)(2,1)}, bf16[512,640]{1,0:T(8,128)(2,1)S(1)}, u32[]{:S(2)}, u32[]{:S(2)}) collective-permute-start(bf16[512,640]{1,0:T(8,128)(2,1)} %get-tuple-element.64), channel_id=1, source_target_pairs={{0,1},{1,0},{2,3},{3,2},{4,5},{5,4},{6,7},{7,6},{8,9},{9,8},{10,11... | collective-permute-start | bytes 1966088 | tf_op jit(solution)/shard_map/ppermute | solution.py:65
  (20 other events, 129.2 us)
Sparse Core Ops, SparseCore 0:
  92.8 55.9 all-gather.4
  150.7 91.3 all-gather.2

commit v4 on v3

v4 whole, which is shorter than its diff:
```python
import functools
import math

import jax
import jax.numpy as jnp
from jax import lax
from jax.experimental import pallas as pl
from jax.experimental.pallas import tpu as pltpu
from jax.sharding import PartitionSpec as P

HEADS = 32
KV_HEADS = 8
HD = 80
WINDOW = 4096
SINKS = 4
BLOCK = 128
CAP = 2


FLOOR_SCORE = -1e30
EPSILON = 1e-05
ROPE_BASE = 10000.0
FAR = 1 << 30
LANES = 128
TILE = 256
ROW_TILE = 128
VMEM_LIMIT = 56 * 1024 * 1024

ANY = pl.BlockSpec(memory_space=pl.ANY)
VMEM = pl.BlockSpec(memory_space=pltpu.VMEM)
SMEM = pl.BlockSpec(memory_space=pltpu.SMEM)


def rms_scale(row_data, gain_vec):
    values = row_data.astype(jnp.float32)
    mean_square = jnp.mean(values * values, axis=-1, keepdims=True)
    return (values * lax.rsqrt(mean_square + EPSILON) * gain_vec).astype(jnp.bfloat16)


def rope_tables(positions):
    half_width = HD // 2
    frequency = ROPE_BASE ** (-2.0 * jnp.arange(half_width, dtype=jnp.float32) / HD)
    angles = positions.astype(jnp.float32)[:, None] * frequency[None, :]
    cosine = jnp.cos(angles)
    sine = jnp.sin(angles)
    return (
        jnp.concatenate([cosine, cosine], axis=1),
        jnp.concatenate([-sine, sine], axis=1),
    )


def slot_ranks(slot_prompt, prompts, slots):
    onehot = (slot_prompt[:, None] == jnp.arange(prompts, dtype=jnp.int32)[None, :]).astype(
        jnp.int32
    )
    running = jnp.cumsum(onehot, axis=0)
    global_rank = jnp.sum(onehot * (running - 1), axis=1)
    local_count = jnp.cumsum(onehot.reshape(-1, slots, prompts), axis=1).reshape(-1, prompts)
    local_rank = jnp.sum(onehot * (local_count - 1), axis=1)
    return (global_rank, local_rank)


def swap(values, axis, bit):
    pairs = [(index, index ^ bit) for index in range(lax.axis_size(axis))]
    return lax.ppermute(values, axis, pairs)


def half_up(width):
    return (width // 2 + LANES - 1) // LANES * LANES


def pack_kernel(layouts, groups, *refs):
    kv_index = lax.axis_index("kv")
    outs = refs[len(refs) - groups * len(layouts) :]
    for choice in range(groups):

        @pl.when(kv_index == choice)
        def _():
            for which, spans in enumerate(layouts):
                for other in range(groups):
                    out = outs[which * groups + other]
                    column = 0
                    for matrix, first, last in spans:
                        start = (choice ^ other) * (refs[matrix].shape[1] // groups)
                        width = last - first
                        out[:, column : column + width] = refs[matrix][
                            :, start + first : start + last
                        ].astype(jnp.bfloat16)
                        column += width


def pack(matrices, groups, layouts, name):
    rows = matrices[0].shape[0]
    shapes = []
    for spans in layouts:
        width = sum(last - first for _, first, last in spans)
        shapes += [jax.ShapeDtypeStruct((rows, width), jnp.bfloat16)] * groups
    flat = pl.pallas_call(
        functools.partial(pack_kernel, layouts, groups),
        out_shape=tuple(shapes),
        in_specs=[VMEM] * len(matrices),
        out_specs=(VMEM,) * len(shapes),
        compiler_params=pltpu.CompilerParams(vmem_limit_bytes=VMEM_LIMIT),
        cost_estimate=pl.CostEstimate(
            flops=0,
            bytes_accessed=6 * rows * sum(matrix.shape[1] for matrix in matrices),
            transcendentals=0,
        ),
        name=name,
    )(*matrices)
    return [flat[first : first + groups] for first in range(0, len(flat), groups)]


def exchange(parts):
    moved = [parts[0]] + [swap(part, "kv", other) for other, part in enumerate(parts) if other]
    return jnp.concatenate(moved, axis=0)


def exchange_in_order(parts, kv_index):
    moved = jnp.stack(
        [parts[0]] + [swap(part, "kv", other) for other, part in enumerate(parts) if other], axis=0
    )
    order = jnp.arange(len(parts), dtype=jnp.int32) ^ kv_index
    return jnp.take(moved, order, axis=0).reshape(-1, moved.shape[2])


def after(values, *earlier):
    return lax.optimization_barrier((values, *earlier))[0]


def plane_gather(piece):
    rows = piece.shape[0]
    by_x = swap(piece, "blk", 2)
    by_y = swap(piece, "blk", 4)
    upper = swap(by_y[: rows // 2], "blk", 2)
    lower = swap(by_x[rows // 2 :], "blk", 4)
    mine = [(0, 0, piece), (2, 0, by_x), (4, 0, by_y), (6, 0, upper), (6, rows // 2, lower)]
    return mine + [(index ^ 1, first, swap(part, "blk", 1)) for index, first, part in mine]


def on_columns(body, index, width, count):
    if width % LANES == 0:
        body(pl.ds(pl.multiple_of(index * width, LANES), width))
        return
    for choice in range(count):
        pl.when(index == choice)(functools.partial(body, pl.ds(choice * width, width)))


def row_copies(sources, refs, buffer, sem, blk_index, kv_index, groups):
    copies = []
    total = buffer.shape[0]
    for (index, begin, _), ref in zip(sources, refs):
        rows = ref.shape[0]
        piece = total // 8
        block = piece // groups
        if rows == total and index is None:
            copies.append(pltpu.make_async_copy(ref, buffer, sem))
            continue
        for first in range(0, rows, block):
            if rows == total:
                base = first // piece * piece
            else:
                base = (blk_index ^ index) * piece
            other = (begin + first) % piece // block
            target = pl.multiple_of(base + (kv_index ^ other) * block, 16)
            copies.append(
                pltpu.make_async_copy(
                    ref.at[pl.ds(first, block)], buffer.at[pl.ds(target, block)], sem
                )
            )
    return copies


EXTRA = 16


def cache_kernel(blocks_ref, flags_ref, keys, values):
    first_row = lax.broadcasted_iota(jnp.int32, (EXTRA, 1), 0) == 0
    bias = jnp.where((flags_ref[...] > -FAR) | jnp.logical_not(first_row), 0.0, FLOOR_SCORE)
    for head in range(blocks_ref.shape[2]):
        keys[head, HD:, :] = bias.astype(jnp.bfloat16)
        for block in range(blocks_ref.shape[1]):
            place = pl.ds(block * BLOCK, BLOCK)
            keys[head, :HD, place] = blocks_ref[0, block, head]
            values[head, place, :] = blocks_ref[1, block, head].astype(jnp.float32).T.astype(
                jnp.bfloat16
            )


def cached_rows(blocks, flags):
    kv_local = blocks.shape[2]
    cached = flags.shape[1]
    return pl.pallas_call(
        cache_kernel,
        out_shape=(
            jax.ShapeDtypeStruct((kv_local, HD + EXTRA, cached), jnp.bfloat16),
            jax.ShapeDtypeStruct((kv_local, cached, HD), jnp.bfloat16),
        ),
        in_specs=[VMEM, VMEM],
        out_specs=(VMEM, VMEM),
        compiler_params=pltpu.CompilerParams(vmem_limit_bytes=VMEM_LIMIT),
        cost_estimate=pl.CostEstimate(
            flops=0, bytes_accessed=4 * blocks.size, transcendentals=0
        ),
        name="cached",
    )(blocks, flags)


def project_kernel(
    sources, groups, kv_local, per_group, place_ref, normed_ref, cos_ref, sin_ref, flags_ref, *refs
):
    count = len(sources)
    pieces = refs[:count]
    queries, keys, values, weights, projected, sem = refs[count:]
    copies = row_copies(sources, pieces, weights, sem.at[0], place_ref[0], place_ref[2], groups)
    for copy in copies:
        copy.start()
    new_rows = normed_ref.shape[0]
    chunk_rows = per_group * ROW_TILE
    first_row = lax.broadcasted_iota(jnp.int32, (EXTRA, 1), 0) == 0
    bias = jnp.where((flags_ref[...] > -FAR) | jnp.logical_not(first_row), 0.0, FLOOR_SCORE)
    marker = jnp.where(
        lax.broadcasted_iota(jnp.int32, (chunk_rows, EXTRA), 1) == 0, 1.0, 0.0
    ).astype(jnp.bfloat16)
    for head in range(kv_local):
        keys[head, HD:, :] = bias.astype(jnp.bfloat16)
        for chunk in range(new_rows // ROW_TILE):
            queries[chunk, head, :, HD:] = marker
    for copy in copies:
        copy.wait()

    def project(step, carry):
        rows = pl.ds(pl.multiple_of(step * TILE, TILE), TILE)
        projected[rows, :] = jnp.dot(
            normed_ref[rows, :], weights[...], preferred_element_type=jnp.float32
        )
        return carry

    lax.fori_loop(0, new_rows // TILE, project, 0)

    def rotated(rows, column):
        part = projected[rows, column : column + HD]
        turned = jnp.concatenate([part[:, HD // 2 :], part[:, : HD // 2]], axis=1)
        return part * cos_ref[rows, :] + turned * sin_ref[rows, :]

    query_width = kv_local * per_group * HD
    for chunk in range(new_rows // ROW_TILE):
        rows = pl.ds(chunk * ROW_TILE, ROW_TILE)
        for head in range(kv_local):
            for sub in range(per_group):
                queries[chunk, head, sub * ROW_TILE : (sub + 1) * ROW_TILE, :HD] = rotated(
                    rows, (head * per_group + sub) * HD
                ).astype(jnp.bfloat16)
            keys[head, :HD, rows] = rotated(rows, query_width + head * HD).T.astype(jnp.bfloat16)
            column = query_width + (kv_local + head) * HD
            values[head, rows, :] = projected[rows, column : column + HD].astype(jnp.bfloat16)


def project_rows(place, normed, tables, flags, sources, groups, kv_local, per_group):
    new_rows = normed.shape[0]
    arrays = [values for _, _, values in sources]
    width = arrays[0].shape[1]
    chunks = new_rows // ROW_TILE
    return pl.pallas_call(
        functools.partial(project_kernel, sources, groups, kv_local, per_group),
        out_shape=(
            jax.ShapeDtypeStruct(
                (chunks, kv_local, per_group * ROW_TILE, HD + EXTRA), jnp.bfloat16
            ),
            jax.ShapeDtypeStruct((kv_local, HD + EXTRA, new_rows), jnp.bfloat16),
            jax.ShapeDtypeStruct((kv_local, new_rows, HD), jnp.bfloat16),
        ),
        in_specs=[SMEM] + [VMEM] * 4 + [ANY] * len(arrays),
        out_specs=(VMEM,) * 3,
        scratch_shapes=[
            pltpu.VMEM((normed.shape[1], width), jnp.bfloat16),
            pltpu.VMEM((new_rows, width), jnp.float32),
            pltpu.SemaphoreType.DMA((1,)),
        ],
        compiler_params=pltpu.CompilerParams(vmem_limit_bytes=VMEM_LIMIT),
        cost_estimate=pl.CostEstimate(
            flops=2 * new_rows * normed.shape[1] * width,
            bytes_accessed=2 * normed.shape[1] * width,
            transcendentals=0,
        ),
        name="project",
    )(place, normed, *tables, flags, *arrays)


def attention_kernel(
    first_step,
    place_ref,
    queries,
    cached_keys,
    cached_values,
    own_keys,
    own_values,
    cached_ref,
    own_ref,
    out_ref,
    scores,
    probs,
    folded,
    shifts,
    summed,
):
    prefix_here = place_ref[1]
    kv_local, _, cached = cached_keys.shape
    new_rows = own_keys.shape[2]
    chunk_rows = queries.shape[2]
    per_group = chunk_rows // ROW_TILE
    factor = math.log2(math.e) / math.sqrt(HD)
    group = 64
    widest = min(4 * LANES, cached)
    tiles = [
        (first, cached_keys, cached_values, first, widest) for first in range(0, cached, widest)
    ]
    tiles.append((cached, own_keys, own_values, 0, new_rows))

    def score(step, head, first, keys, _, begin, width):
        scores[head, :, pl.ds(first, width)] = jnp.dot(
            queries[step, head],
            keys[head, :, pl.ds(begin, width)],
            preferred_element_type=jnp.float32,
        )
        own = keys is own_keys
        for part in range(chunk_rows // group):
            rows = pl.ds(part * group, group)
            if own:
                row_id = (first_step + step) * ROW_TILE + (part * group) % ROW_TILE + (
                    lax.broadcasted_iota(jnp.int32, (group, LANES), 0)
                )
            top = folded[head, rows, :]
            for lane in range(0, width, LANES):
                place = pl.ds(first + lane, LANES)
                piece = scores[head, rows, place]
                if own:
                    own_id = lane + lax.broadcasted_iota(jnp.int32, (group, LANES), 1)
                    piece = jnp.where(own_id <= row_id, piece, FLOOR_SCORE)
                    scores[head, rows, place] = piece
                top = jnp.maximum(top, piece)
            folded[head, rows, :] = top

    def narrow(step, head):
        def some(part, inner):
            rows = pl.ds(pl.multiple_of(part * 16, 16), 16)
            row_id = (first_step + step) * ROW_TILE + lax.rem(part * 16, ROW_TILE) + (
                lax.broadcasted_iota(jnp.int32, (16, 1), 0)
            )
            oldest = prefix_here + row_id - WINDOW
            old = jnp.where(cached_ref[...] > oldest, scores[head, rows, :cached], FLOOR_SCORE)
            new = jnp.where(own_ref[...] > oldest, scores[head, rows, cached:], FLOOR_SCORE)
            scores[head, rows, :cached] = old
            scores[head, rows, cached:] = new
            top = jnp.maximum(
                jnp.max(old, axis=1, keepdims=True), jnp.max(new, axis=1, keepdims=True)
            )
            folded[head, rows, :] = jnp.broadcast_to(top, (16, LANES))
            return inner

        lax.fori_loop(0, chunk_rows // 16, some, 0)

    def weigh(head, start, first, _, values, begin, width):
        for part in range(chunk_rows // group):
            rows = pl.ds(part * group, group)
            shift = shifts[head, rows, :]
            total = None if start else folded[head, rows, :]
            for lane in range(0, width, LANES):
                place = pl.ds(first + lane, LANES)
                piece = jnp.exp2(scores[head, rows, place] * factor - shift)
                total = piece if total is None else total + piece
                probs[head, rows, place] = piece.astype(jnp.bfloat16)
            folded[head, rows, :] = total
        return jnp.dot(
            probs[head, :, pl.ds(first, width)],
            values[head, pl.ds(begin, width), :],
            preferred_element_type=jnp.float32,
        )

    def attend(windowed, step, carry):
        for head in range(kv_local):
            folded[head] = jnp.full(folded.shape[1:], FLOOR_SCORE, jnp.float32)
            for tile in tiles:
                score(step, head, *tile)
        for head in range(kv_local):
            if windowed:
                narrow(step, head)
            for part in range(chunk_rows // group):
                rows = pl.ds(part * group, group)
                top = jnp.max(folded[head, rows, :], axis=1, keepdims=True) * factor
                shifts[head, rows, :] = jnp.broadcast_to(top, (group, LANES))
            for which, tile in enumerate(tiles):
                part = weigh(head, which == 0, *tile)
                summed[head] = part if which == 0 else summed[head] + part
            rows = pl.ds(pl.multiple_of(step * ROW_TILE, ROW_TILE), ROW_TILE)
            for sub in range(per_group):
                part = pl.ds(sub * ROW_TILE, ROW_TILE)
                total = jnp.sum(folded[head, part, :], axis=1, keepdims=True)
                column = (head * per_group + sub) * HD
                out_ref[rows, column : column + HD] = (summed[head, part, :] / total).astype(
                    jnp.bfloat16
                )
        return carry

    behind = prefix_here + new_rows > WINDOW
    for windowed in (False, True):

        @pl.when(behind == windowed)
        def _():
            lax.fori_loop(0, queries.shape[0], functools.partial(attend, windowed), 0)


def attend_rows(place, first_step, queries, cached, own, cached_pos, own_pos):
    chunks, kv_local, chunk_rows, _ = queries.shape
    span = cached_pos.shape[1] + own_pos.shape[1]
    heads = kv_local * chunk_rows // ROW_TILE
    new_rows = chunks * ROW_TILE
    return pl.pallas_call(
        functools.partial(attention_kernel, first_step),
        out_shape=jax.ShapeDtypeStruct((new_rows, heads * HD), jnp.bfloat16),
        in_specs=[SMEM] + [VMEM] * 7,
        out_specs=VMEM,
        scratch_shapes=[
            pltpu.VMEM((kv_local, chunk_rows, span), jnp.float32),
            pltpu.VMEM((kv_local, chunk_rows, span), jnp.bfloat16),
            pltpu.VMEM((kv_local, chunk_rows, LANES), jnp.float32),
            pltpu.VMEM((kv_local, chunk_rows, LANES), jnp.float32),
            pltpu.VMEM((kv_local, chunk_rows, HD), jnp.float32),
        ],
        compiler_params=pltpu.CompilerParams(vmem_limit_bytes=VMEM_LIMIT),
        cost_estimate=pl.CostEstimate(
            flops=8 * heads * new_rows * span * LANES,
            bytes_accessed=4 * span * LANES * kv_local,
            transcendentals=heads * new_rows * span,
        ),
        name="attention",
    )(place, queries, *cached, *own, cached_pos, own_pos)


def middle_kernel(sources, groups, place_ref, tokens_ref, gain_ref, *refs):
    parts = len(refs) - len(sources) - 7
    att = refs[:parts]
    own_ref = refs[parts]
    rest = refs[parts + 1 :]
    shares = rest[: len(sources)]
    normed_ref, residual_ref, gathered, weights, middle, sem = rest[len(sources) :]
    blk_index = place_ref[0]
    kv_index = place_ref[2]
    group_rows = own_ref.shape[0]
    new_rows, model = tokens_ref.shape
    tile = 2 * TILE
    loads = []
    for step in range(model // tile):
        columns = pl.ds(step * tile, tile)
        copies = []
        if shares[0].ndim == 3:
            copies.append((own_ref.at[:, columns], weights.at[pl.ds(0, group_rows), columns]))
            for (index, _, _), ref in zip(sources, shares):
                part = ref.shape[1]
                first = pl.multiple_of((blk_index ^ index) * part, 16)
                for other in range(1, groups):
                    rows = pl.ds(other * group_rows + first, part)
                    copies.append((ref.at[other - 1, :, columns], weights.at[rows, columns]))
        else:
            for other in range(groups):
                first = pl.multiple_of((kv_index ^ other) * group_rows, 16)
                rows = pl.ds(other * group_rows, group_rows)
                copies.append(
                    (shares[0].at[pl.ds(first, group_rows), columns], weights.at[rows, columns])
                )
        loads.append(
            [pltpu.make_async_copy(source, target, sem.at[step]) for source, target in copies]
        )
        for copy in loads[-1]:
            copy.start()
    some_rows, feature = att[0].shape
    for at, part in enumerate(att):
        first, other = at // groups * some_rows, at % groups
        gathered[first : first + some_rows, other * feature : (other + 1) * feature] = part[...]
    for step in range(model // tile):
        columns = pl.ds(step * tile, tile)
        for copy in loads[step]:
            copy.wait()
        summed = jnp.dot(gathered[...], weights[:, columns], preferred_element_type=jnp.float32)
        middle[:, columns] = (tokens_ref[:, columns].astype(jnp.float32) + summed).astype(
            jnp.bfloat16
        )

    def scale(step, carry):
        rows = pl.ds(pl.multiple_of(step * 16, 16), 16)
        part = middle[rows, :].astype(jnp.float32)
        mean_square = jnp.mean(part * part, axis=1, keepdims=True)
        normed_ref[rows, :] = (part * lax.rsqrt(mean_square + EPSILON) * gain_ref[...]).astype(
            jnp.bfloat16
        )
        return carry

    lax.fori_loop(0, new_rows // 16, scale, 0, unroll=2)
    out_width = model // groups

    def keep(columns):
        residual_ref[...] = middle[:, columns]

    on_columns(keep, kv_index, out_width, groups)


def middle_rows(place, tokens, gain, attended, own, sources, groups):
    new_rows, model = tokens.shape
    arrays = [values for _, _, values in sources]
    return pl.pallas_call(
        functools.partial(middle_kernel, sources, groups),
        out_shape=(
            jax.ShapeDtypeStruct((new_rows, model), jnp.bfloat16),
            jax.ShapeDtypeStruct((new_rows, model // groups), jnp.bfloat16),
        ),
        in_specs=[SMEM, VMEM, VMEM] + [VMEM] * len(attended) + [ANY] * (1 + len(arrays)),
        out_specs=(VMEM, VMEM),
        scratch_shapes=[
            pltpu.VMEM((new_rows, model), jnp.bfloat16),
            pltpu.VMEM((model, model), jnp.bfloat16),
            pltpu.VMEM((new_rows, model), jnp.bfloat16),
            pltpu.SemaphoreType.DMA((model // (2 * TILE),)),
        ],
        compiler_params=pltpu.CompilerParams(vmem_limit_bytes=VMEM_LIMIT),
        cost_estimate=pl.CostEstimate(
            flops=2 * new_rows * model * model,
            bytes_accessed=2 * model * model,
            transcendentals=0,
        ),
        name="middle",
    )(place, tokens, gain, *attended, own, *arrays)


def hidden_chunks(width):
    whole = width // LANES * LANES
    chunks = []
    first = 0
    while first < whole:
        units = min(TILE, whole - first)
        chunks.append((first, first, whole + first, units))
        first += units
    if width > whole:
        chunks.append((whole, 2 * whole, 2 * whole + width - whole, width - whole))
    return chunks


def mlp_kernel(groups, widths, place_ref, normed_ref, down_ref, left, right, *refs):
    outs = refs[:groups]
    first_half, second_half, down, hidden, sems = refs[groups:]
    kv_index = place_ref[2]
    chunks = []
    base = 0
    for width, source, buffer in zip(widths, (left, right), (first_half, second_half)):
        for first, gate, up, units in hidden_chunks(width):
            if units < LANES:
                spans = [(gate, 2 * units)]
            else:
                spans = [(gate, units), (up, units)]
            copies = [
                pltpu.make_async_copy(
                    source.at[:, pl.ds(column, count)],
                    buffer.at[:, pl.ds(column, count)],
                    sems.at[len(chunks)],
                )
                for column, count in spans
            ]
            chunks.append((buffer, spans, base + first, units, copies))
        base += width
    last = pltpu.make_async_copy(down_ref, down, sems.at[len(chunks)])
    ahead = 3
    for _, _, _, _, copies in chunks[:ahead]:
        for copy in copies:
            copy.start()
    for at, (buffer, spans, first, units, copies) in enumerate(chunks):
        for copy in copies:
            copy.wait()
        if at + ahead < len(chunks):
            for copy in chunks[at + ahead][4]:
                copy.start()
        elif at + ahead == len(chunks):
            last.start()
        products = [
            jnp.dot(
                normed_ref[...],
                buffer[:, column : column + count],
                preferred_element_type=jnp.float32,
            )
            for column, count in spans
        ]
        if len(products) == 2:
            gated, raised = products
        else:
            gated, raised = products[0][:, :units], products[0][:, units:]
        hidden[:, first : first + units] = (gated / (1.0 + jnp.exp(-gated)) * raised).astype(
            jnp.bfloat16
        )
    last.wait()
    out_width = outs[0].shape[1]
    for other in range(groups):

        def product(columns, out=outs[other]):
            out[...] = jnp.dot(
                hidden[...], down[:, columns], preferred_element_type=jnp.float32
            ).astype(out.dtype)

        on_columns(product, kv_index ^ other, out_width, groups)


def mlp_parts(place, normed, w_down, left, right, groups, widths):
    new_rows, model = normed.shape
    out_width = model // groups
    return pl.pallas_call(
        functools.partial(mlp_kernel, groups, widths),
        out_shape=tuple(
            jax.ShapeDtypeStruct((new_rows, out_width), jnp.bfloat16 if other else jnp.float32)
            for other in range(groups)
        ),
        in_specs=[SMEM, VMEM, ANY, ANY, ANY],
        out_specs=(VMEM,) * groups,
        scratch_shapes=[
            pltpu.VMEM(left.shape, jnp.bfloat16),
            pltpu.VMEM(right.shape, jnp.bfloat16),
            pltpu.VMEM(w_down.shape, jnp.bfloat16),
            pltpu.VMEM((new_rows, w_down.shape[0]), jnp.bfloat16),
            pltpu.SemaphoreType.DMA((1 + sum(len(hidden_chunks(width)) for width in widths),)),
        ],
        compiler_params=pltpu.CompilerParams(vmem_limit_bytes=VMEM_LIMIT),
        cost_estimate=pl.CostEstimate(
            flops=6 * new_rows * model * w_down.shape[0],
            bytes_accessed=6 * model * w_down.shape[0],
            transcendentals=new_rows * w_down.shape[0],
        ),
        name="mlp",
    )(place, normed, w_down, left, right)


def shards(
    tokens,
    attn_gain,
    mlp_gain,
    w_query,
    w_key,
    w_value,
    w_gate,
    w_up,
    w_out,
    w_down,
    cache,
    slot_prompt,
    prefix_len,
    new_len,
):
    groups = lax.axis_size("kv")
    blk_index = lax.axis_index("blk")
    kv_index = lax.axis_index("kv")
    query_width = w_query.shape[1] // groups
    key_width = w_key.shape[1] // groups
    per_group = HEADS // KV_HEADS
    new_rows = tokens.shape[0]
    prompts = prefix_len.shape[0]
    slots = cache.shape[1]
    prefix_here = prefix_len[blk_index]
    live_count = new_len[blk_index]
    place = jnp.stack([blk_index, prefix_here, kv_index]).astype(jnp.int32)

    global_rank, local_rank = slot_ranks(slot_prompt, prompts, slots)
    own_prompts = lax.dynamic_slice_in_dim(slot_prompt, blk_index * slots, slots)
    own_ranks = lax.dynamic_slice_in_dim(local_rank, blk_index * slots, slots)
    placed = own_prompts * CAP + own_ranks
    buffer_ids = jnp.arange(prompts * CAP, dtype=jnp.int32)
    matches = placed[None, :] == buffer_ids[:, None]
    source_slot = jnp.sum(
        jnp.where(matches, jnp.arange(slots, dtype=jnp.int32)[None, :], 0), axis=1
    )
    outgoing = jnp.take(cache, source_slot, axis=1)
    arrived = lax.all_to_all(outgoing, "blk", split_axis=1, concat_axis=1, tiled=True)
    slot_ids = jnp.arange(prompts * slots, dtype=jnp.int32)
    landing = slot_ids // slots * CAP + local_rank
    for_me = slot_prompt == blk_index
    received = (landing[None, :] == buffer_ids[:, None]) & for_me[None, :]
    block_number = jnp.sum(jnp.where(received, global_rank[None, :], 0), axis=1)
    block_live = jnp.any(received, axis=1)
    key_pos = block_number[:, None] * BLOCK + jnp.arange(BLOCK, dtype=jnp.int32)[None, :]
    key_live = block_live[:, None] & (key_pos < prefix_here)
    cached_pos = jnp.where(key_live, jnp.where(key_pos < SINKS, FAR, key_pos), -FAR)
    cached_pos = cached_pos.reshape(1, -1)
    row_ids = jnp.arange(new_rows, dtype=jnp.int32)
    positions = prefix_here + row_ids
    own_pos = jnp.where(
        row_ids < live_count, jnp.where(positions < SINKS, FAR, positions), -FAR
    ).reshape(1, -1)

    normed = rms_scale(tokens, attn_gain)
    tables = rope_tables(positions)

    in_place = lax.axis_size("blk") == 8 and w_query.shape[0] % 16 == 0
    spans = [(0, 0, query_width), (1, 0, key_width), (2, 0, key_width)]
    (qkv_parts,) = pack((w_query, w_key, w_value), groups, [spans], "pack_qkv")
    if in_place:
        moved_qkv = exchange(qkv_parts)
        qkv = plane_gather(after(moved_qkv, normed, *tables, own_pos))
        across = [qkv[at][2] for at in (3, 4)]
    else:
        moved_qkv = exchange_in_order(qkv_parts, kv_index)
        qkv = [(None, 0, lax.all_gather(moved_qkv, "blk", axis=0, tiled=True))]
        across = [moved_qkv]

    hidden_width = w_gate.shape[1] // groups
    cut = half_up(hidden_width)
    widths = (cut, hidden_width - cut)
    layouts = []
    for first, last in ((0, cut), (cut, hidden_width)):
        whole = first + (last - first) // LANES * LANES
        layouts.append([(0, first, whole), (1, first, whole)])
        if whole < last:
            layouts[-1] += [(0, whole, last), (1, whole, last)]
    packed = pack((w_gate, w_up), groups, layouts, "pack_pair")

    moved = exchange_in_order(after(packed[1], moved_qkv, arrived), kv_index)
    second_half = lax.all_gather(after(moved, *across), "blk", axis=0, tiled=True)

    eighth = w_out.shape[0] // lax.axis_size("blk")
    spread = in_place and eighth % 16 == 0
    if spread:
        share = lax.dynamic_slice_in_dim(w_out, blk_index * eighth, eighth, 0)
        share = after(share, *across)
        shares = jnp.stack([swap(share, "kv", other) for other in range(1, groups)], axis=0)

    cached = cached_rows(arrived, cached_pos)
    queries, *own = project_rows(
        place, normed, tables, own_pos, qkv, groups, cache.shape[2], per_group
    )
    half = queries.shape[0] // 2
    upper = attend_rows(place, 0, queries[:half], cached, own, cached_pos, own_pos)
    earlier = (upper, shares) if spread else (upper,)
    moved = exchange_in_order(after(packed[0], *earlier), kv_index)
    if spread:
        shares = after(shares, upper)
        by_x = swap(shares, "blk", 2)
        by_y = swap(shares, "blk", 4)
    lower = attend_rows(place, half, queries[half:], cached, own, cached_pos, own_pos)
    earlier = (lower, by_x, by_y) if spread else (lower,)
    first_half = lax.all_gather(after(moved, *earlier), "blk", axis=0, tiled=True)
    attended = jnp.concatenate([upper, lower], axis=0)
    everyone = [attended] + [swap(attended, "kv", other) for other in range(1, groups)]

    if spread:
        by_y = after(by_y, lower)
        mine = [(0, 0, shares), (2, 0, by_x), (4, 0, by_y), (6, 0, swap(by_y, "blk", 2))]
        w_out_sources = mine + [
            (index ^ 1, first, swap(part, "blk", 1)) for index, first, part in mine
        ]
    else:
        w_out_sources = [(0, 0, lax.all_gather(w_out, "kv", axis=0, tiled=True))]

    normed_mid, residual = middle_rows(
        place, tokens, mlp_gain.reshape(1, -1), everyone, w_out, w_out_sources, groups
    )
    parts = mlp_parts(place, normed_mid, w_down, first_half, second_half, groups, widths)
    reduced = parts[0]
    for other in range(1, groups):
        reduced = reduced + swap(parts[other], "kv", other).astype(jnp.float32)
    mixed = jnp.where(
        (row_ids < live_count)[:, None], residual.astype(jnp.float32) + reduced, 0.0
    )
    return mixed.astype(jnp.bfloat16)


def solution(mesh):
    return jax.shard_map(
        shards,
        mesh=mesh,
        in_specs=(
            P("blk", None),
            P(),
            P(),
            P(("blk", "kv"), None),
            P(("blk", "kv"), None),
            P(("blk", "kv"), None),
            P(("blk", "kv"), None),
            P(("blk", "kv"), None),
            P("kv", None),
            P("kv", None),
            P(None, "blk", "kv", None, None),
            P(),
            P(),
            P(),
        ),
        out_specs=P("blk", "kv"),
        check_vma=False,
    )
```

time: 386 us -> 329 us (0.85); the launches traced: 386 us -> 323 us
  waiting for transfers between devices: 180 us -> 125 us
  starting transfers between devices: 61.3 us -> 51.8 us
  Pallas kernels: 100 us -> 91.9 us
  local copies, waits for them, and re-layouts: 14.8 us -> 20.4 us
  other arithmetic: 15.5 us -> 19.5 us
    ppermute x34, waiting for transfers between devices: 179 us -> 125 us  [swap(): return lax.ppermute(values, axis, pairs)]
    ppermute x34, starting transfers between devices: 57.4 us -> 46.8 us  [swap(): return lax.ppermute(values, axis, pairs)]
    pallas_call x2 -> x5, Pallas kernels: 74.9 us -> 69.3 us  [the longest x2 27.4 us: attend_rows(): pl.pallas_call(functools.partial(attention_kernel, first_step), out_shape...]
    unnamed x72 -> x70, local copies, waits for them, and re-layouts: 5.68 us -> 9.44 us
  transfers between devices with their start and end apart: 37 -> 37, of which waited for: 11 -> 11; matrix products, arithmetic and copies ran while one was open for 6% -> 10% of each run, Pallas kernels for 19% -> 20%
where the time goes in v4:
time: 329 us; the launch traced here: 323 us
  waiting for transfers between devices  125 us (38%)
  Pallas kernels  91.9 us (28%)
  starting transfers between devices  51.8 us (16%)
  local copies, waits for them, and re-layouts  20.4 us (6%)
  other arithmetic  19.5 us (6%)
  between operations  14 us (4%)
    ppermute x34, waiting for transfers between devices, swap(): return lax.ppermute(values, axis, pairs)  125 us
    ppermute x34, starting transfers between devices, swap(): return lax.ppermute(values, axis, pairs)  46.8 us
    pallas_call x2, Pallas kernels, attend_rows(): pl.pallas_call(functools.partial(attention_kernel, first_step), out_shape...  27.4 us
    pallas_call x1, Pallas kernels, mlp_parts(): pl.pallas_call(functools.partial(mlp_kernel, groups, widths), out_shape=t...  23.9 us
    pallas_call x1, Pallas kernels, middle_rows(): pl.pallas_call(functools.partial(middle_kernel, sources, groups), out_sha...  16 us
    pallas_call x1, Pallas kernels, project_rows(): pl.pallas_call(functools.partial(project_kernel, sources, groups, kv_loca...  15.1 us
    unnamed x70, local copies, waits for them, and re-layouts  9.44 us
  transfers between devices with their start and end apart: 37, of which 11 were waited for; matrix products, arithmetic and copies ran while one was open for 10% of the time, Pallas kernels for 20%

profile of v4, /device:TPU:0, one launch (start us, length us, event | category | flops | bytes accessed | tf_op | source)
XLA Modules:
  0.0 322.8 jit_solution(9599578522849590766)
XLA Ops:
  6.5 2.3 pack_qkv.1
  8.9 3.0 collective-permute-start
  11.9 2.6 collective-permute-start.1
  16.1 1.3 select_bitcast_fusion
  17.3 4.5 %all-to-all-start = ((bf16[2,16,2,80,128]{4,3,2,0,1:T(8,128)(2,1)}), bf16[2,16,2,80,128]{4,3,2,0,1:T(8,128)(2,1)}, u32[]{:S(2)}, u32[]{:S(2)}) async-start(bf16[2,16,2,80,128]{4,3,2,0,1:T(8,128)(2,1)} %select_bitcast_fusion), calls=%async_computation | async-start | bytes 2621440 | tf_op jit(solution)/shard_map/all_to_all | solution.py:676
  23.8 2.1 fusion.2.normed_ref
  26.0 1.0 fusion.3
  26.9 1.0 pad_maximum_fusion.4
  29.3 1.8 compare_select_fusion.2.flags_ref.own_ref
  31.1 1.6 constant_dynamic-update-slice_fusion.2
  32.7 1.6 constant_dynamic-update-slice_fusion.1
  35.0 1.9 collective-permute-start.4
  36.9 1.5 collective-permute-start.3
  38.3 4.2 %pack_pair.1 = (bf16[80,1792]{1,0:T(8,128)(2,1)}, bf16[80,1792]{1,0:T(8,128)(2,1)}, bf16[80,1792]{1,0:T(8,128)(2,1)}, bf16[80,1792]{1,0:T(8,128)(2,1)}, bf16[80,...) custom-call(f32[80,6912]{1,0:T(8,128)} %refs_0_.3, ...), custom_call_target="tpu_custom_call" | custom-call | bytes 6635520 | tf_op jit(solution)/shard_map/pack_pair/pallas_call | solution.py:98
  42.5 3.9 %collective-permute-start.30 = (bf16[80,1664]{1,0:T(8,128)(2,1)}, bf16[80,1664]{1,0:T(8,128)(2,1)S(1)}, u32[]{:S(2)}, u32[]{:S(2)}) collective-permute-start(bf16[80,1664]{1,0:T(8,128)(2,1)} %get-tuple-element.73), channel_id=1, source_target_pairs={{0,3},{1,2},{2,1},{3,0},{4,7},{5,6},{6,5},{7,4},{8,11},{9,10},{10,... | collective-permute-start | bytes 798728 | tf_op jit(solution)/shard_map/ppermute | solution.py:65
  47.2 6.8 %collective-permute-done.4.refs_2_ = bf16[320,960]{1,0:T(8,128)(2,1)S(1)} collective-permute-done((bf16[320,960]{1,0:T(8,128)(2,1)}, bf16[320,960]{1,0:T(8,128)(2,1)S(1)}, u32[]{:S(2)}, u32[]{:S(2)}) %collective-permute-start.4) | collective-permute-done | bytes 614432 | tf_op jit(solution)/shard_map/ppermute | solution.py:65
  55.5 12.6 %collective-permute-done.29 = bf16[80,1664]{1,0:T(8,128)(2,1)S(1)} collective-permute-done((bf16[80,1664]{1,0:T(8,128)(2,1)}, bf16[80,1664]{1,0:T(8,128)(2,1)S(1)}, u32[]{:S(2)}, u32[]{:S(2)}) %collective-permute-start.29) | collective-permute-done | bytes 266272 | tf_op jit(solution)/shard_map/ppermute | solution.py:65
  69.1 1.2 bitcast_select_fusion.1
  72.2 1.2 fusion.6.flags_ref.cached_ref
  73.4 1.2 pad_add_fusion.place_ref
  75.2 1.1 constant_dynamic-slice_fusion
  76.2 2.6 copy.19.blocks_ref
  78.9 3.0 cached.1
  81.9 2.6 collective-permute-start.17
  84.5 1.7 collective-permute-start.15
  87.7 15.1 %project.1 = (bf16[4,2,512,96]{3,2,1,0:T(8,128)(2,1)}, bf16[2,96,512]{2,1,0:T(8,128)(2,1)}, bf16[2,512,80]{2,1,0:T(8,128)(2,1)}) custom-call(s32[3]{0:T(128)} %pad_add_fusion.place_ref, bf16[512,2560]{1,0:T(8,128)(2,1)} %fusion.2.normed_ref, f32[512,80]{1,0:T(8,128)} %get-tuple-element.84.cos_ref, f32[512,80]{1,0:T(8,128)} %get-tuple-element.85.sin_ref, ...), custom_call_target="tpu_custom_call" | custom-call | flops 2516582400 | bytes 4915200 | tf_op jit(solution)/shard_map/project/pallas_call | solution.py:264
  102.9 2.3 fusion.13
  105.1 13.6 %attention.2 = bf16[256,640]{1,0:T(8,128)(2,1)} custom-call(s32[3]{0:T(128)} %pad_add_fusion.place_ref, bf16[2,2,512,96]{3,2,1,0:T(8,128)(2,1)} %get-tuple-element.79.queries, bf16[2,96,2048]{2,1,0:T(8,128)(2,1)} %get-tuple-element.48.cached_keys, bf16[2,2048,80]{2,1,0:T(8,128)(2,1)} %get-tuple-element.49.cached_values, ...), custom_call_target="tpu_custom_call" | custom-call | flops 5368709120 | bytes 2621440 | tf_op jit(solution)/shard_map/attention/pallas_call | solution.py:418
  119.3 1.2 pad_maximum_fusion.refs_5_
  121.3 2.0 collective-permute-start.27
  123.3 2.4 collective-permute-start.25
  125.7 13.8 %attention.3 = bf16[256,640]{1,0:T(8,128)(2,1)} custom-call(s32[3]{0:T(128)} %pad_add_fusion.place_ref, bf16[2,2,512,96]{3,2,1,0:T(8,128)(2,1)} %get-tuple-element.80.queries, bf16[2,96,2048]{2,1,0:T(8,128)(2,1)} %get-tuple-element.48.cached_keys, bf16[2,2048,80]{2,1,0:T(8,128)(2,1)} %get-tuple-element.49.cached_values, ...), custom_call_target="tpu_custom_call" | custom-call | flops 5368709120 | bytes 2621440 | tf_op jit(solution)/shard_map/attention/pallas_call | solution.py:418
  139.5 7.4 %collective-permute-done.26 = bf16[80,1792]{1,0:T(8,128)(2,1)S(1)} collective-permute-done((bf16[80,1792]{1,0:T(8,128)(2,1)S(1)}, bf16[80,1792]{1,0:T(8,128)(2,1)S(1)}, u32[]{:S(2)}, u32[]{:S(2)}) %collective-permute-start.26) | collective-permute-done | bytes 286752 | tf_op jit(solution)/shard_map/ppermute | solution.py:65
  147.7 1.2 bitcast_select_fusion
  149.5 1.7 collective-permute-start.20
  151.4 2.6 collective-permute-start.13
  154.4 25.4 %collective-permute-done.12.refs_1_ = bf16[512,640]{1,0:T(8,128)(2,1)S(1)} collective-permute-done((bf16[512,640]{1,0:T(8,128)(2,1)S(1)}, bf16[512,640]{1,0:T(8,128)(2,1)S(1)}, u32[]{:S(2)}, u32[]{:S(2)}) %collective-permute-start.12) | collective-permute-done | bytes 655392 | tf_op jit(solution)/shard_map/ppermute | solution.py:65
  179.8 9.8 %collective-permute-done.20.refs_8_ = bf16[3,80,2560]{2,1,0:T(8,128)(2,1)S(1)} collective-permute-done((bf16[3,80,2560]{2,1,0:T(8,128)(2,1)}, bf16[3,80,2560]{2,1,0:T(8,128)(2,1)S(1)}, u32[]{:S(2)}, u32[]{:S(2)}) %collective-permute-start.20) | collective-permute-done | bytes 1228832 | tf_op jit(solution)/shard_map/ppermute | solution.py:65
  190.6 1.9 collective-permute-start.14
  193.1 16.5 %collective-permute-done.14.refs_3_ = bf16[512,640]{1,0:T(8,128)(2,1)S(1)} collective-permute-done((bf16[512,640]{1,0:T(8,128)(2,1)S(1)}, bf16[512,640]{1,0:T(8,128)(2,1)S(1)}, u32[]{:S(2)}, u32[]{:S(2)}) %collective-permute-start.14) | collective-permute-done | bytes 655392 | tf_op jit(solution)/shard_map/ppermute | solution.py:65
  211.7 1.0 copy-done.20
  212.7 16.0 %middle.1 = (bf16[512,2560]{1,0:T(8,128)(2,1)}, bf16[512,640]{1,0:T(8,128)(2,1)}) custom-call(s32[3]{0:T(128)} %pad_add_fusion.place_ref, bf16[512,2560]{1,0:T(8,128)(2,1)} %tokens_ref.1, f32[1,2560]{1,0:T(1,128)} %reshape.188.gain_ref, bf16[512,640]{1,0:T(8,128)(2,1)} %copy-done.4, bf16[512,640]{1,0:T(8,128)(2,1)} %copy-done.23, ...), custom_call_target="tpu_custom_call" | custom-call | flops 6710886400 | bytes 13107200 | tf_op jit(solution)/shard_map/middle/pallas_call | solution.py:510
  228.8 23.9 %mlp.1 = (f32[512,640]{1,0:T(8,128)}, bf16[512,640]{1,0:T(8,128)(2,1)}, bf16[512,640]{1,0:T(8,128)(2,1)}, bf16[512,640]{1,0:T(8,128)(2,1)}) custom-call(s32[3]{0:T(128)} %pad_add_fusion.place_ref, bf16[512,2560]{1,0:T(8,128)(2,1)} %get-tuple-element.56.normed_ref, bf16[1728,2560]{1,0:T(8,128)(2,1)} %down_ref.1, ...), custom_call_target="tpu_custom_call" | custom-call | flops 13589544960 | bytes 26542080 | tf_op jit(solution)/shard_map/mlp/pallas_call | solution.py:612
  252.6 2.1 collective-permute-start.33
  254.8 12.2 %collective-permute-start.32 = (bf16[512,640]{1,0:T(8,128)(2,1)}, bf16[512,640]{1,0:T(8,128)(2,1)S(1)}, u32[]{:S(2)}, u32[]{:S(2)}) collective-permute-start(bf16[512,640]{1,0:T(8,128)(2,1)} %get-tuple-element.77), channel_id=1, source_target_pairs={{0,2},{1,3},{2,0},{3,1},{4,6},{5,7},{6,4},{7,5},{8,10},{9,11},{10,... | collective-permute-start | bytes 1966088 | tf_op jit(solution)/shard_map/ppermute | solution.py:65
  267.7 4.6 %collective-permute-done.33 = bf16[512,640]{1,0:T(8,128)(2,1)S(1)} collective-permute-done((bf16[512,640]{1,0:T(8,128)(2,1)}, bf16[512,640]{1,0:T(8,128)(2,1)S(1)}, u32[]{:S(2)}, u32[]{:S(2)}) %collective-permute-start.33) | collective-permute-done | bytes 655392 | tf_op jit(solution)/shard_map/ppermute | solution.py:65
  272.4 40.7 %collective-permute-done.32 = bf16[512,640]{1,0:T(8,128)(2,1)S(1)} collective-permute-done((bf16[512,640]{1,0:T(8,128)(2,1)}, bf16[512,640]{1,0:T(8,128)(2,1)S(1)}, u32[]{:S(2)}, u32[]{:S(2)}) %collective-permute-start.32) | collective-permute-done | bytes 655392 | tf_op jit(solution)/shard_map/ppermute | solution.py:65
  313.1 2.7 select_convert_fusion
  (161 shorter events, 20.1 us)
Async XLA Ops:
  6.5 8.7 %copy-start = (bf16[2,8,2,80,128]{4,3,2,1,0:T(8,128)(2,1)S(1)}, bf16[2,8,2,80,128]{4,3,2,1,0:T(8,128)(2,1)}, u32[]{:S(2)}) copy-start(bf16[2,8,2,80,128]{4,3,2,1,0:T(8,128)(2,1)} %param.24) | copy-start | bytes 1966084
  6.5 7.9 %copy-start.15 = (s32[64]{0:T(128)S(1)}, s32[64]{0:T(128)}, u32[]{:S(2)}) copy-start(s32[64]{0:T(128)} %param.25) | copy-start | bytes 772
  8.9 22.3 %collective-permute-start = (bf16[80,960]{1,0:T(8,128)(2,1)}, bf16[80,960]{1,0:T(8,128)(2,1)}, u32[]{:S(2)}, u32[]{:S(2)}) collective-permute-start(bf16[80,960]{1,0:T(8,128)(2,1)} %get-tuple-element.43), channel_id=1, source_target_pairs={{0,1},{1,0},{2,3},{3,2},{4,5},{5,4},{6,7},{7,6},{8,9},{9,8},{10,11... | collective-permute-start | bytes 460808 | tf_op jit(solution)/shard_map/ppermute | solution.py:65
  11.9 20.8 %collective-permute-start.1 = (bf16[80,960]{1,0:T(8,128)(2,1)}, bf16[80,960]{1,0:T(8,128)(2,1)}, u32[]{:S(2)}, u32[]{:S(2)}) collective-permute-start(bf16[80,960]{1,0:T(8,128)(2,1)} %get-tuple-element.44), channel_id=1, source_target_pairs={{0,2},{1,3},{2,0},{3,1},{4,6},{5,7},{6,4},{7,5},{8,10},{9,11},{10,... | collective-permute-start | bytes 460808 | tf_op jit(solution)/shard_map/ppermute | solution.py:65
  14.5 19.8 %collective-permute-start.2 = (bf16[80,960]{1,0:T(8,128)(2,1)}, bf16[80,960]{1,0:T(8,128)(2,1)S(1)}, u32[]{:S(2)}, u32[]{:S(2)}) collective-permute-start(bf16[80,960]{1,0:T(8,128)(2,1)} %get-tuple-element.45), channel_id=1, source_target_pairs={{0,3},{1,2},{2,1},{3,0},{4,7},{5,6},{6,5},{7,4},{8,11},{9,10},{10,... | collective-permute-start | bytes 460808 | tf_op jit(solution)/shard_map/ppermute | solution.py:65
  17.3 25.2 %all-to-all-start = ((bf16[2,16,2,80,128]{4,3,2,0,1:T(8,128)(2,1)}), bf16[2,16,2,80,128]{4,3,2,0,1:T(8,128)(2,1)}, u32[]{:S(2)}, u32[]{:S(2)}) async-start(bf16[2,16,2,80,128]{4,3,2,0,1:T(8,128)(2,1)} %select_bitcast_fusion), calls=%async_computation | async-start | bytes 2621440 | tf_op jit(solution)/shard_map/all_to_all | solution.py:676
  21.9 206.9 %all-gather.5.cloned.1.call-start = ((), (), s32[]{:S(2)}) async-start(), calls=%async_computation.2 | async-start | bytes 9584640 | tf_op jit(solution)/shard_map/all_gather | solution.py:720
  35.0 19.0 %collective-permute-start.4 = (bf16[320,960]{1,0:T(8,128)(2,1)}, bf16[320,960]{1,0:T(8,128)(2,1)S(1)}, u32[]{:S(2)}, u32[]{:S(2)}) collective-permute-start(bf16[320,960]{1,0:T(8,128)(2,1)} %constant_dynamic-update-slice_fusion.refs_0_), channel_id=1, source_target_pairs={{0,16},{4,20},{8,24},{12,28},{16,0},{20,4},{24,8},{28,12},{1,17},{... | collective-permute-start | bytes 1843208 | tf_op jit(solution)/shard_map/ppermute | solution.py:65
  36.9 17.8 %collective-permute-start.3 = (bf16[320,960]{1,0:T(8,128)(2,1)}, bf16[320,960]{1,0:T(8,128)(2,1)S(1)}, u32[]{:S(2)}, u32[]{:S(2)}) collective-permute-start(bf16[320,960]{1,0:T(8,128)(2,1)} %constant_dynamic-update-slice_fusion.refs_0_), channel_id=1, source_target_pairs={{0,8},{4,12},{8,0},{12,4},{16,24},{20,28},{24,16},{28,20},{1,9},{5... | collective-permute-start | bytes 1843208 | tf_op jit(solution)/shard_map/ppermute | solution.py:65
  42.5 25.6 %copy-start.8 = (bf16[80,1664]{1,0:T(8,128)(2,1)S(1)}, bf16[80,1664]{1,0:T(8,128)(2,1)}, u32[]{:S(2)}) copy-start(bf16[80,1664]{1,0:T(8,128)(2,1)} %get-tuple-element.70) | copy-start | bytes 798724
  42.5 13.0 %collective-permute-start.30 = (bf16[80,1664]{1,0:T(8,128)(2,1)}, bf16[80,1664]{1,0:T(8,128)(2,1)S(1)}, u32[]{:S(2)}, u32[]{:S(2)}) collective-permute-start(bf16[80,1664]{1,0:T(8,128)(2,1)} %get-tuple-element.73), channel_id=1, source_target_pairs={{0,3},{1,2},{2,1},{3,0},{4,7},{5,6},{6,5},{7,4},{8,11},{9,10},{10,... | collective-permute-start | bytes 798728 | tf_op jit(solution)/shard_map/ppermute | solution.py:65
  46.4 21.7 %collective-permute-start.29 = (bf16[80,1664]{1,0:T(8,128)(2,1)}, bf16[80,1664]{1,0:T(8,128)(2,1)S(1)}, u32[]{:S(2)}, u32[]{:S(2)}) collective-permute-start(bf16[80,1664]{1,0:T(8,128)(2,1)} %get-tuple-element.72), channel_id=1, source_target_pairs={{0,2},{1,3},{2,0},{3,1},{4,6},{5,7},{6,4},{7,5},{8,10},{9,11},{10,... | collective-permute-start | bytes 798728 | tf_op jit(solution)/shard_map/ppermute | solution.py:65
  46.4 21.7 %collective-permute-start.28 = (bf16[80,1664]{1,0:T(8,128)(2,1)}, bf16[80,1664]{1,0:T(8,128)(2,1)S(1)}, u32[]{:S(2)}, u32[]{:S(2)}) collective-permute-start(bf16[80,1664]{1,0:T(8,128)(2,1)} %get-tuple-element.71), channel_id=1, source_target_pairs={{0,1},{1,0},{2,3},{3,2},{4,5},{5,4},{6,7},{7,6},{8,9},{9,8},{10,11... | collective-permute-start | bytes 798728 | tf_op jit(solution)/shard_map/ppermute | solution.py:65
  54.0 18.1 %copy-start.9 = (bf16[320,960]{1,0:T(8,128)(2,1)}, bf16[320,960]{1,0:T(8,128)(2,1)S(1)}, u32[]{:S(2)}) copy-start(bf16[320,960]{1,0:T(8,128)(2,1)S(1)} %collective-permute-done.4.refs_2_) | copy-start | bytes 1843204
  54.1 16.2 %collective-permute-start.5 = (bf16[160,960]{1,0:T(8,128)(2,1)S(1)}, bf16[160,960]{1,0:T(8,128)(2,1)}, u32[]{:S(2)}, u32[]{:S(2)}) collective-permute-start(bf16[160,960]{1,0:T(8,128)(2,1)S(1)} %slice.22), channel_id=1, source_target_pairs={{0,8},{4,12},{8,0},{12,4},{16,24},{20,28},{24,16},{28,20},{1,9},{5... | collective-permute-start | bytes 921608 | tf_op jit(solution)/shard_map/ppermute | solution.py:65
  54.6 13.5 %copy-start.10 = (bf16[320,960]{1,0:T(8,128)(2,1)}, bf16[320,960]{1,0:T(8,128)(2,1)S(1)}, u32[]{:S(2)}) copy-start(bf16[320,960]{1,0:T(8,128)(2,1)S(1)} %collective-permute-done.3.refs_1_) | copy-start | bytes 1843204
  54.7 15.6 %collective-permute-start.6 = (bf16[160,960]{1,0:T(8,128)(2,1)S(1)}, bf16[160,960]{1,0:T(8,128)(2,1)}, u32[]{:S(2)}, u32[]{:S(2)}) collective-permute-start(bf16[160,960]{1,0:T(8,128)(2,1)S(1)} %slice.23), channel_id=1, source_target_pairs={{0,16},{4,20},{8,24},{12,28},{16,0},{20,4},{24,8},{28,12},{1,17},{... | collective-permute-start | bytes 921608 | tf_op jit(solution)/shard_map/ppermute | solution.py:65
  70.3 158.4 %all-gather.3.cloned.1.call-start = ((), (), s32[]{:S(2)}) async-start(), calls=%async_computation.1 | async-start | bytes 10321920 | tf_op jit(solution)/shard_map/all_gather | solution.py:743
  71.6 10.3 %collective-permute-start.7 = (bf16[320,960]{1,0:T(8,128)(2,1)}, bf16[320,960]{1,0:T(8,128)(2,1)S(1)}, u32[]{:S(2)}, u32[]{:S(2)}) collective-permute-start(bf16[320,960]{1,0:T(8,128)(2,1)} %constant_dynamic-update-slice_fusion.refs_0_), channel_id=1, source_target_pairs={{0,4},{4,0},{8,12},{12,8},{16,20},{20,16},{24,28},{28,24},{1,5},{5... | collective-permute-start | bytes 1843208 | tf_op jit(solution)/shard_map/ppermute | solution.py:65
  71.6 12.9 %collective-permute-start.8 = (bf16[320,960]{1,0:T(8,128)(2,1)S(1)}, bf16[320,960]{1,0:T(8,128)(2,1)S(1)}, u32[]{:S(2)}, u32[]{:S(2)}) collective-permute-start(bf16[320,960]{1,0:T(8,128)(2,1)S(1)} %copy-done.11), channel_id=1, source_target_pairs={{0,4},{4,0},{8,12},{12,8},{16,20},{20,16},{24,28},{28,24},{1,5},{5... | collective-permute-start | bytes 1843208 | tf_op jit(solution)/shard_map/ppermute | solution.py:65
  72.1 12.4 %collective-permute-start.9 = (bf16[320,960]{1,0:T(8,128)(2,1)S(1)}, bf16[320,960]{1,0:T(8,128)(2,1)}, u32[]{:S(2)}, u32[]{:S(2)}) collective-permute-start(bf16[320,960]{1,0:T(8,128)(2,1)S(1)} %collective-permute-done.4.refs_2_), channel_id=1, source_target_pairs={{0,4},{4,0},{8,12},{12,8},{16,20},{20,16},{24,28},{28,24},{1,5},{5... | collective-permute-start | bytes 1843208 | tf_op jit(solution)/shard_map/ppermute | solution.py:65
  74.7 11.6 %collective-permute-start.10 = (bf16[160,960]{1,0:T(8,128)(2,1)}, bf16[160,960]{1,0:T(8,128)(2,1)S(1)}, u32[]{:S(2)}, u32[]{:S(2)}) collective-permute-start(bf16[160,960]{1,0:T(8,128)(2,1)} %collective-permute-done.5.refs_3_), channel_id=1, source_target_pairs={{0,4},{4,0},{8,12},{12,8},{16,20},{20,16},{24,28},{28,24},{1,5},{5... | collective-permute-start | bytes 921608 | tf_op jit(solution)/shard_map/ppermute | solution.py:65
  75.1 11.2 %collective-permute-start.11 = (bf16[160,960]{1,0:T(8,128)(2,1)}, bf16[160,960]{1,0:T(8,128)(2,1)S(1)}, u32[]{:S(2)}, u32[]{:S(2)}) collective-permute-start(bf16[160,960]{1,0:T(8,128)(2,1)} %collective-permute-done.6.refs_4_), channel_id=1, source_target_pairs={{0,4},{4,0},{8,12},{12,8},{16,20},{20,16},{24,28},{28,24},{1,5},{5... | collective-permute-start | bytes 921608 | tf_op jit(solution)/shard_map/ppermute | solution.py:65
  81.9 36.9 %collective-permute-start.17 = (bf16[80,2560]{1,0:T(8,128)(2,1)S(1)}, bf16[80,2560]{1,0:T(8,128)(2,1)S(1)}, u32[]{:S(2)}, u32[]{:S(2)}) collective-permute-start(bf16[80,2560]{1,0:T(8,128)(2,1)S(1)} %constant_dynamic-slice_fusion), channel_id=1, source_target_pairs={{0,3},{1,2},{2,1},{3,0},{4,7},{5,6},{6,5},{7,4},{8,11},{9,10},{10,... | collective-permute-start | bytes 1228808 | tf_op jit(solution)/shard_map/ppermute | solution.py:65
  84.5 34.7 %collective-permute-start.16 = (bf16[80,2560]{1,0:T(8,128)(2,1)S(1)}, bf16[80,2560]{1,0:T(8,128)(2,1)S(1)}, u32[]{:S(2)}, u32[]{:S(2)}) collective-permute-start(bf16[80,2560]{1,0:T(8,128)(2,1)S(1)} %constant_dynamic-slice_fusion), channel_id=1, source_target_pairs={{0,2},{1,3},{2,0},{3,1},{4,6},{5,7},{6,4},{7,5},{8,10},{9,11},{10,... | collective-permute-start | bytes 1228808 | tf_op jit(solution)/shard_map/ppermute | solution.py:65
  84.5 34.7 %collective-permute-start.15 = (bf16[80,2560]{1,0:T(8,128)(2,1)S(1)}, bf16[80,2560]{1,0:T(8,128)(2,1)S(1)}, u32[]{:S(2)}, u32[]{:S(2)}) collective-permute-start(bf16[80,2560]{1,0:T(8,128)(2,1)S(1)} %constant_dynamic-slice_fusion), channel_id=1, source_target_pairs={{0,1},{1,0},{2,3},{3,2},{4,5},{5,4},{6,7},{7,6},{8,9},{9,8},{10,11... | collective-permute-start | bytes 1228808 | tf_op jit(solution)/shard_map/ppermute | solution.py:65
  120.5 28.9 %collective-permute-start.18 = (bf16[3,80,2560]{2,1,0:T(8,128)(2,1)}, bf16[3,80,2560]{2,1,0:T(8,128)(2,1)}, u32[]{:S(2)}, u32[]{:S(2)}) collective-permute-start(bf16[3,80,2560]{2,1,0:T(8,128)(2,1)} %pad_maximum_fusion.refs_5_), channel_id=1, source_target_pairs={{0,8},{4,12},{8,0},{12,4},{16,24},{20,28},{24,16},{28,20},{1,9},{5... | collective-permute-start | bytes 3686408 | tf_op jit(solution)/shard_map/ppermute | solution.py:65
  121.0 28.5 %collective-permute-start.19 = (bf16[3,80,2560]{2,1,0:T(8,128)(2,1)}, bf16[3,80,2560]{2,1,0:T(8,128)(2,1)}, u32[]{:S(2)}, u32[]{:S(2)}) collective-permute-start(bf16[3,80,2560]{2,1,0:T(8,128)(2,1)} %pad_maximum_fusion.refs_5_), channel_id=1, source_target_pairs={{0,16},{4,20},{8,24},{12,28},{16,0},{20,4},{24,8},{28,12},{1,17},{... | collective-permute-start | bytes 3686408 | tf_op jit(solution)/shard_map/ppermute | solution.py:65
  121.3 18.2 %collective-permute-start.27 = (bf16[80,1792]{1,0:T(8,128)(2,1)S(1)}, bf16[80,1792]{1,0:T(8,128)(2,1)S(1)}, u32[]{:S(2)}, u32[]{:S(2)}) collective-permute-start(bf16[80,1792]{1,0:T(8,128)(2,1)S(1)} %copy-done.30), channel_id=1, source_target_pairs={{0,3},{1,2},{2,1},{3,0},{4,7},{5,6},{6,5},{7,4},{8,11},{9,10},{10,... | collective-permute-start | bytes 860168 | tf_op jit(solution)/shard_map/ppermute | solution.py:65
  123.3 23.6 %collective-permute-start.26 = (bf16[80,1792]{1,0:T(8,128)(2,1)S(1)}, bf16[80,1792]{1,0:T(8,128)(2,1)S(1)}, u32[]{:S(2)}, u32[]{:S(2)}) collective-permute-start(bf16[80,1792]{1,0:T(8,128)(2,1)S(1)} %copy-done.29), channel_id=1, source_target_pairs={{0,2},{1,3},{2,0},{3,1},{4,6},{5,7},{6,4},{7,5},{8,10},{9,11},{10,... | collective-permute-start | bytes 860168 | tf_op jit(solution)/shard_map/ppermute | solution.py:65
  123.3 23.6 %collective-permute-start.25 = (bf16[80,1792]{1,0:T(8,128)(2,1)S(1)}, bf16[80,1792]{1,0:T(8,128)(2,1)S(1)}, u32[]{:S(2)}, u32[]{:S(2)}) collective-permute-start(bf16[80,1792]{1,0:T(8,128)(2,1)S(1)} %copy-done.28), channel_id=1, source_target_pairs={{0,1},{1,0},{2,3},{3,2},{4,5},{5,4},{6,7},{7,6},{8,9},{9,8},{10,11... | collective-permute-start | bytes 860168 | tf_op jit(solution)/shard_map/ppermute | solution.py:65
  125.7 21.2 %copy-start.7 = (bf16[80,1792]{1,0:T(8,128)(2,1)S(1)}, bf16[80,1792]{1,0:T(8,128)(2,1)}, u32[]{:S(2)}) copy-start(bf16[80,1792]{1,0:T(8,128)(2,1)} %get-tuple-element.61) | copy-start | bytes 860164
  148.9 43.5 %copy-start.13 = (f32[2560]{0:T(1024)S(1)}, f32[2560]{0:T(1024)}, u32[]{:S(2)}) copy-start(f32[2560]{0:T(1024)} %param.16) | copy-start | bytes 30724
  149.5 40.2 %collective-permute-start.20 = (bf16[3,80,2560]{2,1,0:T(8,128)(2,1)}, bf16[3,80,2560]{2,1,0:T(8,128)(2,1)S(1)}, u32[]{:S(2)}, u32[]{:S(2)}) collective-permute-start(bf16[3,80,2560]{2,1,0:T(8,128)(2,1)} %collective-permute-done.19.refs_7_), channel_id=1, source_target_pairs={{0,8},{4,12},{8,0},{12,4},{16,24},{20,28},{24,16},{28,20},{1,9},{5... | collective-permute-start | bytes 3686408 | tf_op jit(solution)/shard_map/ppermute | solution.py:65
  151.3 59.2 %copy-start.4 = (bf16[512,640]{1,0:T(8,128)(2,1)}, bf16[512,640]{1,0:T(8,128)(2,1)S(1)}, u32[]{:S(2)}) copy-start(bf16[512,640]{1,0:T(8,128)(2,1)S(1)} %pad_maximum_fusion.3.refs_0_) | copy-start | bytes 1966084
  151.3 28.6 %collective-permute-start.12 = (bf16[512,640]{1,0:T(8,128)(2,1)S(1)}, bf16[512,640]{1,0:T(8,128)(2,1)S(1)}, u32[]{:S(2)}, u32[]{:S(2)}) collective-permute-start(bf16[512,640]{1,0:T(8,128)(2,1)S(1)} %pad_maximum_fusion.3.refs_0_), channel_id=1, source_target_pairs={{0,1},{1,0},{2,3},{3,2},{4,5},{5,4},{6,7},{7,6},{8,9},{9,8},{10,11... | collective-permute-start | bytes 1966088 | tf_op jit(solution)/shard_map/ppermute | solution.py:65
  151.4 38.3 %collective-permute-start.13 = (bf16[512,640]{1,0:T(8,128)(2,1)S(1)}, bf16[512,640]{1,0:T(8,128)(2,1)S(1)}, u32[]{:S(2)}, u32[]{:S(2)}) collective-permute-start(bf16[512,640]{1,0:T(8,128)(2,1)S(1)} %pad_maximum_fusion.3.refs_0_), channel_id=1, source_target_pairs={{0,2},{1,3},{2,0},{3,1},{4,6},{5,7},{6,4},{7,5},{8,10},{9,11},{10,... | collective-permute-start | bytes 1966088 | tf_op jit(solution)/shard_map/ppermute | solution.py:65
  153.9 55.7 %collective-permute-start.21 = (bf16[3,80,2560]{2,1,0:T(8,128)(2,1)}, bf16[3,80,2560]{2,1,0:T(8,128)(2,1)S(1)}, u32[]{:S(2)}, u32[]{:S(2)}) collective-permute-start(bf16[3,80,2560]{2,1,0:T(8,128)(2,1)} %pad_maximum_fusion.refs_5_), channel_id=1, source_target_pairs={{0,4},{4,0},{8,12},{12,8},{16,20},{20,16},{24,28},{28,24},{1,5},{5... | collective-permute-start | bytes 3686408 | tf_op jit(solution)/shard_map/ppermute | solution.py:65
  153.9 55.7 %collective-permute-start.23 = (bf16[3,80,2560]{2,1,0:T(8,128)(2,1)}, bf16[3,80,2560]{2,1,0:T(8,128)(2,1)S(1)}, u32[]{:S(2)}, u32[]{:S(2)}) collective-permute-start(bf16[3,80,2560]{2,1,0:T(8,128)(2,1)} %collective-permute-done.19.refs_7_), channel_id=1, source_target_pairs={{0,4},{4,0},{8,12},{12,8},{16,20},{20,16},{24,28},{28,24},{1,5},{5... | collective-permute-start | bytes 3686408 | tf_op jit(solution)/shard_map/ppermute | solution.py:65
  179.8 30.6 %copy-start.23 = (bf16[512,640]{1,0:T(8,128)(2,1)}, bf16[512,640]{1,0:T(8,128)(2,1)S(1)}, u32[]{:S(2)}) copy-start(bf16[512,640]{1,0:T(8,128)(2,1)S(1)} %collective-permute-done.12.refs_1_) | copy-start | bytes 1966084
  179.8 29.8 %collective-permute-start.22 = (bf16[3,80,2560]{2,1,0:T(8,128)(2,1)}, bf16[3,80,2560]{2,1,0:T(8,128)(2,1)S(1)}, u32[]{:S(2)}, u32[]{:S(2)}) collective-permute-start(bf16[3,80,2560]{2,1,0:T(8,128)(2,1)} %collective-permute-done.18.refs_6_), channel_id=1, source_target_pairs={{0,4},{4,0},{8,12},{12,8},{16,20},{20,16},{24,28},{28,24},{1,5},{5... | collective-permute-start | bytes 3686408 | tf_op jit(solution)/shard_map/ppermute | solution.py:65
  189.7 20.8 %copy-start.16 = (bf16[3,80,2560]{2,1,0:T(8,128)(2,1)}, bf16[3,80,2560]{2,1,0:T(8,128)(2,1)S(1)}, u32[]{:S(2)}) copy-start(bf16[3,80,2560]{2,1,0:T(8,128)(2,1)S(1)} %collective-permute-done.20.refs_8_) | copy-start | bytes 3686404
  189.7 20.8 %collective-permute-start.24 = (bf16[3,80,2560]{2,1,0:T(8,128)(2,1)S(1)}, bf16[3,80,2560]{2,1,0:T(8,128)(2,1)S(1)}, u32[]{:S(2)}, u32[]{:S(2)}) collective-permute-start(bf16[3,80,2560]{2,1,0:T(8,128)(2,1)S(1)} %collective-permute-done.20.refs_8_), channel_id=1, source_target_pairs={{0,4},{4,0},{8,12},{12,8},{16,20},{20,16},{24,28},{28,24},{1,5},{5... | collective-permute-start | bytes 3686408 | tf_op jit(solution)/shard_map/ppermute | solution.py:65
  190.6 19.0 %collective-permute-start.14 = (bf16[512,640]{1,0:T(8,128)(2,1)S(1)}, bf16[512,640]{1,0:T(8,128)(2,1)S(1)}, u32[]{:S(2)}, u32[]{:S(2)}) collective-permute-start(bf16[512,640]{1,0:T(8,128)(2,1)S(1)} %pad_maximum_fusion.3.refs_0_), channel_id=1, source_target_pairs={{0,3},{1,2},{2,1},{3,0},{4,7},{5,6},{6,5},{7,4},{8,11},{9,10},{10,... | collective-permute-start | bytes 1966088 | tf_op jit(solution)/shard_map/ppermute | solution.py:65
  228.8 84.4 %copy-start.3 = (bf16[512,640]{1,0:T(8,128)(2,1)S(1)}, bf16[512,640]{1,0:T(8,128)(2,1)}, u32[]{:S(2)}) copy-start(bf16[512,640]{1,0:T(8,128)(2,1)} %get-tuple-element.55) | copy-start | bytes 1966084
  252.6 19.7 %collective-permute-start.33 = (bf16[512,640]{1,0:T(8,128)(2,1)}, bf16[512,640]{1,0:T(8,128)(2,1)S(1)}, u32[]{:S(2)}, u32[]{:S(2)}) collective-permute-start(bf16[512,640]{1,0:T(8,128)(2,1)} %get-tuple-element.78), channel_id=1, source_target_pairs={{0,3},{1,2},{2,1},{3,0},{4,7},{5,6},{6,5},{7,4},{8,11},{9,10},{10,... | collective-permute-start | bytes 1966088 | tf_op jit(solution)/shard_map/ppermute | solution.py:65
  254.8 58.3 %collective-permute-start.32 = (bf16[512,640]{1,0:T(8,128)(2,1)}, bf16[512,640]{1,0:T(8,128)(2,1)S(1)}, u32[]{:S(2)}, u32[]{:S(2)}) collective-permute-start(bf16[512,640]{1,0:T(8,128)(2,1)} %get-tuple-element.77), channel_id=1, source_target_pairs={{0,2},{1,3},{2,0},{3,1},{4,6},{5,7},{6,4},{7,5},{8,10},{9,11},{10,... | collective-permute-start | bytes 1966088 | tf_op jit(solution)/shard_map/ppermute | solution.py:65
  267.0 46.1 %collective-permute-start.31 = (bf16[512,640]{1,0:T(8,128)(2,1)}, bf16[512,640]{1,0:T(8,128)(2,1)S(1)}, u32[]{:S(2)}, u32[]{:S(2)}) collective-permute-start(bf16[512,640]{1,0:T(8,128)(2,1)} %get-tuple-element.76), channel_id=1, source_target_pairs={{0,1},{1,0},{2,3},{3,2},{4,5},{5,4},{6,7},{7,6},{8,9},{9,8},{10,11... | collective-permute-start | bytes 1966088 | tf_op jit(solution)/shard_map/ppermute | solution.py:65
  (22 other events, 48.7 us)
Sparse Core Ops, SparseCore 0:
  70.4 53.1 all-gather.4
  149.6 69.2 all-gather.2
